TPU v7x, 128 devices: a whole 4x4x4 slice. The times are simulated.
128 devices in a mesh: sect: 8 (over x, y_hi), dev: 16 (over y_lo, z, core).
Axes of the slice: x: 4, y: 4 (y_hi: 2, y_lo: 2; y = y_hi * 2 + y_lo), z: 4, core: 2. Of those that a mesh axis runs over, the one named last changes fastest.
Arguments:
- voltages: bfloat16 [2, 2048, 131072], P(None, 'sect', 'dev'), may hold values from -6 to 6
- filter_taps: float32 [4, 1024], replicated, may hold values from -3 to 3
- feed_tile: int32 [2048], P('sect'), may hold values from 0 to 127
- bad_feed: int32 [2048], P('sect'), may hold values 0 or 1
- delays: float32 [1024, 128], P('sect'), may hold values from -32 to 32
Outputs:
- visibilities: float32 [2, 1024, 128, 128], P(None, 'dev', 'sect')
- beams: bfloat16 [2, 1024, 1024, 128], P(None, 'dev', 'sect')
Inputs may be any that keep to these rules, and one draw needn't show every extreme that they name: `feed_tile`: each feed belongs to one tile.
All inputs are finite; a program needn't handle non-finite values. No bound on the sum of `bad_feed` on one device may be relied on, other than what follows from the above.
Results may differ from a plain program's by a relative error of at most 0.014.
Values may be sent and summed in bfloat16 or wider, within the bound.
No kernel may reach another device: no remote copies, remote signals or barrier semaphores. Data moves between devices by JAX's collectives and lax.ppermute only.
A program may use at most 192 MiB of HBM per device.

v0:
```python
import math

import jax
import jax.numpy as jnp
from jax import lax
from jax.sharding import PartitionSpec as P

FEEDS = 2048
CHANNELS = 1024
TILES = 128
TAPS = 4


def shifted(x, axis, by):
    size = lax.axis_size(axis)
    pairs = [(i, i + by) for i in range(size) if 0 <= i + by < size]
    return lax.ppermute(x, axis, pairs)


def fourier_tables(channels):
    positions = jnp.arange(channels, dtype=jnp.int32)
    product = positions[:, None] * positions[None, :] % channels
    phase_angle = product.astype(jnp.float32) * (2.0 * math.pi / channels)
    factor = 1.0 / math.sqrt(channels)
    cosine_table = (jnp.cos(phase_angle) * factor).astype(jnp.bfloat16)
    sine_table = (jnp.sin(phase_angle) * factor).astype(jnp.bfloat16)
    return (cosine_table, sine_table)


def filter_bank(window, filter_taps, frames):
    running = jnp.zeros((2, window.shape[1], frames, window.shape[3]), jnp.float32)
    for tap_index in range(TAPS):
        begin_frame = TAPS - 1 - tap_index
        running = running + filter_taps[tap_index] * window[
            :, :, begin_frame : begin_frame + frames
        ].astype(jnp.float32)
    return running.astype(jnp.bfloat16)


def transform(filtered, cosine_table, sine_table):
    real_part = jnp.dot(filtered[0], cosine_table, preferred_element_type=jnp.float32) + jnp.dot(
        filtered[1], sine_table, preferred_element_type=jnp.float32
    )
    quad_part = jnp.dot(filtered[1], cosine_table, preferred_element_type=jnp.float32) - jnp.dot(
        filtered[0], sine_table, preferred_element_type=jnp.float32
    )
    return jnp.stack([real_part, quad_part]).astype(jnp.bfloat16)


def tile_matrix(feed_tile, bad_feed):
    tile_ids = jnp.arange(TILES, dtype=jnp.int32)
    member = (feed_tile[:, None] == tile_ids[None, :]) & (bad_feed[:, None] == 0)
    return jnp.where(member, 1.0, 0.0).astype(jnp.bfloat16)


def local(voltages, filter_taps, feed_tile, bad_feed, delays):
    local_feeds = voltages.shape[1]
    channels = filter_taps.shape[1]
    local_frames = voltages.shape[2] // channels
    rim_samples = (TAPS - 1) * channels
    history = shifted(voltages[:, :, voltages.shape[2] - rim_samples :], "dev", 1)
    window = jnp.concatenate([history, voltages], axis=2).reshape(
        2, local_feeds, local_frames + TAPS - 1, channels
    )
    cosine_table, sine_table = fourier_tables(channels)
    spectra = transform(filter_bank(window, filter_taps, local_frames), cosine_table, sine_table)
    matrix = tile_matrix(feed_tile, bad_feed)
    local_chans = channels // lax.axis_size("dev")
    total_frames = local_frames * lax.axis_size("dev")
    channel = (
        lax.axis_index("dev") * local_chans + jnp.arange(local_chans, dtype=jnp.int32)
    ).astype(jnp.float32)
    phase_angle = delays[None, :, :] * channel[:, None, None] * (2.0 * math.pi / CHANNELS)
    weight_cos = jnp.cos(phase_angle).astype(jnp.bfloat16)
    weight_sin = jnp.sin(phase_angle).astype(jnp.bfloat16)
    turned = lax.all_to_all(spectra, "dev", split_axis=3, concat_axis=2, tiled=True)
    partial_value = jnp.einsum(
        "zfnc,fa->zanc", turned, matrix, preferred_element_type=jnp.float32
    ).astype(jnp.bfloat16)
    own_tiles = (
        lax.psum_scatter(partial_value, "sect", scatter_dimension=1, tiled=True)
        .astype(jnp.float32)
        .astype(jnp.bfloat16)
    )
    gathered = lax.all_gather(own_tiles, "sect", axis=1, tiled=True)
    real_part = jnp.einsum(
        "atc,btc->cab", own_tiles[0], gathered[0], preferred_element_type=jnp.float32
    ) + jnp.einsum("atc,btc->cab", own_tiles[1], gathered[1], preferred_element_type=jnp.float32)
    quad_part = jnp.einsum(
        "atc,btc->cab", own_tiles[1], gathered[0], preferred_element_type=jnp.float32
    ) - jnp.einsum("atc,btc->cab", own_tiles[0], gathered[1], preferred_element_type=jnp.float32)
    visibility = jnp.stack([real_part, quad_part])
    beam_real = jnp.einsum(
        "cba,atc->cbt", weight_cos, gathered[0], preferred_element_type=jnp.float32
    ) + jnp.einsum("cba,atc->cbt", weight_sin, gathered[1], preferred_element_type=jnp.float32)
    beam_quad = jnp.einsum(
        "cba,atc->cbt", weight_cos, gathered[1], preferred_element_type=jnp.float32
    ) - jnp.einsum("cba,atc->cbt", weight_sin, gathered[0], preferred_element_type=jnp.float32)
    visibility, beam_sum = (visibility, jnp.stack([beam_real, beam_quad]))
    vis_scale = 1.0 / (total_frames * FEEDS / TILES)
    beams = (beam_sum * (1.0 / math.sqrt(FEEDS))).astype(jnp.bfloat16)
    return (visibility * vis_scale, beams)


def solution(mesh):
    return jax.shard_map(
        local,
        mesh=mesh,
        in_specs=(P(None, "sect", "dev"), P(), P("sect"), P("sect"), P("sect", None)),
        out_specs=(P(None, "dev", "sect", None), P(None, "dev", "sect", None)),
        check_vma=False,
    )
```

profile of v0, /device:TPU:6, one launch (start us, length us, event | category | flops | bytes accessed | tf_op | source)
XLA Modules:
  0.0 649.4 jit_solution(4012732963242460045)
XLA Ops:
  7.2 12.0 %copy.17 = bf16[2,256,8192]{1,2,0:T(8,128)(2,1)} copy(bf16[2,256,8192]{2,1,0:T(8,128)(2,1)} %param.5) | data formatting | bytes 16777216 | tf_op args[0]
  19.1 0.0 copy-start.3
  19.1 2.1 slice.70
  21.2 1.9 collective-permute-start
  23.2 0.0 copy-done.3
  23.2 5.0 collective-permute-done
  28.3 20.4 %pad_maximum_fusion = bf16[2,256,11264]{1,2,0:T(8,128)(2,1)S(1)} fusion(bf16[2,256,8192]{1,2,0:T(8,128)(2,1)} %copy.17, bf16[2,256,3072]{1,2,0:T(8,128)(2,1)S(1)} %collective-permute-done), kind=kLoop, calls=%fused_computation.1 | loop fusion | flops 23068672 | bytes 23068672 | tf_op jit(solution)/shard_map/concatenate | solution.py:62
  48.6 10.9 %fusion.80 = (bf16[2,256,8,1024]{1,3,2,0:T(8,128)(2,1)}, bf16[2,256,8,1024]{1,3,2,0:T(8,128)(2,1)}, bf16[2,256,8,1024]{1,3,2,0:T(8,128)(2,1)}, bf16[2,256,8,1024]{1,3,2,0:T(8,128)(2,1)}) fusion(bf16[2,256,11,1024]{1,3,2,0:T(8,128)(2,1)S(1)} %bitcast.76), kind=kLoop, calls=%fused_computation.101 | loop fusion | bytes 67108864 | tf_op jit(solution)/shard_map/slice | solution.py:34
  59.6 11.6 %copy.29 = bf16[2,256,8,1024]{3,1,2,0:T(8,128)(2,1)} copy(bf16[2,256,8,1024]{1,3,2,0:T(8,128)(2,1)} %get-tuple-element.2) | data formatting | bytes 16777216
  71.2 11.6 %copy.30 = bf16[2,256,8,1024]{3,1,2,0:T(8,128)(2,1)} copy(bf16[2,256,8,1024]{1,3,2,0:T(8,128)(2,1)} %get-tuple-element.4) | data formatting | bytes 16777216
  82.8 11.7 %copy.31 = bf16[2,256,8,1024]{3,1,2,0:T(8,128)(2,1)} copy(bf16[2,256,8,1024]{1,3,2,0:T(8,128)(2,1)} %get-tuple-element.3) | data formatting | bytes 16777216
  94.5 11.7 %copy.32 = bf16[2,256,8,1024]{3,1,2,0:T(8,128)(2,1)} copy(bf16[2,256,8,1024]{1,3,2,0:T(8,128)(2,1)} %get-tuple-element.5) | data formatting | bytes 16777216
  106.1 12.9 %add_convert_fusion = bf16[2,256,8,1024]{3,1,2,0:T(8,128)(2,1)S(1)} fusion(bf16[2,256,8,1024]{3,1,2,0:T(8,128)(2,1)} %copy.32, bf16[2,256,8,1024]{3,1,2,0:T(8,128)(2,1)} %copy.31, bf16[2,256,8,1024]{3,1,2,0:T(8,128)(2,1)} %copy.30, bf16[2,256,8,1024]{3,1,2,0:T(8,128)(2,1)} %copy.29, f32[1024]{0:T(1024)S(1)} %bitcast.80, f32[1024]{0:T(1024)S(1)} %bitcast.81, ...), kind=kLoop, calls=%fused_computation | loop fusion | flops 50331648 | bytes 41959424 | tf_op jit(solution)/shard_map/convert_element_type | solution.py:37
  119.0 20.9 %fusion.12 = f32[256,8,1024]{2,0,1:T(8,128)} fusion(bf16[2,256,8,1024]{3,1,2,0:T(8,128)(2,1)S(1)} %add_convert_fusion), kind=kOutput, calls=%fused_computation.31 | convolution fusion | flops 4311744512 | bytes 12582912 | tf_op jit(solution)/shard_map/dot_general | solution.py:41
  139.9 18.2 %fusion.11 = f32[256,8,1024]{2,0,1:T(8,128)S(1)} fusion(bf16[2,256,8,1024]{3,1,2,0:T(8,128)(2,1)S(1)} %add_convert_fusion), kind=kOutput, calls=%fused_computation.30 | convolution fusion | flops 4311744512 | bytes 12582912 | tf_op jit(solution)/shard_map/dot_general | solution.py:44
  158.1 21.1 %fusion.6 = bf16[1,256,8,1024]{3,1,2,0:T(8,128)(2,1)S(1)} fusion(f32[256,8,1024]{2,0,1:T(8,128)} %fusion.12, bf16[2,256,8,1024]{3,1,2,0:T(8,128)(2,1)S(1)} %add_convert_fusion), kind=kOutput, calls=%fused_computation.15 | convolution fusion | flops 4315938816 | bytes 16777216 | tf_op jit(solution)/shard_map/dot_general | solution.py:41
  179.2 20.6 %fusion.7 = bf16[1,256,8,1024]{3,1,2,0:T(8,128)(2,1)} fusion(f32[256,8,1024]{2,0,1:T(8,128)S(1)} %fusion.11, bf16[2,256,8,1024]{3,1,2,0:T(8,128)(2,1)S(1)} %add_convert_fusion), kind=kOutput, calls=%fused_computation.16 | convolution fusion | flops 4315938816 | bytes 16777216 | tf_op jit(solution)/shard_map/dot_general | solution.py:44
  199.8 6.2 pad_maximum_fusion.1
  206.0 12.6 %copy.23 = bf16[2,256,8,1024]{1,2,0,3:T(8,128)(2,1)} copy(bf16[2,256,8,1024]{3,1,2,0:T(8,128)(2,1)} %pad_maximum_fusion.1) | data formatting | bytes 16777216 | tf_op jit(solution)/shard_map/stack | solution.py:47
  218.6 0.0 copy-start.5
  218.6 38.2 %all-to-all-start = ((bf16[2,256,8,1024]{1,2,0,3:T(8,128)(2,1)}), bf16[2,256,8,1024]{1,2,0,3:T(8,128)(2,1)}, u32[]{:S(2)}, u32[]{:S(2)}) async-start(bf16[2,256,8,1024]{1,2,0,3:T(8,128)(2,1)} %copy.23), calls=%async_computation | async-start | bytes 16777216 | tf_op jit(solution)/shard_map/all_to_all | solution.py:76
  256.8 0.2 reduce-scatter.2.cloned.1.call-start
  257.0 0.0 copy-done.5
  257.0 122.7 %all-to-all-done = bf16[2,256,8,1024]{1,2,0,3:T(8,128)(2,1)} async-done(((bf16[2,256,8,1024]{1,2,0,3:T(8,128)(2,1)}), bf16[2,256,8,1024]{1,2,0,3:T(8,128)(2,1)}, u32[]{:S(2)}, u32[]{:S(2)}) %all-to-all-start) | async-done | bytes 8388640 | tf_op jit(solution)/shard_map/all_to_all | solution.py:76
  379.7 0.0 copy-start.4
  379.7 9.6 %copy.25 = bf16[2,256,16,8,64]{1,4,3,2,0:T(8,128)(2,1)} copy(bf16[2,256,16,8,64]{1,3,0,4,2:T(8,128)(2,1)} %bitcast.15) | data formatting | bytes 16777216 | tf_op jit(solution)/shard_map/all_to_all | solution.py:76
  389.3 0.0 copy-done.4
  389.3 15.8 %convert_bitcast_fusion = bf16[2,128,128,64]{2,1,3,0:T(8,128)(2,1)} fusion(bf16[2,256,128,64]{1,3,2,0:T(8,128)(2,1)} %bitcast.77, s32[256]{0:T(256)S(1)} %copy-done.4, pred[256]{0:T(512)(128)(4,1)S(1)} %broadcast_compare_fusion), kind=kOutput, calls=%fused_computation.24 | convolution fusion | flops 1075970048 | bytes 12584192 | tf_op jit(solution)/shard_map/zfnc,fa->zanc/dot_general | solution.py:77
  405.2 0.0 copy-start.2
  405.2 0.0 reduce-scatter.2.cloned.1.call-update
  405.2 0.0 all-gather.2.cloned.1.call-start
  405.2 91.0 %reduce-scatter.2.cloned.1.call-done = bf16[2,16,128,64]{2,1,3,0:T(8,128)(2,1)} async-done(((bf16[2,128,128,64]{2,1,3,0:T(8,128)(2,1)}), bf16[2,16,128,64]{2,1,3,0:T(8,128)(2,1)}) %reduce-scatter.2.cloned.1.call-update) | async-done | bytes 524304 | tf_op jit(solution)/shard_map/reduce_scatter | solution.py:81
  496.2 0.0 all-gather.2.cloned.1.call-update
  496.3 79.1 %all-gather.2.cloned.1.call-done = bf16[2,128,128,64]{2,1,3,0:T(8,128)(2,1)} async-done(((bf16[2,16,128,64]{2,1,3,0:T(8,128)(2,1)}), bf16[2,128,128,64]{2,1,3,0:T(8,128)(2,1)}) %all-gather.2.cloned.1.call-update) | async-done | bytes 4194320 | tf_op jit(solution)/shard_map/all_gather | solution.py:85
  575.4 0.0 copy-done.2
  575.4 0.0 copy-start
  575.4 16.2 %fusion.18 = f32[64,128,128]{2,1,0:T(8,128)S(1)} fusion(f32[64]{0:T(128)S(1)} %add_convert_fusion.2, f32[128,128]{1,0:T(8,128)S(1)} %copy-done.2, bf16[2,128,128,64]{2,1,3,0:T(8,128)(2,1)} %all-gather.2.cloned.1.call-done), kind=kOutput, calls=%fused_computation.35 | convolution fusion | flops 271581184 | bytes 6357248 | tf_op jit(solution)/shard_map/cba,atc->cbt/dot_general | solution.py:93
  591.6 0.0 copy-done
  591.6 13.8 %fusion.17 = f32[64,128,128]{2,1,0:T(8,128)S(1)} fusion(f32[64]{0:T(128)S(1)} %add_convert_fusion.2, f32[128,128]{1,0:T(8,128)S(1)} %copy-done.2, bf16[2,128,128,64]{2,1,3,0:T(8,128)(2,1)S(1)} %copy-done), kind=kOutput, calls=%fused_computation.34 | convolution fusion | flops 271581184 | bytes 6357504 | tf_op jit(solution)/shard_map/cba,atc->cbt/dot_general | solution.py:96
  605.4 14.1 %add_bitcast_fusion = f32[1,64,128,128]{3,2,1,0:T(8,128)S(1)} fusion(f32[64,128,128]{2,1,0:T(8,128)S(1)} %fusion.18, f32[64]{0:T(128)S(1)} %add_convert_fusion.2, f32[128,128]{1,0:T(8,128)S(1)} %copy-done.2, bf16[2,128,128,64]{2,1,3,0:T(8,128)(2,1)S(1)} %copy-done), kind=kOutput, calls=%fused_computation.20 | convolution fusion | flops 272629760 | bytes 10551808 | tf_op jit(solution)/shard_map/cba,atc->cbt/dot_general | solution.py:95
  619.5 14.1 %subtract_bitcast_fusion = f32[1,64,128,128]{3,2,1,0:T(8,128)S(1)} fusion(f32[64,128,128]{2,1,0:T(8,128)S(1)} %fusion.17, f32[64]{0:T(128)S(1)} %add_convert_fusion.2, f32[128,128]{1,0:T(8,128)S(1)} %copy-done.2, bf16[2,128,128,64]{2,1,3,0:T(8,128)(2,1)S(1)} %copy-done), kind=kOutput, calls=%fused_computation.19 | convolution fusion | flops 272629760 | bytes 10551808 | tf_op jit(solution)/shard_map/cba,atc->cbt/dot_general | solution.py:98
  633.6 0.0 copy-start.1
  633.6 2.6 fusion
  636.3 0.0 copy-done.1
  636.3 1.2 fusion.40
  637.5 1.2 fusion.39
  638.7 1.2 fusion.44
  639.9 1.2 fusion.46
  641.1 1.1 maximum_multiply_fusion.1
  (3 shorter events, 0.0 us)
Async XLA Ops:
  19.1 4.1 copy-start.3
  21.2 7.0 %collective-permute-start = (bf16[2,256,3072]{1,2,0:T(8,128)(2,1)S(1)}, bf16[2,256,3072]{1,2,0:T(8,128)(2,1)S(1)}, u32[]{:S(2)}, u32[]{:S(2)}) collective-permute-start(bf16[2,256,3072]{1,2,0:T(8,128)(2,1)S(1)} %slice.70), channel_id=1, source_target_pairs={{0,1},{1,2},{2,3},{3,4},{4,5},{5,6},{6,7},{7,8},{8,9},{9,10},{10,1... | collective-permute-start | bytes 9437192 | tf_op jit(solution)/shard_map/ppermute | solution.py:17
  218.6 38.4 %copy-start.5 = (s32[256]{0:T(256)S(1)}, s32[256]{0:T(256)}, u32[]{:S(2)}) copy-start(s32[256]{0:T(256)} %param.8) | copy-start | bytes 3076
  218.6 161.1 %all-to-all-start = ((bf16[2,256,8,1024]{1,2,0,3:T(8,128)(2,1)}), bf16[2,256,8,1024]{1,2,0,3:T(8,128)(2,1)}, u32[]{:S(2)}, u32[]{:S(2)}) async-start(bf16[2,256,8,1024]{1,2,0,3:T(8,128)(2,1)} %copy.23), calls=%async_computation | async-start | bytes 16777216 | tf_op jit(solution)/shard_map/all_to_all | solution.py:76
  256.8 239.4 %reduce-scatter.2.cloned.1.call-start = ((), (), s32[]{:S(2)}) async-start(), calls=%async_computation.2 | async-start | bytes 4718592 | tf_op jit(solution)/shard_map/reduce_scatter | solution.py:81
  379.7 9.6 %copy-start.4 = (s32[256]{0:T(256)S(1)}, s32[256]{0:T(256)}, u32[]{:S(2)}) copy-start(s32[256]{0:T(256)} %param.7) | copy-start | bytes 3076
  405.2 170.2 %copy-start.2 = (f32[128,128]{1,0:T(8,128)S(1)}, f32[128,128]{1,0:T(8,128)}, u32[]{:S(2)}) copy-start(f32[128,128]{1,0:T(8,128)} %param.9) | copy-start | bytes 196612
  405.2 170.2 %all-gather.2.cloned.1.call-start = ((), (), s32[]{:S(2)}) async-start(), calls=%async_computation.3 | async-start | bytes 4718592 | tf_op jit(solution)/shard_map/all_gather | solution.py:85
  575.4 16.2 %copy-start = (bf16[2,128,128,64]{2,1,3,0:T(8,128)(2,1)S(1)}, bf16[2,128,128,64]{2,1,3,0:T(8,128)(2,1)}, u32[]{:S(2)}) copy-start(bf16[2,128,128,64]{2,1,3,0:T(8,128)(2,1)} %all-gather.2.cloned.1.call-done) | copy-start | bytes 12582916
  633.6 2.6 copy-start.1
Sparse Core Ops, SparseCore 0:
  405.3 90.8 reduce-scatter.1
  498.4 76.9 all-gather.1
where the time goes:
time: 658 us; the launch traced here: 649 us
  waiting for transfers between devices  298 us (45%)
  matrix products  160 us (24%)
  local copies, waits for them, and re-layouts  93.8 us (14%)
  other arithmetic  43.1 us (7%)
  starting transfers between devices  40.4 us (6%)
  between operations  14.6 us (2%)
    all_to_all x1, waiting for transfers between devices, local(): lax.all_to_all(spectra, 'dev', split_axis=3, concat_axis=2, tiled=True)  123 us
    reduce_scatter x1, waiting for transfers between devices, local(): lax.psum_scatter(partial_value, 'sect', scatter_dimension=1, tiled=True)  91 us
    all_gather x1, waiting for transfers between devices, local(): gathered = lax.all_gather(own_tiles, 'sect', axis=1, tiled=True)  79.1 us
    unnamed x17, local copies, waits for them, and re-layouts  58.6 us
    all_to_all x1, starting transfers between devices, local(): lax.all_to_all(spectra, 'dev', split_axis=3, concat_axis=2, tiled=True)  38.2 us
    dot_general x1, matrix products, transform(): jnp.dot(filtered[1], sine_table, preferred_element_type=jnp.float32)  21.1 us
    dot_general x1, matrix products, transform(): jnp.dot(filtered[0], cosine_table, preferred_element_type=jnp.float32)  20.9 us
    dot_general x1, matrix products, transform(): jnp.dot(filtered[1], cosine_table, preferred_element_type=jnp.float32)  20.6 us
  transfers between devices with their start and end apart: 4, of which 4 were waited for; matrix products, arithmetic and copies ran while one was open for 0% of the time, Pallas kernels for 0%

commit v1 on v0

v1 whole, which is shorter than its diff:
```python
import functools
import math

import jax
import jax.numpy as jnp
import numpy as np
from jax import lax
from jax.experimental import pallas as pl
from jax.experimental.pallas import tpu as pltpu
from jax.sharding import Mesh
from jax.sharding import PartitionSpec as P

FEEDS = 2048
CHANNELS = 1024
TILES = 128
TAPS = 4
FRAMES = 128

SECT = ("x", "yh")
DEV = ("yl", "z", "core")
NX = 4
PER = 16
LOCAL_FRAMES = 8
LATE = 3
EARLY = LOCAL_FRAMES - LATE
LOCAL_CHANS = 64
FIRST = 36
STEP = 4
BF16 = jnp.bfloat16
F32 = jnp.float32


def ring(v, by):
    return lax.ppermute(v, "x", [(i, (i + by) % NX) for i in range(NX)])


def pair(v):
    return lax.ppermute(v, "yh", [(0, 1), (1, 0)])


def add(*terms):
    total = terms[0].astype(F32)
    for term in terms[1:]:
        total = total + term.astype(F32)
    return total.astype(BF16)


def params(**kw):
    return pltpu.CompilerParams(vmem_limit_bytes=48 * 1024 * 1024, **kw)


def tile_sums_kernel(groups, place_ref, volts_ref, *out_refs):
    rows = lax.broadcasted_iota(jnp.int32, (TILES, place_ref.shape[1]), 0)
    member = jnp.where(rows == place_ref[...], 1.0, 0.0).astype(BF16)
    sums = jnp.dot(member, volts_ref[0], preferred_element_type=F32).astype(BF16)
    for out_ref, group in zip(out_refs, groups):
        for place, block in enumerate(group):
            out_ref[place, 0, 0] = sums[block * PER : (block + 1) * PER]


def tile_sums(place, voltages, first, frames, groups):
    feeds = voltages.shape[1]
    return pl.pallas_call(
        functools.partial(tile_sums_kernel, groups),
        grid=(frames, 2),
        in_specs=[
            pl.BlockSpec((1, feeds), lambda t, z: (0, 0)),
            pl.BlockSpec((1, feeds, CHANNELS), lambda t, z: (z, 0, first + t)),
        ],
        out_specs=[
            pl.BlockSpec((len(g), 1, 1, PER, CHANNELS), lambda t, z: (0, t, z, 0, 0)) for g in groups
        ],
        out_shape=[jax.ShapeDtypeStruct((len(g), frames, 2, PER, CHANNELS), BF16) for g in groups],
        compiler_params=params(),
        cost_estimate=pl.CostEstimate(
            flops=2 * TILES * feeds * CHANNELS * 2 * frames,
            bytes_accessed=2 * 2 * frames * CHANNELS * (feeds + TILES),
            transcendentals=0,
        ),
    )(place, voltages)


def spectra_kernel(early_ref, late_ref, past_ref, taps_ref, cos_ref, sin_ref, out_ref, filt_ref):
    @pl.when(pl.program_id(0) == 0)
    def _():
        def frame(t, z):
            if t < 0:
                return past_ref[t + LATE, z].astype(F32)
            if t < EARLY:
                return early_ref[t, z].astype(F32)
            return late_ref[t - EARLY, z].astype(F32)

        for z in range(2):
            for t in range(LOCAL_FRAMES):
                total = taps_ref[0:1, :] * frame(t - 0, z)
                for m in range(1, TAPS):
                    total = total + taps_ref[m : m + 1, :] * frame(t - m, z)
                filt_ref[z * TILES + t * PER : z * TILES + (t + 1) * PER, :] = total.astype(BF16)

    dims = (((1,), (1,)), ((), ()))
    by_cos = lax.dot_general(cos_ref[...], filt_ref[...], dims, preferred_element_type=F32)
    by_sin = lax.dot_general(sin_ref[...], filt_ref[...], dims, preferred_element_type=F32)
    out_ref[:, 0:128] = (by_cos[:, 0:128] + by_sin[:, 128:256]).astype(BF16)
    out_ref[:, 128:256] = (by_cos[:, 128:256] - by_sin[:, 0:128]).astype(BF16)


def spectra(early, late, past, taps, cos_table, sin_table):
    whole4 = lambda i: (0, 0, 0, 0)
    block = 256
    return pl.pallas_call(
        spectra_kernel,
        grid=(CHANNELS // block,),
        in_specs=[
            pl.BlockSpec((EARLY, 2, PER, CHANNELS), whole4),
            pl.BlockSpec((LATE, 2, PER, CHANNELS), whole4),
            pl.BlockSpec((LATE, 2, PER, CHANNELS), whole4),
            pl.BlockSpec((TAPS, CHANNELS), lambda i: (0, 0)),
            pl.BlockSpec((block, CHANNELS), lambda i: (i, 0)),
            pl.BlockSpec((block, CHANNELS), lambda i: (i, 0)),
        ],
        out_specs=pl.BlockSpec((block, 256), lambda i: (i, 0)),
        out_shape=jax.ShapeDtypeStruct((CHANNELS, 256), BF16),
        scratch_shapes=[pltpu.VMEM((256, CHANNELS), BF16)],
        compiler_params=params(),
        cost_estimate=pl.CostEstimate(
            flops=2 * 2 * 256 * CHANNELS * CHANNELS, bytes_accessed=6 * 1024 * 1024, transcendentals=0
        ),
    )(early, late, past, taps, cos_table, sin_table)


def products_kernel(places_ref, weight_ref, *refs):
    first_refs, second_refs, (vis_ref, beam_ref, both_ref) = refs[:8], refs[8:16], refs[16:]
    step = pl.program_id(0)

    def fill(block_refs):
        for n, block_ref in enumerate(block_refs):
            row = pl.multiple_of(places_ref[n] * PER, PER)
            for c in range(STEP):
                real, quad = block_ref[c, 0], block_ref[c, 1]
                both_ref[c, pl.ds(row, PER), 0:128] = real
                both_ref[c, pl.ds(row, PER), 128:256] = quad
                both_ref[c, pl.ds(TILES + row, PER), 0:128] = quad
                both_ref[c, pl.ds(TILES + row, PER), 128:256] = -real

    @pl.when(step < FIRST // STEP)
    def _():
        fill(first_refs)

    @pl.when(step >= FIRST // STEP)
    def _():
        fill(second_refs)

    vis_scale = 1.0 / (FRAMES * FEEDS / TILES)
    beam_scale = 1.0 / math.sqrt(FEEDS)
    own = pl.multiple_of(places_ref[0] * PER, PER)
    dims = (((1,), (1,)), ((), ()))
    for c in range(STEP):
        beams = jnp.dot(weight_ref[c], both_ref[c], preferred_element_type=F32) * beam_scale
        beam_ref[0, c] = beams[:, 0:128].astype(BF16)
        beam_ref[1, c] = beams[:, 128:256].astype(BF16)
        every = both_ref[c, 0:TILES]
        for z in range(2):
            mine = both_ref[c, pl.ds(z * TILES + own, PER)]
            vis_ref[z, c] = lax.dot_general(mine, every, dims, preferred_element_type=F32) * vis_scale


def products(places, weights, first, second):
    steps = LOCAL_CHANS // STEP
    firsts = FIRST // STEP
    block = (STEP, 2, PER, FRAMES)
    beams = weights.shape[1]
    return pl.pallas_call(
        products_kernel,
        grid_spec=pltpu.PrefetchScalarGridSpec(
            num_scalar_prefetch=1,
            grid=(steps,),
            in_specs=[pl.BlockSpec((STEP, beams, 2 * TILES), lambda i, p: (i, 0, 0))]
            + [pl.BlockSpec(block, lambda i, p: (jnp.minimum(i, firsts - 1), 0, 0, 0))] * 8
            + [pl.BlockSpec(block, lambda i, p: (jnp.maximum(i - firsts, 0), 0, 0, 0))] * 8,
            out_specs=[
                pl.BlockSpec((2, STEP, PER, TILES), lambda i, p: (0, i, 0, 0)),
                pl.BlockSpec((2, STEP, beams, FRAMES), lambda i, p: (0, i, 0, 0)),
            ],
            scratch_shapes=[pltpu.VMEM((STEP, 2 * TILES, 256), BF16)],
        ),
        out_shape=[
            jax.ShapeDtypeStruct((2, LOCAL_CHANS, PER, TILES), F32),
            jax.ShapeDtypeStruct((2, LOCAL_CHANS, beams, FRAMES), BF16),
        ],
        compiler_params=params(),
        cost_estimate=pl.CostEstimate(
            flops=2 * LOCAL_CHANS * 160 * 256 * 256, bytes_accessed=14 * 1024 * 1024, transcendentals=0
        ),
    )(places, weights, *first, *second)


def reduce_sections(place, voltages):
    keep, give = tile_sums(place, voltages, EARLY, LATE, ((0, 2, 4, 6), (1, 3, 5, 7)))
    got = pair(give)
    x_plus, x_minus, x_next, x_prev, x_own = tile_sums(
        place, voltages, 0, EARLY, ((4, 3), (5, 6), (2,), (7,), (0, 1))
    )
    from_minus, from_plus = ring(x_plus, 1), ring(x_minus, -1)
    last_minus = ring(add(x_next[0], from_minus[0]), 1)
    last_plus = ring(add(x_prev[0], from_plus[0]), -1)
    early_own = add(x_own[0], last_minus, from_plus[1])
    early_give = add(x_own[1], last_plus, from_minus[1])
    early = add(early_own, pair(early_give))

    kept = add(keep, got)
    y_plus = jnp.stack([kept[2][:, 0], kept[1][:, 1]])
    y_minus = jnp.stack([kept[2][:, 1], kept[3][:, 0]])
    from_minus, from_plus = ring(y_plus, 1), ring(y_minus, -1)
    last_minus = ring(add(kept[1][:, 0], from_minus[0]), 1)
    last_plus = ring(add(kept[3][:, 1], from_plus[0]), -1)
    late = jnp.stack(
        [
            add(kept[0][:, 0], last_minus, from_plus[1]),
            add(kept[0][:, 1], last_plus, from_minus[1]),
        ],
        axis=1,
    )
    return early, late


def gather_sections(own):
    first, second = own[:FIRST], own[FIRST:]
    first_pair = pair(first)
    own_minus, own_plus = ring(first, 1), ring(first, -1)
    pair_minus, pair_plus = ring(first_pair, 1), ring(first_pair, -1)
    own_far, pair_far = ring(own_minus, 1), ring(pair_plus, -1)
    firsts = (first, first_pair, own_plus, pair_plus, own_far, pair_far, own_minus, pair_minus)

    half = second.shape[0] // 2
    x_minus, x_plus = ring(second, 1), ring(second, -1)
    x_far = jnp.concatenate([ring(x_minus[:half], 1), ring(x_plus[half:], -1)])
    mine = (second, x_plus, x_far, x_minus)
    theirs = [pair(v) for v in mine]
    seconds = [v for both in zip(mine, theirs) for v in both]
    return firsts, seconds


def fourier_tables():
    positions = np.arange(CHANNELS, dtype=np.int64)
    angle = (positions[:, None] * positions[None, :] % CHANNELS) * (2.0 * math.pi / CHANNELS)
    factor = 1.0 / math.sqrt(CHANNELS)
    cos_table = (np.cos(angle) * factor).astype(np.float32).astype(BF16)
    sin_table = (np.sin(angle) * factor).astype(np.float32).astype(BF16)
    return jnp.asarray(cos_table), jnp.asarray(sin_table)


def local(voltages, filter_taps, feed_tile, bad_feed, delays):
    x, y = lax.axis_index("x"), lax.axis_index("yh")
    section = feed_tile // PER
    place = (((section // 2 - x) % NX) * 2 + (section % 2 ^ y)) * PER + feed_tile % PER
    place = jnp.where(bad_feed == 0, place, -1)[None, :]
    cos_table, sin_table = fourier_tables()

    channel = (lax.axis_index(DEV) * LOCAL_CHANS + jnp.arange(LOCAL_CHANS, dtype=jnp.int32)).astype(F32)
    phase = delays[None, :, :] * channel[:, None, None] * (2.0 * math.pi / CHANNELS)
    weights = jnp.concatenate([jnp.cos(phase).astype(BF16), jnp.sin(phase).astype(BF16)], axis=2)

    early, late = reduce_sections(place, voltages)
    past = lax.ppermute(late, DEV, [(i, i + 1) for i in range(FRAMES // LOCAL_FRAMES - 1)])
    spec = spectra(early, late, past, filter_taps, cos_table, sin_table)
    turned = lax.all_to_all(spec.reshape(16, LOCAL_CHANS, 2, TILES), DEV, 0, 0, tiled=True)
    turned = turned.reshape(16, LOCAL_CHANS, 2, LOCAL_FRAMES, PER)
    own = jnp.transpose(turned, (1, 2, 4, 0, 3)).reshape(LOCAL_CHANS, 2, PER, FRAMES)
    firsts, seconds = gather_sections(own)
    rel = jnp.arange(8, dtype=jnp.int32)
    places = ((x + rel // 2) % NX) * 2 + (rel % 2 ^ y)
    return tuple(products(places.astype(jnp.int32), weights, firsts, seconds))


def solution(mesh):
    fine = Mesh(mesh.devices.reshape(NX, 2, 2, 4, 2), SECT + DEV)
    return jax.shard_map(
        local,
        mesh=fine,
        in_specs=(P(None, SECT, DEV), P(), P(SECT), P(SECT), P(SECT, None)),
        out_specs=(P(None, DEV, SECT, None), P(None, DEV, SECT, None)),
        check_vma=False,
    )
```

time: 658 us -> 150 us (0.23); the launches traced: 649 us -> 150 us
  waiting for transfers between devices: 298 us -> 35.4 us
  matrix products: 160 us -> 0 us
  local copies, waits for them, and re-layouts: 93.8 us -> 2.96 us
  Pallas kernels: 0 us -> 27.5 us
  other arithmetic: 43.1 us -> 20.1 us
  blocking collectives: 0 us -> 18.4 us
  between operations: 14.6 us -> 0.99 us
    dot_general x13 -> x0, matrix products: 160 us -> none  [the longest x1 21.1 us: transform(): jnp.dot(filtered[1], sine_table, preferred_element_type=jnp.float32)]
    all_to_all x1 -> x0, waiting for transfers between devices: 123 us -> none  [local(): lax.all_to_all(spectra, 'dev', split_axis=3, concat_axis=2, tiled=True)]
    reduce_scatter x1 -> x0, waiting for transfers between devices: 91 us -> none  [local(): lax.psum_scatter(partial_value, 'sect', scatter_dimension=1, tiled=True)]
    all_gather x1 -> x0, waiting for transfers between devices: 79.1 us -> none  [local(): gathered = lax.all_gather(own_tiles, 'sect', axis=1, tiled=True)]
    unnamed x17 -> x9, local copies, waits for them, and re-layouts: 58.6 us -> 0.03 us
    ppermute x1 -> x26, starting transfers between devices: 1.94 us -> 44.5 us  [the longest x18 26.4 us: ring(): return lax.ppermute(v, 'x', [(i, (i + by) % NX) for i in range(NX)])]
    all_to_all x1 -> x0, starting transfers between devices: 38.2 us -> none  [local(): lax.all_to_all(spectra, 'dev', split_axis=3, concat_axis=2, tiled=True)]
    ppermute x1 -> x26, waiting for transfers between devices: 5.04 us -> 35.4 us  [the longest x7 18.8 us: pair(): return lax.ppermute(v, 'yh', [(0, 1), (1, 0)])]
  transfers between devices with their start and end apart: 4 -> 26, of which waited for: 4 -> 8; matrix products, arithmetic and copies ran while one was open for 0% -> 14% of each run, Pallas kernels for 0% -> 3%
where the time goes in v1:
time: 150 us
  starting transfers between devices  44.5 us (30%)
  waiting for transfers between devices  35.4 us (24%)
  Pallas kernels  27.5 us (18%)
  other arithmetic  20.1 us (13%)
  blocking collectives  18.4 us (12%)
  local copies, waits for them, and re-layouts  2.96 us (2%)
    ppermute x18, starting transfers between devices, ring(): return lax.ppermute(v, 'x', [(i, (i + by) % NX) for i in range(NX)])  26.4 us
    ppermute x7, waiting for transfers between devices, pair(): return lax.ppermute(v, 'yh', [(0, 1), (1, 0)])  18.8 us
    all_to_all x1, blocking collectives, local(): lax.all_to_all(spec.reshape(16, LOCAL_CHANS, 2, TILES), DEV, 0, 0, tiled=...  18.4 us
    ppermute x7, starting transfers between devices, pair(): return lax.ppermute(v, 'yh', [(0, 1), (1, 0)])  16.8 us
    ppermute x18, waiting for transfers between devices, ring(): return lax.ppermute(v, 'x', [(i, (i + by) % NX) for i in range(NX)])  16.5 us
    convert_element_type x1, other arithmetic, local(): jnp.cos(phase).astype(BF16)  15.6 us
    pallas_call x1, Pallas kernels, products(): pl.pallas_call(products_kernel, grid_spec=pltpu.PrefetchScalarGridSpec(nu...  13.9 us
    pallas_call x2, Pallas kernels, tile_sums(): pl.pallas_call(functools.partial(tile_sums_kernel, groups), grid=(frames,...  11.3 us
  transfers between devices with their start and end apart: 26, of which 8 were waited for; matrix products, arithmetic and copies ran while one was open for 14% of the time, Pallas kernels for 3%

profile of v1, /device:TPU:6, one launch (start us, length us, event | category | flops | bytes accessed | tf_op | source)
XLA Modules:
  0.0 149.8 jit_solution(15586007318045598128)
XLA Ops:
  0.6 0.7 compare_select_fusion.4
  1.4 7.0 %shard_map.86 = (bf16[2,5,2,16,1024]{4,3,2,1,0:T(8,128)(2,1)S(1)}, bf16[2,5,2,16,1024]{4,3,2,1,0:T(8,128)(2,1)S(1)}, bf16[1,5,2,16,1024]{4,3,2,1,0:T(8,128)(2,1)...) custom-call(s32[1,256]{1,0:T(1,128)S(1)} %bitcast.93, bf16[2,256,8192]{2,1,0:T(8,128)(2,1)} %volts_ref.3), custom_call_target="tpu_custom_call" | custom-call | flops 671088640 | bytes 7864320 | tf_op jit(solution)/shard_map/pallas_call | solution.py:63
  8.4 0.5 collective-permute-start
  8.8 1.6 %collective-permute-start.2 = (bf16[2,5,2,16,1024]{4,3,2,1,0:T(8,128)(2,1)S(1)}, bf16[2,5,2,16,1024]{4,3,2,1,0:T(8,128)(2,1)S(1)}, u32[]{:S(2)}, u32[]{:S(2)}) collective-permute-start(bf16[2,5,2,16,1024]{4,3,2,1,0:T(8,128)(2,1)S(1)} %get-tuple-element.12), channel_id=1, source_target_pairs={{0,96},{32,0},{64,32},{96,64},{1,97},{33,1},{65,33},{97,65},{2,98}... | collective-permute-start | bytes 1966088 | tf_op jit(solution)/shard_map/ppermute | solution.py:34
  10.4 4.3 %shard_map.87 = (bf16[4,3,2,16,1024]{4,3,2,1,0:T(8,128)(2,1)S(1)}, bf16[4,3,2,16,1024]{4,3,2,1,0:T(8,128)(2,1)S(1)}) custom-call(s32[1,256]{1,0:T(1,128)S(1)} %bitcast.94, bf16[2,256,8192]{2,1,0:T(8,128)(2,1)} %volts_ref.3), custom_call_target="tpu_custom_call" | custom-call | flops 402653184 | bytes 4718592 | tf_op jit(solution)/shard_map/pallas_call | solution.py:63
  14.7 0.1 copy.27
  14.8 3.3 %collective-permute-start.5 = (bf16[4,3,2,16,1024]{4,3,1,2,0:T(8,128)(2,1)S(1)}, bf16[4,3,2,16,1024]{4,3,1,2,0:T(8,128)(2,1)S(1)}, u32[]{:S(2)}, u32[]{:S(2)}) collective-permute-start(bf16[4,3,2,16,1024]{4,3,1,2,0:T(8,128)(2,1)S(1)} %copy.27), channel_id=1, source_target_pairs={{0,16},{16,0},{1,17},{17,1},{2,18},{18,2},{3,19},{19,3},{4,20},{20... | collective-permute-start | bytes 2359304 | tf_op jit(solution)/shard_map/ppermute | solution.py:38
  18.1 6.8 %collective-permute-done = bf16[2,5,2,16,1024]{4,3,2,1,0:T(8,128)(2,1)S(1)} collective-permute-done((bf16[2,5,2,16,1024]{4,3,2,1,0:T(8,128)(2,1)S(1)}, bf16[2,5,2,16,1024]{4,3,2,1,0:T(8,128)(2,1)S(1)}, u32[]{:S(2)}, u32[]{:S(2)}) %collective-permute-start) | collective-permute-done | bytes 655392 | tf_op jit(solution)/shard_map/ppermute | solution.py:34
  24.9 0.1 fusion.2
  25.0 1.6 %collective-permute-start.1 = (bf16[5,2,16,1024]{3,2,1,0:T(8,128)(2,1)S(1)}, bf16[5,2,16,1024]{3,2,1,0:T(8,128)(2,1)S(1)}, u32[]{:S(2)}, u32[]{:S(2)}) collective-permute-start(bf16[5,2,16,1024]{3,2,1,0:T(8,128)(2,1)S(1)} %fusion.2), channel_id=1, source_target_pairs={{0,32},{32,64},{64,96},{96,0},{1,33},{33,65},{65,97},{97,1},{2,34}... | collective-permute-start | bytes 983048 | tf_op jit(solution)/shard_map/ppermute | solution.py:34
  26.6 0.0 collective-permute-done.2
  26.6 0.1 fusion.3
  26.7 0.6 collective-permute-start.3
  27.3 7.8 %collective-permute-done.5 = bf16[4,3,2,16,1024]{4,3,1,2,0:T(8,128)(2,1)S(1)} collective-permute-done((bf16[4,3,2,16,1024]{4,3,1,2,0:T(8,128)(2,1)S(1)}, bf16[4,3,2,16,1024]{4,3,1,2,0:T(8,128)(2,1)S(1)}, u32[]{:S(2)}, u32[]{:S(2)}) %collective-permute-start.5) | collective-permute-done | bytes 786464 | tf_op jit(solution)/shard_map/ppermute | solution.py:38
  35.1 0.3 add_convert_fusion
  35.4 0.0 copy-start
  35.5 0.0 copy-start.1
  35.5 0.0 copy-start.2
  35.5 0.1 slice_bitcast_fusion.5
  35.6 0.9 collective-permute-start.8
  36.5 2.5 %collective-permute-start.6 = (bf16[2,3,16,1024]{3,2,1,0:T(8,128)(2,1)S(1)}, bf16[2,3,16,1024]{3,2,1,0:T(8,128)(2,1)S(1)}, u32[]{:S(2)}, u32[]{:S(2)}) collective-permute-start(bf16[2,3,16,1024]{3,2,1,0:T(8,128)(2,1)S(1)} %pad_maximum_fusion.1), channel_id=1, source_target_pairs={{0,32},{32,64},{64,96},{96,0},{1,33},{33,65},{65,97},{97,1},{2,34}... | collective-permute-start | bytes 589832 | tf_op jit(solution)/shard_map/ppermute | solution.py:34
  39.0 3.5 %collective-permute-done.8 = bf16[2,3,16,1024]{3,2,1,0:T(8,128)(2,1)S(1)} collective-permute-done((bf16[2,3,16,1024]{3,2,1,0:T(8,128)(2,1)S(1)}, bf16[2,3,16,1024]{3,2,1,0:T(8,128)(2,1)S(1)}, u32[]{:S(2)}, u32[]{:S(2)}) %collective-permute-start.8) | collective-permute-done | bytes 196640 | tf_op jit(solution)/shard_map/ppermute | solution.py:34
  42.6 0.1 collective-permute-start.9
  42.7 0.0 collective-permute-done.6
  42.7 3.3 %collective-permute-start.7 = (bf16[3,16,1024]{2,1,0:T(8,128)(2,1)S(1)}, bf16[3,16,1024]{2,1,0:T(8,128)(2,1)S(1)}, u32[]{:S(2)}, u32[]{:S(2)}) collective-permute-start(bf16[3,16,1024]{2,1,0:T(8,128)(2,1)S(1)} %fusion.7), channel_id=1, source_target_pairs={{0,32},{32,64},{64,96},{96,0},{1,33},{33,65},{65,97},{97,1},{2,34}... | collective-permute-start | bytes 294920 | tf_op jit(solution)/shard_map/ppermute | solution.py:34
  46.0 0.0 collective-permute-done.3
  46.0 0.2 fusion
  46.2 3.3 %collective-permute-start.4 = (bf16[5,2,16,1024]{3,2,1,0:T(8,128)(2,1)S(1)}, bf16[5,2,16,1024]{3,2,1,0:T(8,128)(2,1)S(1)}, u32[]{:S(2)}, u32[]{:S(2)}) collective-permute-start(bf16[5,2,16,1024]{3,2,1,0:T(8,128)(2,1)S(1)} %fusion), channel_id=1, source_target_pairs={{0,16},{16,0},{1,17},{17,1},{2,18},{18,2},{3,19},{19,3},{4,20},{20... | collective-permute-start | bytes 983048 | tf_op jit(solution)/shard_map/ppermute | solution.py:38
  49.4 0.0 collective-permute-done.9
  49.5 0.0 collective-permute-done.7
  49.5 0.1 fusion.8
  49.6 1.3 collective-permute-start.10
  50.9 4.0 %collective-permute-done.4 = bf16[5,2,16,1024]{3,2,1,0:T(8,128)(2,1)S(1)} collective-permute-done((bf16[5,2,16,1024]{3,2,1,0:T(8,128)(2,1)S(1)}, bf16[5,2,16,1024]{3,2,1,0:T(8,128)(2,1)S(1)}, u32[]{:S(2)}, u32[]{:S(2)}) %collective-permute-start.4) | collective-permute-done | bytes 327712 | tf_op jit(solution)/shard_map/ppermute | solution.py:38
  54.8 0.2 add_convert_fusion.1.early_ref
  55.1 2.4 %shard_map.88 = bf16[1024,256]{1,0:T(8,128)(2,1)S(1)} custom-call(bf16[5,2,16,1024]{3,2,1,0:T(8,128)(2,1)S(1)} %add_convert_fusion.1.early_ref, bf16[3,2,16,1024]{3,2,1,0:T(8,128)(2,1)S(1)} %pad_maximum_fusion.3.late_ref, bf16[3,2,16,1024]{3,2,1,0:T(8,128)(2,1)S(1)} %collective-permute-done.10.past_ref, f32[4,1024]{1,0:T(4,128)S(1)} %copy-done.2, ...), custom_call_target="tpu_custom_call" | custom-call | flops 1073741824 | bytes 6291456 | tf_op jit(solution)/shard_map/pallas_call | solution.py:110
  57.5 0.1 reshape.51
  57.6 0.1 copy.29
  57.7 18.4 %all_to_all.5 = bf16[16,64,2,128]{3,1,2,0:T(8,128)(2,1)S(1)} all-to-all(bf16[16,64,2,128]{3,1,2,0:T(8,128)(2,1)S(1)} %copy.29), channel_id=1, replica_groups=mesh['x'=4,'yh'=2,'yl'=2,'z'=4,'core'=2] {'yl','z','core'}, dimensions={0} | all-to-all | bytes 1048576 | tf_op jit(solution)/shard_map/all_to_all | solution.py:266
  76.1 0.5 copy.30
  76.6 0.0 copy-start.3
  76.6 0.3 copy.45
  76.9 0.6 copy.39.refs_0_
  77.5 3.1 %collective-permute-start.11 = (bf16[36,2,16,128]{3,2,1,0:T(8,128)(2,1)S(1)}, bf16[36,2,16,128]{3,2,1,0:T(8,128)(2,1)S(1)}, u32[]{:S(2)}, u32[]{:S(2)}) collective-permute-start(bf16[36,2,16,128]{3,2,1,0:T(8,128)(2,1)S(1)} %copy.39.refs_0_), channel_id=1, source_target_pairs={{0,16},{16,0},{1,17},{17,1},{2,18},{18,2},{3,19},{19,3},{4,20},{20... | collective-permute-start | bytes 884744 | tf_op jit(solution)/shard_map/ppermute | solution.py:38
  80.6 0.4 slice.137
  80.9 0.3 copy.44
  81.2 0.5 copy.40.refs_8_
  81.7 2.5 %collective-permute-start.21 = (bf16[28,2,16,128]{3,2,1,0:T(8,128)(2,1)S(1)}, bf16[28,2,16,128]{3,2,1,0:T(8,128)(2,1)S(1)}, u32[]{:S(2)}, u32[]{:S(2)}) collective-permute-start(bf16[28,2,16,128]{3,2,1,0:T(8,128)(2,1)S(1)} %copy.40.refs_8_), channel_id=1, source_target_pairs={{0,32},{32,64},{64,96},{96,0},{1,33},{33,65},{65,97},{97,1},{2,34}... | collective-permute-start | bytes 688136 | tf_op jit(solution)/shard_map/ppermute | solution.py:34
  84.3 3.2 %collective-permute-start.14 = (bf16[36,2,16,128]{3,2,1,0:T(8,128)(2,1)S(1)}, bf16[36,2,16,128]{3,2,1,0:T(8,128)(2,1)S(1)}, u32[]{:S(2)}, u32[]{:S(2)}) collective-permute-start(bf16[36,2,16,128]{3,2,1,0:T(8,128)(2,1)S(1)} %copy.39.refs_0_), channel_id=1, source_target_pairs={{0,32},{32,64},{64,96},{96,0},{1,33},{33,65},{65,97},{97,1},{2,34}... | collective-permute-start | bytes 884744 | tf_op jit(solution)/shard_map/ppermute | solution.py:34
  87.5 2.8 %collective-permute-done.21.refs_14_ = bf16[28,2,16,128]{3,2,1,0:T(8,128)(2,1)S(1)} collective-permute-done((bf16[28,2,16,128]{3,2,1,0:T(8,128)(2,1)S(1)}, bf16[28,2,16,128]{3,2,1,0:T(8,128)(2,1)S(1)}, u32[]{:S(2)}, u32[]{:S(2)}) %collective-permute-start.21) | collective-permute-done | bytes 229408 | tf_op jit(solution)/shard_map/ppermute | solution.py:34
  90.3 3.7 %collective-permute-start.22 = (bf16[14,2,16,128]{3,2,1,0:T(8,128)(2,1)S(1)}, bf16[14,2,16,128]{3,2,1,0:T(8,128)(2,1)S(1)}, u32[]{:S(2)}, u32[]{:S(2)}) collective-permute-start(bf16[14,2,16,128]{3,2,1,0:T(8,128)(2,1)S(1)} %slice.138), channel_id=1, source_target_pairs={{0,32},{32,64},{64,96},{96,0},{1,33},{33,65},{65,97},{97,1},{2,34}... | collective-permute-start | bytes 344072 | tf_op jit(solution)/shard_map/ppermute | solution.py:34
  94.1 0.1 collective-permute-start.23
  94.2 0.3 collective-permute-start.13
  94.5 15.6 %cosine_convert_fusion = (bf16[64,128,128]{2,1,0:T(8,128)(2,1)S(1)}, bf16[64,128,128]{2,1,0:T(8,128)(2,1)S(1)}) fusion(f32[64]{0:T(128)S(1)} %add_convert_fusion.4, f32[128,128]{1,0:T(8,128)S(1)} %copy-done.3), kind=kLoop, calls=%fused_computation.2 | loop fusion | flops 4194304 | bytes 4260096 | tf_op jit(solution)/shard_map/convert_element_type | solution.py:261
  110.1 0.7 collective-permute-start.18
  110.8 2.9 %collective-permute-start.25 = (bf16[28,2,16,128]{3,2,1,0:T(8,128)(2,1)S(1)}, bf16[28,2,16,128]{3,2,1,0:T(8,128)(2,1)S(1)}, u32[]{:S(2)}, u32[]{:S(2)}) collective-permute-start(bf16[28,2,16,128]{3,2,1,0:T(8,128)(2,1)S(1)} %collective-permute-done.21.refs_14_), channel_id=1, source_target_pairs={{0,16},{16,0},{1,17},{17,1},{2,18},{18,2},{3,19},{19,3},{4,20},{20... | collective-permute-start | bytes 688136 | tf_op jit(solution)/shard_map/ppermute | solution.py:38
  113.7 5.1 %collective-permute-done.18.refs_9_ = bf16[28,2,16,128]{3,2,1,0:T(8,128)(2,1)S(1)} collective-permute-done((bf16[28,2,16,128]{3,2,1,0:T(8,128)(2,1)S(1)}, bf16[28,2,16,128]{3,2,1,0:T(8,128)(2,1)S(1)}, u32[]{:S(2)}, u32[]{:S(2)}) %collective-permute-start.18) | collective-permute-done | bytes 229408 | tf_op jit(solution)/shard_map/ppermute | solution.py:38
  118.8 0.6 collective-permute-start.20
  119.4 3.5 %collective-permute-start.17 = (bf16[36,2,16,128]{3,2,1,0:T(8,128)(2,1)S(1)}, bf16[36,2,16,128]{3,2,1,0:T(8,128)(2,1)S(1)}, u32[]{:S(2)}, u32[]{:S(2)}) collective-permute-start(bf16[36,2,16,128]{3,2,1,0:T(8,128)(2,1)S(1)} %collective-permute-done.11.refs_1_), channel_id=1, source_target_pairs={{0,32},{32,64},{64,96},{96,0},{1,33},{33,65},{65,97},{97,1},{2,34}... | collective-permute-start | bytes 884744 | tf_op jit(solution)/shard_map/ppermute | solution.py:34
  122.9 2.1 %collective-permute-start.15 = (bf16[36,2,16,128]{3,2,1,0:T(8,128)(2,1)S(1)}, bf16[36,2,16,128]{3,2,1,0:T(8,128)(2,1)S(1)}, u32[]{:S(2)}, u32[]{:S(2)}) collective-permute-start(bf16[36,2,16,128]{3,2,1,0:T(8,128)(2,1)S(1)} %collective-permute-done.14.refs_6_), channel_id=1, source_target_pairs={{0,32},{32,64},{64,96},{96,0},{1,33},{33,65},{65,97},{97,1},{2,34}... | collective-permute-start | bytes 884744 | tf_op jit(solution)/shard_map/ppermute | solution.py:34
  125.0 2.9 %collective-permute-start.24 = (bf16[28,2,16,128]{3,2,1,0:T(8,128)(2,1)S(1)}, bf16[28,2,16,128]{3,2,1,0:T(8,128)(2,1)S(1)}, u32[]{:S(2)}, u32[]{:S(2)}) collective-permute-start(bf16[28,2,16,128]{3,2,1,0:T(8,128)(2,1)S(1)} %constant_dynamic-update-slice_fusion.refs_12_), channel_id=1, source_target_pairs={{0,16},{16,0},{1,17},{17,1},{2,18},{18,2},{3,19},{19,3},{4,20},{20... | collective-permute-start | bytes 688136 | tf_op jit(solution)/shard_map/ppermute | solution.py:38
  127.9 2.6 %pad_maximum_fusion.weight_ref = bf16[64,128,256]{2,1,0:T(8,128)(2,1)} fusion(bf16[64,128,128]{2,1,0:T(8,128)(2,1)S(1)} %get-tuple-element.25, bf16[64,128,128]{2,1,0:T(8,128)(2,1)S(1)} %get-tuple-element.24), kind=kLoop, calls=%fused_computation | loop fusion | flops 8388608 | bytes 8388608 | tf_op jit(solution)/shard_map/concatenate | solution.py:261
  130.6 2.0 %collective-permute-done.24.refs_13_ = bf16[28,2,16,128]{3,2,1,0:T(8,128)(2,1)S(1)} collective-permute-done((bf16[28,2,16,128]{3,2,1,0:T(8,128)(2,1)S(1)}, bf16[28,2,16,128]{3,2,1,0:T(8,128)(2,1)S(1)}, u32[]{:S(2)}, u32[]{:S(2)}) %collective-permute-start.24) | collective-permute-done | bytes 229408 | tf_op jit(solution)/shard_map/ppermute | solution.py:38
  132.6 3.3 %collective-permute-done.16.refs_5_ = bf16[36,2,16,128]{3,2,1,0:T(8,128)(2,1)S(1)} collective-permute-done((bf16[36,2,16,128]{3,2,1,0:T(8,128)(2,1)S(1)}, bf16[36,2,16,128]{3,2,1,0:T(8,128)(2,1)S(1)}, u32[]{:S(2)}, u32[]{:S(2)}) %collective-permute-start.16) | collective-permute-done | bytes 294944 | tf_op jit(solution)/shard_map/ppermute | solution.py:34
  135.9 13.9 %shard_map.89 = (f32[2,64,16,128]{3,2,1,0:T(8,128)}, bf16[2,64,128,128]{3,2,1,0:T(8,128)(2,1)}) custom-call(s32[8]{0:T(128)S(1)} %fusion.16.places_ref, bf16[64,128,256]{2,1,0:T(8,128)(2,1)} %pad_maximum_fusion.weight_ref, bf16[36,2,16,128]{3,2,1,0:T(8,128)(2,1)S(1)} %copy.39.refs_0_, bf16[36,2,16,128]{3,2,1,0:T(8,128)(2,1)S(1)} %collective-permute-done.11.refs_1_, ...), custom_call_target="tpu_custom_call" | custom-call | flops 1342177280 | bytes 14680064 | tf_op jit(solution)/shard_map/pallas_call | solution.py:172
  (34 shorter events, 0.3 us)
Async XLA Ops:
  8.4 16.5 %collective-permute-start = (bf16[2,5,2,16,1024]{4,3,2,1,0:T(8,128)(2,1)S(1)}, bf16[2,5,2,16,1024]{4,3,2,1,0:T(8,128)(2,1)S(1)}, u32[]{:S(2)}, u32[]{:S(2)}) collective-permute-start(bf16[2,5,2,16,1024]{4,3,2,1,0:T(8,128)(2,1)S(1)} %get-tuple-element.11), channel_id=1, source_target_pairs={{0,32},{32,64},{64,96},{96,0},{1,33},{33,65},{65,97},{97,1},{2,34}... | collective-permute-start | bytes 1966088 | tf_op jit(solution)/shard_map/ppermute | solution.py:34
  8.8 17.8 %collective-permute-start.2 = (bf16[2,5,2,16,1024]{4,3,2,1,0:T(8,128)(2,1)S(1)}, bf16[2,5,2,16,1024]{4,3,2,1,0:T(8,128)(2,1)S(1)}, u32[]{:S(2)}, u32[]{:S(2)}) collective-permute-start(bf16[2,5,2,16,1024]{4,3,2,1,0:T(8,128)(2,1)S(1)} %get-tuple-element.12), channel_id=1, source_target_pairs={{0,96},{32,0},{64,32},{96,64},{1,97},{33,1},{65,33},{97,65},{2,98}... | collective-permute-start | bytes 1966088 | tf_op jit(solution)/shard_map/ppermute | solution.py:34
  14.8 20.3 %collective-permute-start.5 = (bf16[4,3,2,16,1024]{4,3,1,2,0:T(8,128)(2,1)S(1)}, bf16[4,3,2,16,1024]{4,3,1,2,0:T(8,128)(2,1)S(1)}, u32[]{:S(2)}, u32[]{:S(2)}) collective-permute-start(bf16[4,3,2,16,1024]{4,3,1,2,0:T(8,128)(2,1)S(1)} %copy.27), channel_id=1, source_target_pairs={{0,16},{16,0},{1,17},{17,1},{2,18},{18,2},{3,19},{19,3},{4,20},{20... | collective-permute-start | bytes 2359304 | tf_op jit(solution)/shard_map/ppermute | solution.py:38
  25.0 25.9 %collective-permute-start.1 = (bf16[5,2,16,1024]{3,2,1,0:T(8,128)(2,1)S(1)}, bf16[5,2,16,1024]{3,2,1,0:T(8,128)(2,1)S(1)}, u32[]{:S(2)}, u32[]{:S(2)}) collective-permute-start(bf16[5,2,16,1024]{3,2,1,0:T(8,128)(2,1)S(1)} %fusion.2), channel_id=1, source_target_pairs={{0,32},{32,64},{64,96},{96,0},{1,33},{33,65},{65,97},{97,1},{2,34}... | collective-permute-start | bytes 983048 | tf_op jit(solution)/shard_map/ppermute | solution.py:34
  26.7 19.3 %collective-permute-start.3 = (bf16[5,2,16,1024]{3,2,1,0:T(8,128)(2,1)S(1)}, bf16[5,2,16,1024]{3,2,1,0:T(8,128)(2,1)S(1)}, u32[]{:S(2)}, u32[]{:S(2)}) collective-permute-start(bf16[5,2,16,1024]{3,2,1,0:T(8,128)(2,1)S(1)} %fusion.3), channel_id=1, source_target_pairs={{0,96},{32,0},{64,32},{96,64},{1,97},{33,1},{65,33},{97,65},{2,98}... | collective-permute-start | bytes 983048 | tf_op jit(solution)/shard_map/ppermute | solution.py:34
  35.4 19.6 %copy-start = (bf16[1024,1024]{1,0:T(8,128)(2,1)S(1)}, bf16[1024,1024]{1,0:T(8,128)(2,1)}, u32[]{:S(2)}) copy-start(bf16[1024,1024]{1,0:T(8,128)(2,1)} %constant.116.clone.sin_ref) | copy-start | bytes 6291460
  35.5 19.6 %copy-start.1 = (bf16[1024,1024]{1,0:T(8,128)(2,1)S(1)}, bf16[1024,1024]{1,0:T(8,128)(2,1)}, u32[]{:S(2)}) copy-start(bf16[1024,1024]{1,0:T(8,128)(2,1)} %constant.115.clone.cos_ref) | copy-start | bytes 6291460
  35.5 19.6 %copy-start.2 = (f32[4,1024]{1,0:T(4,128)S(1)}, f32[4,1024]{1,0:T(4,128)}, u32[]{:S(2)}) copy-start(f32[4,1024]{1,0:T(4,128)} %taps_ref.1) | copy-start | bytes 49156
  35.6 6.9 %collective-permute-start.8 = (bf16[2,3,16,1024]{3,2,1,0:T(8,128)(2,1)S(1)}, bf16[2,3,16,1024]{3,2,1,0:T(8,128)(2,1)S(1)}, u32[]{:S(2)}, u32[]{:S(2)}) collective-permute-start(bf16[2,3,16,1024]{3,2,1,0:T(8,128)(2,1)S(1)} %pad_maximum_fusion.2), channel_id=1, source_target_pairs={{0,96},{32,0},{64,32},{96,64},{1,97},{33,1},{65,33},{97,65},{2,98}... | collective-permute-start | bytes 589832 | tf_op jit(solution)/shard_map/ppermute | solution.py:34
  36.5 6.1 %collective-permute-start.6 = (bf16[2,3,16,1024]{3,2,1,0:T(8,128)(2,1)S(1)}, bf16[2,3,16,1024]{3,2,1,0:T(8,128)(2,1)S(1)}, u32[]{:S(2)}, u32[]{:S(2)}) collective-permute-start(bf16[2,3,16,1024]{3,2,1,0:T(8,128)(2,1)S(1)} %pad_maximum_fusion.1), channel_id=1, source_target_pairs={{0,32},{32,64},{64,96},{96,0},{1,33},{33,65},{65,97},{97,1},{2,34}... | collective-permute-start | bytes 589832 | tf_op jit(solution)/shard_map/ppermute | solution.py:34
  42.6 6.9 %collective-permute-start.9 = (bf16[3,16,1024]{2,1,0:T(8,128)(2,1)S(1)}, bf16[3,16,1024]{2,1,0:T(8,128)(2,1)S(1)}, u32[]{:S(2)}, u32[]{:S(2)}) collective-permute-start(bf16[3,16,1024]{2,1,0:T(8,128)(2,1)S(1)} %fusion.5), channel_id=1, source_target_pairs={{0,96},{32,0},{64,32},{96,64},{1,97},{33,1},{65,33},{97,65},{2,98}... | collective-permute-start | bytes 294920 | tf_op jit(solution)/shard_map/ppermute | solution.py:34
  42.7 6.7 %collective-permute-start.7 = (bf16[3,16,1024]{2,1,0:T(8,128)(2,1)S(1)}, bf16[3,16,1024]{2,1,0:T(8,128)(2,1)S(1)}, u32[]{:S(2)}, u32[]{:S(2)}) collective-permute-start(bf16[3,16,1024]{2,1,0:T(8,128)(2,1)S(1)} %fusion.7), channel_id=1, source_target_pairs={{0,32},{32,64},{64,96},{96,0},{1,33},{33,65},{65,97},{97,1},{2,34}... | collective-permute-start | bytes 294920 | tf_op jit(solution)/shard_map/ppermute | solution.py:34
  46.2 8.7 %collective-permute-start.4 = (bf16[5,2,16,1024]{3,2,1,0:T(8,128)(2,1)S(1)}, bf16[5,2,16,1024]{3,2,1,0:T(8,128)(2,1)S(1)}, u32[]{:S(2)}, u32[]{:S(2)}) collective-permute-start(bf16[5,2,16,1024]{3,2,1,0:T(8,128)(2,1)S(1)} %fusion), channel_id=1, source_target_pairs={{0,16},{16,0},{1,17},{17,1},{2,18},{18,2},{3,19},{19,3},{4,20},{20... | collective-permute-start | bytes 983048 | tf_op jit(solution)/shard_map/ppermute | solution.py:38
  49.6 5.5 %collective-permute-start.10 = (bf16[3,2,16,1024]{3,2,1,0:T(8,128)(2,1)S(1)}, bf16[3,2,16,1024]{3,2,1,0:T(8,128)(2,1)S(1)}, u32[]{:S(2)}, u32[]{:S(2)}) collective-permute-start(bf16[3,2,16,1024]{3,2,1,0:T(8,128)(2,1)S(1)} %pad_maximum_fusion.3.late_ref), channel_id=1, source_target_pairs={{0,1},{1,2},{2,3},{3,4},{4,5},{5,6},{6,7},{7,8},{8,9},{9,10},{10,1... | collective-permute-start | bytes 589832 | tf_op jit(solution)/shard_map/ppermute | solution.py:264
  76.6 17.9 %copy-start.3 = (f32[128,128]{1,0:T(8,128)S(1)}, f32[128,128]{1,0:T(8,128)}, u32[]{:S(2)}) copy-start(f32[128,128]{1,0:T(8,128)} %param.11) | copy-start | bytes 196612
  77.5 16.7 %collective-permute-start.11 = (bf16[36,2,16,128]{3,2,1,0:T(8,128)(2,1)S(1)}, bf16[36,2,16,128]{3,2,1,0:T(8,128)(2,1)S(1)}, u32[]{:S(2)}, u32[]{:S(2)}) collective-permute-start(bf16[36,2,16,128]{3,2,1,0:T(8,128)(2,1)S(1)} %copy.39.refs_0_), channel_id=1, source_target_pairs={{0,16},{16,0},{1,17},{17,1},{2,18},{18,2},{3,19},{19,3},{4,20},{20... | collective-permute-start | bytes 884744 | tf_op jit(solution)/shard_map/ppermute | solution.py:38
  81.7 8.6 %collective-permute-start.21 = (bf16[28,2,16,128]{3,2,1,0:T(8,128)(2,1)S(1)}, bf16[28,2,16,128]{3,2,1,0:T(8,128)(2,1)S(1)}, u32[]{:S(2)}, u32[]{:S(2)}) collective-permute-start(bf16[28,2,16,128]{3,2,1,0:T(8,128)(2,1)S(1)} %copy.40.refs_8_), channel_id=1, source_target_pairs={{0,32},{32,64},{64,96},{96,0},{1,33},{33,65},{65,97},{97,1},{2,34}... | collective-permute-start | bytes 688136 | tf_op jit(solution)/shard_map/ppermute | solution.py:34
  84.3 9.8 %collective-permute-start.19 = (bf16[28,2,16,128]{3,2,1,0:T(8,128)(2,1)S(1)}, bf16[28,2,16,128]{3,2,1,0:T(8,128)(2,1)S(1)}, u32[]{:S(2)}, u32[]{:S(2)}) collective-permute-start(bf16[28,2,16,128]{3,2,1,0:T(8,128)(2,1)S(1)} %copy.40.refs_8_), channel_id=1, source_target_pairs={{0,96},{32,0},{64,32},{96,64},{1,97},{33,1},{65,33},{97,65},{2,98}... | collective-permute-start | bytes 688136 | tf_op jit(solution)/shard_map/ppermute | solution.py:34
  84.3 35.2 %collective-permute-start.14 = (bf16[36,2,16,128]{3,2,1,0:T(8,128)(2,1)S(1)}, bf16[36,2,16,128]{3,2,1,0:T(8,128)(2,1)S(1)}, u32[]{:S(2)}, u32[]{:S(2)}) collective-permute-start(bf16[36,2,16,128]{3,2,1,0:T(8,128)(2,1)S(1)} %copy.39.refs_0_), channel_id=1, source_target_pairs={{0,32},{32,64},{64,96},{96,0},{1,33},{33,65},{65,97},{97,1},{2,34}... | collective-permute-start | bytes 884744 | tf_op jit(solution)/shard_map/ppermute | solution.py:34
  87.5 35.5 %collective-permute-start.12 = (bf16[36,2,16,128]{3,2,1,0:T(8,128)(2,1)S(1)}, bf16[36,2,16,128]{3,2,1,0:T(8,128)(2,1)S(1)}, u32[]{:S(2)}, u32[]{:S(2)}) collective-permute-start(bf16[36,2,16,128]{3,2,1,0:T(8,128)(2,1)S(1)} %copy.39.refs_0_), channel_id=1, source_target_pairs={{0,96},{32,0},{64,32},{96,64},{1,97},{33,1},{65,33},{97,65},{2,98}... | collective-permute-start | bytes 884744 | tf_op jit(solution)/shard_map/ppermute | solution.py:34
  90.3 19.7 %collective-permute-start.22 = (bf16[14,2,16,128]{3,2,1,0:T(8,128)(2,1)S(1)}, bf16[14,2,16,128]{3,2,1,0:T(8,128)(2,1)S(1)}, u32[]{:S(2)}, u32[]{:S(2)}) collective-permute-start(bf16[14,2,16,128]{3,2,1,0:T(8,128)(2,1)S(1)} %slice.138), channel_id=1, source_target_pairs={{0,32},{32,64},{64,96},{96,0},{1,33},{33,65},{65,97},{97,1},{2,34}... | collective-permute-start | bytes 344072 | tf_op jit(solution)/shard_map/ppermute | solution.py:34
  94.1 16.7 %collective-permute-start.23 = (bf16[14,2,16,128]{3,2,1,0:T(8,128)(2,1)S(1)}, bf16[14,2,16,128]{3,2,1,0:T(8,128)(2,1)S(1)}, u32[]{:S(2)}, u32[]{:S(2)}) collective-permute-start(bf16[14,2,16,128]{3,2,1,0:T(8,128)(2,1)S(1)} %slice.139), channel_id=1, source_target_pairs={{0,96},{32,0},{64,32},{96,64},{1,97},{33,1},{65,33},{97,65},{2,98}... | collective-permute-start | bytes 344072 | tf_op jit(solution)/shard_map/ppermute | solution.py:34
  94.2 33.7 %collective-permute-start.13 = (bf16[36,2,16,128]{3,2,1,0:T(8,128)(2,1)S(1)}, bf16[36,2,16,128]{3,2,1,0:T(8,128)(2,1)S(1)}, u32[]{:S(2)}, u32[]{:S(2)}) collective-permute-start(bf16[36,2,16,128]{3,2,1,0:T(8,128)(2,1)S(1)} %collective-permute-done.11.refs_1_), channel_id=1, source_target_pairs={{0,96},{32,0},{64,32},{96,64},{1,97},{33,1},{65,33},{97,65},{2,98}... | collective-permute-start | bytes 884744 | tf_op jit(solution)/shard_map/ppermute | solution.py:34
  110.1 8.7 %collective-permute-start.18 = (bf16[28,2,16,128]{3,2,1,0:T(8,128)(2,1)S(1)}, bf16[28,2,16,128]{3,2,1,0:T(8,128)(2,1)S(1)}, u32[]{:S(2)}, u32[]{:S(2)}) collective-permute-start(bf16[28,2,16,128]{3,2,1,0:T(8,128)(2,1)S(1)} %copy.40.refs_8_), channel_id=1, source_target_pairs={{0,16},{16,0},{1,17},{17,1},{2,18},{18,2},{3,19},{19,3},{4,20},{20... | collective-permute-start | bytes 688136 | tf_op jit(solution)/shard_map/ppermute | solution.py:38
  110.8 14.2 %collective-permute-start.25 = (bf16[28,2,16,128]{3,2,1,0:T(8,128)(2,1)S(1)}, bf16[28,2,16,128]{3,2,1,0:T(8,128)(2,1)S(1)}, u32[]{:S(2)}, u32[]{:S(2)}) collective-permute-start(bf16[28,2,16,128]{3,2,1,0:T(8,128)(2,1)S(1)} %collective-permute-done.21.refs_14_), channel_id=1, source_target_pairs={{0,16},{16,0},{1,17},{17,1},{2,18},{18,2},{3,19},{19,3},{4,20},{20... | collective-permute-start | bytes 688136 | tf_op jit(solution)/shard_map/ppermute | solution.py:38
  118.8 11.8 %collective-permute-start.20 = (bf16[28,2,16,128]{3,2,1,0:T(8,128)(2,1)S(1)}, bf16[28,2,16,128]{3,2,1,0:T(8,128)(2,1)S(1)}, u32[]{:S(2)}, u32[]{:S(2)}) collective-permute-start(bf16[28,2,16,128]{3,2,1,0:T(8,128)(2,1)S(1)} %collective-permute-done.19.refs_10_), channel_id=1, source_target_pairs={{0,16},{16,0},{1,17},{17,1},{2,18},{18,2},{3,19},{19,3},{4,20},{20... | collective-permute-start | bytes 688136 | tf_op jit(solution)/shard_map/ppermute | solution.py:38
  119.4 13.1 %collective-permute-start.17 = (bf16[36,2,16,128]{3,2,1,0:T(8,128)(2,1)S(1)}, bf16[36,2,16,128]{3,2,1,0:T(8,128)(2,1)S(1)}, u32[]{:S(2)}, u32[]{:S(2)}) collective-permute-start(bf16[36,2,16,128]{3,2,1,0:T(8,128)(2,1)S(1)} %collective-permute-done.11.refs_1_), channel_id=1, source_target_pairs={{0,32},{32,64},{64,96},{96,0},{1,33},{33,65},{65,97},{97,1},{2,34}... | collective-permute-start | bytes 884744 | tf_op jit(solution)/shard_map/ppermute | solution.py:34
  122.9 9.6 %collective-permute-start.15 = (bf16[36,2,16,128]{3,2,1,0:T(8,128)(2,1)S(1)}, bf16[36,2,16,128]{3,2,1,0:T(8,128)(2,1)S(1)}, u32[]{:S(2)}, u32[]{:S(2)}) collective-permute-start(bf16[36,2,16,128]{3,2,1,0:T(8,128)(2,1)S(1)} %collective-permute-done.14.refs_6_), channel_id=1, source_target_pairs={{0,32},{32,64},{64,96},{96,0},{1,33},{33,65},{65,97},{97,1},{2,34}... | collective-permute-start | bytes 884744 | tf_op jit(solution)/shard_map/ppermute | solution.py:34
  125.0 7.5 %collective-permute-start.24 = (bf16[28,2,16,128]{3,2,1,0:T(8,128)(2,1)S(1)}, bf16[28,2,16,128]{3,2,1,0:T(8,128)(2,1)S(1)}, u32[]{:S(2)}, u32[]{:S(2)}) collective-permute-start(bf16[28,2,16,128]{3,2,1,0:T(8,128)(2,1)S(1)} %constant_dynamic-update-slice_fusion.refs_12_), channel_id=1, source_target_pairs={{0,16},{16,0},{1,17},{17,1},{2,18},{18,2},{3,19},{19,3},{4,20},{20... | collective-permute-start | bytes 688136 | tf_op jit(solution)/shard_map/ppermute | solution.py:38
  127.9 7.9 %collective-permute-start.16 = (bf16[36,2,16,128]{3,2,1,0:T(8,128)(2,1)S(1)}, bf16[36,2,16,128]{3,2,1,0:T(8,128)(2,1)S(1)}, u32[]{:S(2)}, u32[]{:S(2)}) collective-permute-start(bf16[36,2,16,128]{3,2,1,0:T(8,128)(2,1)S(1)} %collective-permute-done.13.refs_3_), channel_id=1, source_target_pairs={{0,96},{32,0},{64,32},{96,64},{1,97},{33,1},{65,33},{97,65},{2,98}... | collective-permute-start | bytes 884744 | tf_op jit(solution)/shard_map/ppermute | solution.py:34

commit v2 on v1

v2 whole, which is shorter than its diff:
```python
import functools
import math

import jax
import jax.numpy as jnp
import numpy as np
from jax import lax
from jax.experimental import pallas as pl
from jax.experimental.pallas import tpu as pltpu
from jax.sharding import Mesh
from jax.sharding import PartitionSpec as P

FEEDS = 2048
CHANNELS = 1024
TILES = 128
TAPS = 4
FRAMES = 128

SECT = ("x", "yh")
DEV = ("yl", "z", "core")
NX = 4
PER = 16
LOCAL_FRAMES = 8
LATE = 3
EARLY = LOCAL_FRAMES - LATE
LOCAL_CHANS = 64
FIRST = 40
STEP = 4
BF16 = jnp.bfloat16
F32 = jnp.float32


def ring(v, by):
    return lax.ppermute(v, "x", [(i, (i + by) % NX) for i in range(NX)])


def pair(v):
    return lax.ppermute(v, "yh", [(0, 1), (1, 0)])


def params(mib):
    return pltpu.CompilerParams(vmem_limit_bytes=mib * 1024 * 1024)


IN_VMEM = pl.BlockSpec(memory_space=pltpu.VMEM)
IN_SMEM = pl.BlockSpec(memory_space=pltpu.SMEM)
ANYWHERE = pl.BlockSpec(memory_space=pl.ANY)
IN_HBM = pl.BlockSpec(memory_space=pltpu.HBM)


def combine_kernel(layout, *refs):
    in_refs, out_refs = refs[: -len(layout)], refs[-len(layout) :]
    for out_ref, blocks in zip(out_refs, layout):
        for place, terms in enumerate(blocks):
            values = [in_refs[array][index] for array, index in terms]
            if len(values) > 1:
                total = values[0].astype(F32)
                for value in values[1:]:
                    total = total + value.astype(F32)
                values = [total.astype(BF16)]
            out_ref[place] = values[0]


def combine(arrays, layout, others=()):
    shapes = []
    for blocks in layout:
        array, index = blocks[0][0]
        shapes.append((len(blocks),) + jax.eval_shape(lambda a, index=index: a[index], arrays[array]).shape)
    return pl.pallas_call(
        functools.partial(combine_kernel, layout),
        in_specs=[IN_VMEM] * len(arrays) + [ANYWHERE] * len(others),
        out_specs=[IN_VMEM] * len(layout),
        out_shape=[jax.ShapeDtypeStruct(shape, BF16) for shape in shapes],
        compiler_params=params(4),
        cost_estimate=pl.CostEstimate(flops=1000, bytes_accessed=1000000, transcendentals=0),
    )(*arrays, *others)


def tile_sums_kernel(first, frames, groups, member_ref, volts_ref, *refs):
    out_refs, (chunk_ref, sems) = refs[-2 - len(groups) : -2], refs[-2:]
    copies = [
        pltpu.make_async_copy(
            volts_ref.at[z, :, pl.ds((first + t) * CHANNELS, CHANNELS)],
            chunk_ref.at[t, z],
            sems.at[t, z],
        )
        for t in range(frames)
        for z in range(2)
    ]
    for copy in copies:
        copy.start()
    for t in range(frames):
        for z in range(2):
            copies[t * 2 + z].wait()
            sums = jnp.dot(member_ref[...], chunk_ref[t, z], preferred_element_type=F32).astype(BF16)
            for out_ref, group in zip(out_refs, groups):
                for place, block in enumerate(group):
                    out_ref[place, t, z] = sums[block * PER : (block + 1) * PER]


def tile_sums(member, voltages, first, frames, groups, others=()):
    feeds = voltages.shape[1]
    return pl.pallas_call(
        functools.partial(tile_sums_kernel, first, frames, groups),
        in_specs=[IN_VMEM, IN_HBM] + [ANYWHERE] * len(others),
        out_specs=[IN_VMEM] * len(groups),
        out_shape=[jax.ShapeDtypeStruct((len(g), frames, 2, PER, CHANNELS), BF16) for g in groups],
        scratch_shapes=[
            pltpu.VMEM((frames, 2, feeds, CHANNELS), BF16),
            pltpu.SemaphoreType.DMA((frames, 2)),
        ],
        compiler_params=params(50),
        cost_estimate=pl.CostEstimate(
            flops=2 * TILES * feeds * CHANNELS * 2 * frames,
            bytes_accessed=2 * 2 * frames * CHANNELS * (feeds + TILES) * 2,
            transcendentals=0,
        ),
    )(member, voltages, *others)


def weights_kernel(base_ref, delays_ref, out_ref):
    @pl.loop(0, out_ref.shape[0])
    def _(c):
        channel = (base_ref[0] + c).astype(F32)
        quarters = (delays_ref[...] * channel) * (4.0 / CHANNELS)
        near = jnp.floor(quarters + 0.5)
        rest = quarters - near
        square = rest * rest
        sine = rest * (
            1.5707963267948966
            + square * (-0.6459640975062462 + square * (0.07969262624616703 + square * -0.004681754135318687))
        )
        cosine = 1.0 + square * (
            -1.2337005501361697
            + square * (0.253669507901048 + square * (-0.020863480763353 + square * 0.000919260274839426))
        )
        turn = near.astype(jnp.int32) & 3
        odd = (turn & 1) == 1
        cos_value, sin_value = jnp.where(odd, sine, cosine), jnp.where(odd, cosine, sine)
        cos_value = jnp.where((turn == 1) | (turn == 2), -cos_value, cos_value)
        sin_value = jnp.where(turn >= 2, -sin_value, sin_value)
        out_ref[c, :, 0:TILES] = cos_value.astype(BF16)
        out_ref[c, :, TILES : 2 * TILES] = sin_value.astype(BF16)


def beam_weights(base, delays, count):
    beams = delays.shape[0]
    return pl.pallas_call(
        weights_kernel,
        in_specs=[IN_SMEM, IN_VMEM],
        out_specs=IN_VMEM,
        out_shape=jax.ShapeDtypeStruct((count, beams, 2 * TILES), BF16),
        compiler_params=params(4),
        cost_estimate=pl.CostEstimate(
            flops=1000, bytes_accessed=count * 400 * 1024, transcendentals=0
        ),
    )(jnp.reshape(base, (1,)), delays)


def spectra_kernel(early_refs, late_ref, past_ref, taps_ref, cos_ref, sin_ref, out_ref, filt_ref):
    def frame(t, z):
        if t < 0:
            return past_ref[t + LATE, z].astype(F32)
        if t < EARLY:
            return early_refs[0][0, t, z].astype(F32) + early_refs[1][0, t, z].astype(F32)
        return late_ref[t - EARLY, z].astype(F32)

    @pl.when(pl.program_id(0) == 0)
    def _():
        for z in range(2):
            for t in range(LOCAL_FRAMES):
                total = taps_ref[0:1, :] * frame(t, z)
                for m in range(1, TAPS):
                    total = total + taps_ref[m : m + 1, :] * frame(t - m, z)
                filt_ref[z * TILES + t * PER : z * TILES + (t + 1) * PER, :] = total.astype(BF16)

    by_cos = jnp.dot(filt_ref[...], cos_ref[...], preferred_element_type=F32)
    by_sin = jnp.dot(filt_ref[...], sin_ref[...], preferred_element_type=F32)
    real = by_cos[0:128] + by_sin[128:256]
    quad = by_cos[128:256] - by_sin[0:128]
    for n in range(real.shape[1] // 128):
        lanes = slice(n * 128, (n + 1) * 128)
        own, other = real[:, lanes], quad[:, lanes]
        out_ref[2 * n] = jnp.concatenate([own[:, 0:64], other[:, 0:64]], axis=1).astype(BF16)
        out_ref[2 * n + 1] = jnp.concatenate([own[:, 64:128], other[:, 64:128]], axis=1).astype(BF16)


def spectra(early, late, past, taps, cos_table, sin_table):
    block = 512
    whole = lambda a: pl.BlockSpec(a.shape, lambda i: (0,) * a.ndim)
    columns = pl.BlockSpec((CHANNELS, block), lambda i: (0, i))

    def kernel(own_ref, got_ref, late_ref, past_ref, taps_ref, cos_ref, sin_ref, *refs):
        spectra_kernel((own_ref, got_ref), late_ref, past_ref, taps_ref, cos_ref, sin_ref, *refs[-2:])

    return pl.pallas_call(
        kernel,
        grid=(CHANNELS // block,),
        in_specs=[whole(a) for a in (*early, late, past, taps)] + [columns] * 2,
        out_specs=pl.BlockSpec((block // LOCAL_CHANS, TILES, 128), lambda i: (i, 0, 0)),
        out_shape=jax.ShapeDtypeStruct((CHANNELS // LOCAL_CHANS, TILES, 128), BF16),
        scratch_shapes=[pltpu.VMEM((256, CHANNELS), BF16)],
        compiler_params=params(12),
        cost_estimate=pl.CostEstimate(
            flops=2 * 2 * 256 * CHANNELS * CHANNELS, bytes_accessed=6 * 1024 * 1024, transcendentals=0
        ),
    )(*early, late, past, taps, cos_table, sin_table)


def turn_kernel(in_ref, first_ref, second_ref, wide_ref, turned_ref):
    for d in range(in_ref.shape[0]):
        wide_ref[d * TILES : (d + 1) * TILES] = in_ref[d].astype(F32)
    for a in range(PER):
        turned_ref[pl.ds(a, 128, stride=PER)] = wide_ref[pl.ds(a, 128, stride=PER)].T
    for z in range(2):
        for ref, begin in ((first_ref, 0), (second_ref, FIRST)):
            for c in range(ref.shape[0]):
                row = (z * LOCAL_CHANS + begin + c) * PER
                ref[c, z] = turned_ref[row : row + PER].astype(BF16)


def turn(value):
    return pl.pallas_call(
        turn_kernel,
        in_specs=[IN_VMEM],
        out_specs=[IN_VMEM] * 2,
        out_shape=[jax.ShapeDtypeStruct((n, 2, PER, FRAMES), BF16) for n in (FIRST, LOCAL_CHANS - FIRST)],
        scratch_shapes=[pltpu.VMEM((FRAMES * PER, 128), F32)] * 2,
        compiler_params=params(4),
        cost_estimate=pl.CostEstimate(flops=1000, bytes_accessed=4000000, transcendentals=0),
    )(value)


def products_kernel(begin, blocks, places_ref, weight_ref, block_refs, vis_ref, beam_ref, both_ref, vis_out, beam_out, vis_sem, beam_sem):
    vis_scale = 1.0 / (FRAMES * FEEDS / TILES)
    beam_scale = 1.0 / math.sqrt(FEEDS)
    dims = (((1,), (1,)), ((), ()))
    steps = weight_ref.shape[0] // STEP

    def copies(step):
        here, there = pl.ds(step * STEP, STEP), pl.ds(begin + step * STEP, STEP)
        return [
            pltpu.make_async_copy(source.at[z, here], target.at[z, there], sem.at[z, step])
            for source, target, sem in ((vis_out, vis_ref, vis_sem), (beam_out, beam_ref, beam_sem))
            for z in range(2)
        ]

    @pl.loop(0, steps)
    def _(step):
        for c in range(STEP):
            here = step * STEP + c
            for place, (array, index) in enumerate(blocks):
                row = pl.multiple_of(places_ref[place] * PER, PER)
                real, quad = block_refs[array][index, here, 0], block_refs[array][index, here, 1]
                both_ref[c, pl.ds(row, PER), 0:128] = real
                both_ref[c, pl.ds(row, PER), 128:256] = quad
                both_ref[c, pl.ds(TILES + row, PER), 0:128] = quad
                both_ref[c, pl.ds(TILES + row, PER), 128:256] = -real
        for c in range(STEP):
            here = step * STEP + c
            beams = jnp.dot(weight_ref[here], both_ref[c], preferred_element_type=F32) * beam_scale
            beam_out[0, here] = beams[:, 0:128].astype(BF16)
            beam_out[1, here] = beams[:, 128:256].astype(BF16)
            array, index = blocks[0]
            real, quad = block_refs[array][index, here, 0], block_refs[array][index, here, 1]
            mine = jnp.concatenate(
                [jnp.concatenate([real, quad], axis=1), jnp.concatenate([quad, -real], axis=1)], axis=0
            )
            vis = lax.dot_general(mine, both_ref[c, 0:TILES], dims, preferred_element_type=F32) * vis_scale
            vis_out[0, here] = vis[:PER]
            vis_out[1, here] = vis[PER:]
        for copy in copies(step):
            copy.start()

    @pl.loop(0, steps)
    def _(step):
        for copy in copies(step):
            copy.wait()


def products(places, weights, begin, blocks, results=()):
    arrays, layout = [], []
    for array, index in blocks:
        if not any(array is a for a in arrays):
            arrays.append(array)
        layout.append((next(n for n, a in enumerate(arrays) if a is array), index))
    count, beams = weights.shape[:2]

    def kernel(places_ref, weight_ref, *refs):
        products_kernel(begin, layout, places_ref, weight_ref, refs[: len(arrays)], *refs[len(arrays) + len(results) :])

    return pl.pallas_call(
        kernel,
        in_specs=[IN_SMEM] + [IN_VMEM] * (1 + len(arrays)) + [IN_HBM] * len(results),
        out_specs=[IN_HBM, IN_HBM],
        out_shape=[
            jax.ShapeDtypeStruct((2, LOCAL_CHANS, PER, TILES), F32),
            jax.ShapeDtypeStruct((2, LOCAL_CHANS, beams, FRAMES), BF16),
        ],
        scratch_shapes=[
            pltpu.VMEM((STEP, 2 * TILES, 256), BF16),
            pltpu.VMEM((2, count, PER, TILES), F32),
            pltpu.VMEM((2, count, beams, FRAMES), BF16),
            pltpu.SemaphoreType.DMA((2, count // STEP)),
            pltpu.SemaphoreType.DMA((2, count // STEP)),
        ],
        input_output_aliases={2 + len(arrays) + n: n for n in range(len(results))},
        compiler_params=params(8),
        cost_estimate=pl.CostEstimate(
            flops=2 * count * 160 * 256 * 256, bytes_accessed=count * 400 * 1024, transcendentals=0
        ),
    )(places, weights, *arrays, *results)


def reduce_sections(member, voltages, others):
    x_plus, x_minus, x_rest = tile_sums(member, voltages, 0, EARLY, ((4, 3), (5, 6), (0, 1, 2, 7)))
    keep, give = tile_sums(member, voltages, EARLY, LATE, ((0, 2, 4, 6), (1, 3, 5, 7)), (x_rest,))
    got = pair(give)
    from_minus, from_plus = ring(x_plus, 1), ring(x_minus, -1)
    x_next, x_prev = combine(
        (x_rest, from_minus, from_plus), ([[(0, 2), (1, 0)]], [[(0, 3), (2, 0)]]), others
    )
    last_minus, last_plus = ring(x_next, 1), ring(x_prev, -1)
    early_own, early_give = combine(
        (x_rest, last_minus, last_plus, from_minus, from_plus),
        ([[(0, 0), (1, 0), (4, 1)]], [[(0, 1), (2, 0), (3, 1)]]),
    )
    early = (early_own, pair(early_give))

    y_own, y_next, y_far, y_prev = combine(
        (keep, got), [[[(0, (rx, t)), (1, (rx, t))] for t in range(LATE)] for rx in range(NX)]
    )
    (late,) = combine(
        (y_own, ring(y_next, 1), ring(y_far, 2), ring(y_prev, 3)),
        ([[(n, t) for n in range(NX)] for t in range(LATE)],),
    )
    return early, late


def gather_sections(first, second):
    (both,) = combine((first, pair(first)), ([[(0, slice(None))], [(1, slice(None))]],))
    both_minus, both_plus = ring(both, 1), ring(both, -1)
    own_far, pair_far = ring(both_minus[:1], 1), ring(both_plus[1:], -1)
    firsts = ((both, 0), (both, 1), (both_plus, 0), (both_plus, 1))
    firsts += ((own_far, 0), (pair_far, 0), (both_minus, 0), (both_minus, 1))

    (mine,) = combine(
        (second, ring(second, -1), ring(second, 2), ring(second, 1)), ([[(n, slice(None))] for n in range(NX)],)
    )
    theirs = pair(mine)
    seconds = tuple((v, n) for n in range(NX) for v in (mine, theirs))
    return firsts, seconds


def fourier_tables():
    positions = np.arange(CHANNELS, dtype=np.int64)
    angle = (positions[:, None] * positions[None, :] % CHANNELS) * (2.0 * math.pi / CHANNELS)
    factor = 1.0 / math.sqrt(CHANNELS)
    cos_table = (np.cos(angle) * factor).astype(np.float32).astype(BF16)
    sin_table = (np.sin(angle) * factor).astype(np.float32).astype(BF16)
    return jnp.asarray(cos_table), jnp.asarray(sin_table)


def local(voltages, filter_taps, feed_tile, bad_feed, delays):
    x, y = lax.axis_index("x"), lax.axis_index("yh")
    section = feed_tile // PER
    place = (((section // 2 - x) % NX) * 2 + (section % 2 ^ y)) * PER + feed_tile % PER
    place = jnp.where(bad_feed == 0, place, -1)
    member = (jnp.arange(TILES, dtype=jnp.int32)[:, None] == place[None, :]).astype(BF16)
    cos_table, sin_table = fourier_tables()
    base = (lax.axis_index(DEV) * LOCAL_CHANS).astype(jnp.int32)
    counts = (FIRST, LOCAL_CHANS - FIRST)
    weights = [beam_weights(base + b, delays, n) for b, n in zip((0, FIRST), counts)]

    early, late = reduce_sections(member, voltages, weights)
    past = lax.ppermute(late, DEV, [(i, i + 1) for i in range(FRAMES // LOCAL_FRAMES - 1)])
    spec = spectra(early, late, past, filter_taps, cos_table, sin_table)
    first, second = turn(lax.all_to_all(spec, DEV, 0, 0, tiled=True))
    rel = jnp.arange(8, dtype=jnp.int32)
    places = ((x + rel // 2) % NX) * 2 + (rel % 2 ^ y)
    places = places.astype(jnp.int32)
    firsts, seconds = gather_sections(first, second)
    results = products(places, weights[1], FIRST, seconds)
    return tuple(products(places, weights[0], 0, firsts, results))


def solution(mesh):
    fine = Mesh(mesh.devices.reshape(NX, 2, 2, 4, 2), SECT + DEV)
    return jax.shard_map(
        local,
        mesh=fine,
        in_specs=(P(None, SECT, DEV), P(), P(SECT), P(SECT), P(SECT, None)),
        out_specs=(P(None, DEV, SECT, None), P(None, DEV, SECT, None)),
        check_vma=False,
    )
```

time: 150 us -> 118 us (0.79)
  other arithmetic: 20.1 us -> 0.76 us
  starting transfers between devices: 44.5 us -> 25.7 us
  waiting for transfers between devices: 35.4 us -> 41.4 us
  blocking collectives: 18.4 us -> 21.8 us
  local copies, waits for them, and re-layouts: 2.96 us -> 0.06 us
    convert_element_type x9 -> x1, other arithmetic: 16.5 us -> 0.02 us  [local(): (jnp.arange(TILES, dtype=jnp.int32)[:, None] == place[None, :]).astype(BF16)]
    ppermute x18 -> x14, starting transfers between devices: 26.4 us -> 14.7 us  [ring(): return lax.ppermute(v, 'x', [(i, (i + by) % NX) for i in range(NX)])]
    ppermute x18 -> x14, waiting for transfers between devices: 16.5 us -> 24.1 us  [ring(): return lax.ppermute(v, 'x', [(i, (i + by) % NX) for i in range(NX)])]
    ppermute x7 -> x4, starting transfers between devices: 16.8 us -> 9.73 us  [pair(): return lax.ppermute(v, 'yh', [(0, 1), (1, 0)])]
    all_to_all x1, blocking collectives: 18.4 us -> 21.8 us  [local(): first, second = turn(lax.all_to_all(spec, DEV, 0, 0, tiled=True))]
    concatenate x1 -> x0, other arithmetic: 2.64 us -> none  [local(): jnp.concatenate([jnp.cos(phase).astype(BF16), jnp.sin(phase).astype(BF16)...]
    ppermute x7 -> x4, waiting for transfers between devices: 18.8 us -> 16.2 us  [pair(): return lax.ppermute(v, 'yh', [(0, 1), (1, 0)])]
    slice x7 -> x2, local copies, waits for them, and re-layouts: 2.02 us -> 0.04 us  [gather_sections(): own_far, pair_far = (ring(both_minus[:1], 1), ring(both_plus[1:], -1))]
  transfers between devices with their start and end apart: 26 -> 19, of which waited for: 8 -> 13; matrix products, arithmetic and copies ran while one was open for 14% -> 0% of each run, Pallas kernels for 3% -> 13%
where the time goes in v2:
time: 118 us
  waiting for transfers between devices  41.4 us (35%)
  Pallas kernels  27.8 us (24%)
  starting transfers between devices  25.7 us (22%)
  blocking collectives  21.8 us (18%)
    ppermute x14, waiting for transfers between devices, ring(): return lax.ppermute(v, 'x', [(i, (i + by) % NX) for i in range(NX)])  24.1 us
    all_to_all x1, blocking collectives, local(): first, second = turn(lax.all_to_all(spec, DEV, 0, 0, tiled=True))  21.8 us
    ppermute x4, waiting for transfers between devices, pair(): return lax.ppermute(v, 'yh', [(0, 1), (1, 0)])  16.2 us
    ppermute x14, starting transfers between devices, ring(): return lax.ppermute(v, 'x', [(i, (i + by) % NX) for i in range(NX)])  14.7 us
    ppermute x4, starting transfers between devices, pair(): return lax.ppermute(v, 'yh', [(0, 1), (1, 0)])  9.73 us
    pallas_call x2, Pallas kernels, products(): pl.pallas_call(kernel, in_specs=[IN_SMEM] + [IN_VMEM] * (1 + len(arrays))...  9.07 us
    pallas_call x2, Pallas kernels, tile_sums(): pl.pallas_call(functools.partial(tile_sums_kernel, first, frames, groups)...  8.01 us
    pallas_call x2, Pallas kernels, beam_weights(): pl.pallas_call(weights_kernel, in_specs=[IN_SMEM, IN_VMEM], out_specs=IN_...  5.69 us
  transfers between devices with their start and end apart: 19, of which 13 were waited for; matrix products, arithmetic and copies ran while one was open for 0% of the time, Pallas kernels for 13%

profile of v2, /device:TPU:6, one launch (start us, length us, event | category | flops | bytes accessed | tf_op | source)
XLA Modules:
  0.0 118.3 jit_solution(12395239446584776565)
XLA Ops:
  0.6 0.7 compare_select_fusion.4
  1.4 4.6 %shard_map.87 = (bf16[2,5,2,16,1024]{4,3,2,1,0:T(8,128)(2,1)}, bf16[2,5,2,16,1024]{4,3,2,1,0:T(8,128)(2,1)}, bf16[4,5,2,16,1024]{4,3,2,1,0:T(8,128)(2,1)S(1)}) custom-call(bf16[128,256]{1,0:T(8,128)(2,1)S(1)} %fusion.member_ref, bf16[2,256,8192]{2,1,0:T(8,128)(2,1)} %volts_ref.3), custom_call_target="tpu_custom_call" | custom-call | flops 671088640 | bytes 15728640 | tf_op jit(solution)/shard_map/pallas_call | solution.py:103
  6.0 0.5 collective-permute-start
  6.4 1.6 %collective-permute-start.1 = (bf16[2,5,2,16,1024]{4,3,2,1,0:T(8,128)(2,1)}, bf16[2,5,2,16,1024]{4,3,2,1,0:T(8,128)(2,1)S(1)}, u32[]{:S(2)}, u32[]{:S(2)}) collective-permute-start(bf16[2,5,2,16,1024]{4,3,2,1,0:T(8,128)(2,1)} %get-tuple-element.21), channel_id=1, source_target_pairs={{0,96},{32,0},{64,32},{96,64},{1,97},{33,1},{65,33},{97,65},{2,98}... | collective-permute-start | bytes 1966088 | tf_op jit(solution)/shard_map/ppermute | solution.py:34
  8.1 0.0 copy-start.2
  8.1 3.4 %shard_map.91 = (bf16[4,3,2,16,1024]{4,3,2,1,0:T(8,128)(2,1)S(1)}, bf16[4,3,2,16,1024]{4,3,2,1,0:T(8,128)(2,1)}) custom-call(bf16[128,256]{1,0:T(8,128)(2,1)S(1)} %fusion.member_ref, bf16[2,256,8192]{2,1,0:T(8,128)(2,1)} %volts_ref.3, bf16[4,5,2,16,1024]{4,3,2,1,0:T(8,128)(2,1)S(1)} %get-tuple-element.19.refs_0_), custom_call_target="tpu_custom_call" | custom-call | flops 402653184 | bytes 9437184 | tf_op jit(solution)/shard_map/pallas_call | solution.py:103
  11.5 3.3 %collective-permute-start.5 = (bf16[4,3,2,16,1024]{4,3,2,1,0:T(8,128)(2,1)}, bf16[4,3,2,16,1024]{4,3,2,1,0:T(8,128)(2,1)}, u32[]{:S(2)}, u32[]{:S(2)}) collective-permute-start(bf16[4,3,2,16,1024]{4,3,2,1,0:T(8,128)(2,1)} %get-tuple-element.27), channel_id=1, source_target_pairs={{0,16},{16,0},{1,17},{17,1},{2,18},{18,2},{3,19},{19,3},{4,20},{20... | collective-permute-start | bytes 2359304 | tf_op jit(solution)/shard_map/ppermute | solution.py:38
  14.8 0.0 copy-done.2
  14.8 2.1 %shard_map.88.refs_4_.weight_ref = bf16[24,128,256]{2,1,0:T(8,128)(2,1)S(1)} custom-call(s32[1]{0:T(128)} %bitcast.1.base_ref, f32[128,128]{1,0:T(8,128)S(1)} %copy-done.2), custom_call_target="tpu_custom_call" | custom-call | flops 1000 | bytes 9830400 | tf_op jit(solution)/shard_map/pallas_call | solution.py:148
  16.9 3.6 %shard_map.86.refs_3_.weight_ref = bf16[40,128,256]{2,1,0:T(8,128)(2,1)S(1)} custom-call(s32[1]{0:T(128)} %bitcast.base_ref, f32[128,128]{1,0:T(8,128)S(1)} %copy-done.2), custom_call_target="tpu_custom_call" | custom-call | flops 1000 | bytes 16384000 | tf_op jit(solution)/shard_map/pallas_call | solution.py:148
  20.5 2.2 %collective-permute-done.refs_1_.refs_3_ = bf16[2,5,2,16,1024]{4,3,2,1,0:T(8,128)(2,1)S(1)} collective-permute-done((bf16[2,5,2,16,1024]{4,3,2,1,0:T(8,128)(2,1)}, bf16[2,5,2,16,1024]{4,3,2,1,0:T(8,128)(2,1)S(1)}, u32[]{:S(2)}, u32[]{:S(2)}) %collective-permute-start) | collective-permute-done | bytes 655392 | tf_op jit(solution)/shard_map/ppermute | solution.py:34
  22.7 1.3 %collective-permute-done.1.refs_2_.refs_4_ = bf16[2,5,2,16,1024]{4,3,2,1,0:T(8,128)(2,1)S(1)} collective-permute-done((bf16[2,5,2,16,1024]{4,3,2,1,0:T(8,128)(2,1)}, bf16[2,5,2,16,1024]{4,3,2,1,0:T(8,128)(2,1)S(1)}, u32[]{:S(2)}, u32[]{:S(2)}) %collective-permute-start.1) | collective-permute-done | bytes 655392 | tf_op jit(solution)/shard_map/ppermute | solution.py:34
  24.0 0.2 shard_map.89
  24.2 0.5 collective-permute-start.2
  24.6 1.6 %collective-permute-start.3 = (bf16[1,5,2,16,1024]{4,3,2,1,0:T(8,128)(2,1)S(1)}, bf16[1,5,2,16,1024]{4,3,2,1,0:T(8,128)(2,1)S(1)}, u32[]{:S(2)}, u32[]{:S(2)}) collective-permute-start(bf16[1,5,2,16,1024]{4,3,2,1,0:T(8,128)(2,1)S(1)} %get-tuple-element.23), channel_id=1, source_target_pairs={{0,96},{32,0},{64,32},{96,64},{1,97},{33,1},{65,33},{97,65},{2,98}... | collective-permute-start | bytes 983048 | tf_op jit(solution)/shard_map/ppermute | solution.py:34
  26.3 5.9 %collective-permute-done.5.refs_1_ = bf16[4,3,2,16,1024]{4,3,2,1,0:T(8,128)(2,1)} collective-permute-done((bf16[4,3,2,16,1024]{4,3,2,1,0:T(8,128)(2,1)}, bf16[4,3,2,16,1024]{4,3,2,1,0:T(8,128)(2,1)}, u32[]{:S(2)}, u32[]{:S(2)}) %collective-permute-start.5) | collective-permute-done | bytes 786464 | tf_op jit(solution)/shard_map/ppermute | solution.py:38
  32.1 0.0 copy-start
  32.1 0.0 copy-start.1
  32.1 0.0 copy-start.3
  32.1 1.5 %shard_map.92 = (bf16[3,2,16,1024]{3,2,1,0:T(8,128)(2,1)S(1)}, bf16[3,2,16,1024]{3,2,1,0:T(8,128)(2,1)S(1)}, bf16[3,2,16,1024]{3,2,1,0:T(8,128)(2,1)S(1)}, bf16[3,2,16,1024]{3,2,1,0:T(8,128)(2,1)S(1)}) custom-call(bf16[4,3,2,16,1024]{4,3,2,1,0:T(8,128)(2,1)S(1)} %get-tuple-element.26.refs_0_, bf16[4,3,2,16,1024]{4,3,2,1,0:T(8,128)(2,1)} %collective-permute-done.5.refs_1_), custom_call_target="tpu_custom_call" | custom-call | flops 1000 | bytes 1000000 | tf_op jit(solution)/shard_map/pallas_call | solution.py:69
  33.6 1.7 %collective-permute-start.6 = (bf16[3,2,16,1024]{3,2,1,0:T(8,128)(2,1)S(1)}, bf16[3,2,16,1024]{3,2,1,0:T(8,128)(2,1)S(1)}, u32[]{:S(2)}, u32[]{:S(2)}) collective-permute-start(bf16[3,2,16,1024]{3,2,1,0:T(8,128)(2,1)S(1)} %get-tuple-element.29), channel_id=1, source_target_pairs={{0,32},{32,64},{64,96},{96,0},{1,33},{33,65},{65,97},{97,1},{2,34}... | collective-permute-start | bytes 589832 | tf_op jit(solution)/shard_map/ppermute | solution.py:34
  35.3 1.3 %collective-permute-start.7 = (bf16[3,2,16,1024]{3,2,1,0:T(8,128)(2,1)S(1)}, bf16[3,2,16,1024]{3,2,1,0:T(8,128)(2,1)S(1)}, u32[]{:S(2)}, u32[]{:S(2)}) collective-permute-start(bf16[3,2,16,1024]{3,2,1,0:T(8,128)(2,1)S(1)} %get-tuple-element.30), channel_id=1, source_target_pairs={{0,64},{32,96},{64,0},{96,32},{1,65},{33,97},{65,1},{97,33},{2,66}... | collective-permute-start | bytes 589832 | tf_op jit(solution)/shard_map/ppermute | solution.py:34
  36.6 0.0 collective-permute-start.8
  36.6 0.0 collective-permute-done.2.refs_1_
  36.6 0.0 collective-permute-done.3.refs_2_
  36.6 0.2 shard_map.90
  36.8 3.3 %collective-permute-start.4 = (bf16[1,5,2,16,1024]{4,3,2,1,0:T(8,128)(2,1)S(1)}, bf16[1,5,2,16,1024]{4,3,2,1,0:T(8,128)(2,1)S(1)}, u32[]{:S(2)}, u32[]{:S(2)}) collective-permute-start(bf16[1,5,2,16,1024]{4,3,2,1,0:T(8,128)(2,1)S(1)} %get-tuple-element.25), channel_id=1, source_target_pairs={{0,16},{16,0},{1,17},{17,1},{2,18},{18,2},{3,19},{19,3},{4,20},{20... | collective-permute-start | bytes 983048 | tf_op jit(solution)/shard_map/ppermute | solution.py:38
  40.1 0.8 collective-permute-done.6.refs_1_
  40.9 3.0 %collective-permute-done.7.refs_2_ = bf16[3,2,16,1024]{3,2,1,0:T(8,128)(2,1)S(1)} collective-permute-done((bf16[3,2,16,1024]{3,2,1,0:T(8,128)(2,1)S(1)}, bf16[3,2,16,1024]{3,2,1,0:T(8,128)(2,1)S(1)}, u32[]{:S(2)}, u32[]{:S(2)}) %collective-permute-start.7) | collective-permute-done | bytes 196640 | tf_op jit(solution)/shard_map/ppermute | solution.py:34
  43.9 2.0 %collective-permute-done.8.refs_3_ = bf16[3,2,16,1024]{3,2,1,0:T(8,128)(2,1)S(1)} collective-permute-done((bf16[3,2,16,1024]{3,2,1,0:T(8,128)(2,1)S(1)}, bf16[3,2,16,1024]{3,2,1,0:T(8,128)(2,1)S(1)}, u32[]{:S(2)}, u32[]{:S(2)}) %collective-permute-start.8) | collective-permute-done | bytes 196640 | tf_op jit(solution)/shard_map/ppermute | solution.py:34
  45.9 0.1 shard_map.93.late_ref
  46.0 1.3 %collective-permute-start.9 = (bf16[3,2,16,1024]{3,2,1,0:T(8,128)(2,1)S(1)}, bf16[3,2,16,1024]{3,2,1,0:T(8,128)(2,1)S(1)}, u32[]{:S(2)}, u32[]{:S(2)}) collective-permute-start(bf16[3,2,16,1024]{3,2,1,0:T(8,128)(2,1)S(1)} %shard_map.93.late_ref), channel_id=1, source_target_pairs={{0,1},{1,2},{2,3},{3,4},{4,5},{5,6},{6,7},{7,8},{8,9},{9,10},{10,1... | collective-permute-start | bytes 589832 | tf_op jit(solution)/shard_map/ppermute | solution.py:376
  47.4 1.0 collective-permute-done.9.past_ref
  48.4 0.0 collective-permute-done.4.got_ref
  48.4 0.0 copy-done
  48.4 0.0 copy-done.1
  48.4 0.0 copy-done.3
  48.4 2.3 %shard_map.94 = bf16[16,128,128]{2,1,0:T(8,128)(2,1)S(1)} custom-call(bf16[1,5,2,16,1024]{4,3,2,1,0:T(8,128)(2,1)S(1)} %get-tuple-element.24.own_ref, bf16[1,5,2,16,1024]{4,3,2,1,0:T(8,128)(2,1)S(1)} %collective-permute-done.4.got_ref, bf16[3,2,16,1024]{3,2,1,0:T(8,128)(2,1)S(1)} %shard_map.93.late_ref, ...), custom_call_target="tpu_custom_call" | custom-call | flops 1073741824 | bytes 6291456 | tf_op jit(solution)/shard_map/pallas_call | solution.py:196
  50.8 21.8 %all_to_all.5.in_ref = bf16[16,128,128]{2,1,0:T(8,128)(2,1)S(1)} all-to-all(bf16[16,128,128]{2,1,0:T(8,128)(2,1)S(1)} %shard_map.94), channel_id=1, replica_groups=mesh['x'=4,'yh'=2,'yl'=2,'z'=4,'core'=2] {'yl','z','core'}, dimensions={0} | all-to-all | bytes 1048576 | tf_op jit(solution)/shard_map/all_to_all | solution.py:378
  72.5 0.7 shard_map.95
  73.2 3.0 %collective-permute-start.10 = (bf16[40,2,16,128]{3,2,1,0:T(8,128)(2,1)S(1)}, bf16[40,2,16,128]{3,2,1,0:T(8,128)(2,1)S(1)}, u32[]{:S(2)}, u32[]{:S(2)}) collective-permute-start(bf16[40,2,16,128]{3,2,1,0:T(8,128)(2,1)S(1)} %get-tuple-element.32.refs_0_), channel_id=1, source_target_pairs={{0,16},{16,0},{1,17},{17,1},{2,18},{18,2},{3,19},{19,3},{4,20},{20... | collective-permute-start | bytes 983048 | tf_op jit(solution)/shard_map/ppermute | solution.py:38
  76.2 0.6 collective-permute-start.17
  76.7 1.2 %collective-permute-start.16 = (bf16[24,2,16,128]{3,2,1,0:T(8,128)(2,1)S(1)}, bf16[24,2,16,128]{3,2,1,0:T(8,128)(2,1)S(1)}, u32[]{:S(2)}, u32[]{:S(2)}) collective-permute-start(bf16[24,2,16,128]{3,2,1,0:T(8,128)(2,1)S(1)} %get-tuple-element.33.refs_0_), channel_id=1, source_target_pairs={{0,64},{32,96},{64,0},{96,32},{1,65},{33,97},{65,1},{97,33},{2,66}... | collective-permute-start | bytes 589832 | tf_op jit(solution)/shard_map/ppermute | solution.py:34
  77.9 0.8 collective-permute-start.15
  78.8 4.9 %collective-permute-done.10.refs_1_ = bf16[40,2,16,128]{3,2,1,0:T(8,128)(2,1)S(1)} collective-permute-done((bf16[40,2,16,128]{3,2,1,0:T(8,128)(2,1)S(1)}, bf16[40,2,16,128]{3,2,1,0:T(8,128)(2,1)S(1)}, u32[]{:S(2)}, u32[]{:S(2)}) %collective-permute-start.10) | collective-permute-done | bytes 327712 | tf_op jit(solution)/shard_map/ppermute | solution.py:38
  83.8 0.6 collective-permute-start.12
  84.4 1.5 %collective-permute-start.11 = (bf16[2,40,2,16,128]{4,3,2,1,0:T(8,128)(2,1)S(1)}, bf16[2,40,2,16,128]{4,3,2,1,0:T(8,128)(2,1)S(1)}, u32[]{:S(2)}, u32[]{:S(2)}) collective-permute-start(bf16[2,40,2,16,128]{4,3,2,1,0:T(8,128)(2,1)S(1)} %shard_map.96.refs_0_), channel_id=1, source_target_pairs={{0,96},{32,0},{64,32},{96,64},{1,97},{33,1},{65,33},{97,65},{2,98}... | collective-permute-start | bytes 1966088 | tf_op jit(solution)/shard_map/ppermute | solution.py:34
  85.9 0.0 collective-permute-done.17.refs_3_
  85.9 0.1 collective-permute-done.16.refs_2_
  86.0 2.7 %collective-permute-done.15.refs_1_ = bf16[24,2,16,128]{3,2,1,0:T(8,128)(2,1)S(1)} collective-permute-done((bf16[24,2,16,128]{3,2,1,0:T(8,128)(2,1)S(1)}, bf16[24,2,16,128]{3,2,1,0:T(8,128)(2,1)S(1)}, u32[]{:S(2)}, u32[]{:S(2)}) %collective-permute-start.15) | collective-permute-done | bytes 196640 | tf_op jit(solution)/shard_map/ppermute | solution.py:34
  88.7 0.1 shard_map.97.refs_0_
  88.7 0.2 collective-permute-start.18
  88.9 11.4 %collective-permute-done.12.refs_4_ = bf16[2,40,2,16,128]{4,3,2,1,0:T(8,128)(2,1)S(1)} collective-permute-done((bf16[2,40,2,16,128]{4,3,2,1,0:T(8,128)(2,1)S(1)}, bf16[2,40,2,16,128]{4,3,2,1,0:T(8,128)(2,1)S(1)}, u32[]{:S(2)}, u32[]{:S(2)}) %collective-permute-start.12) | collective-permute-done | bytes 655392 | tf_op jit(solution)/shard_map/ppermute | solution.py:34
  100.3 2.7 %collective-permute-start.13 = (bf16[1,40,2,16,128]{4,3,2,1,0:T(8,128)(2,1)S(1)}, bf16[1,40,2,16,128]{4,3,2,1,0:T(8,128)(2,1)S(1)}, u32[]{:S(2)}, u32[]{:S(2)}) collective-permute-start(bf16[1,40,2,16,128]{4,3,2,1,0:T(8,128)(2,1)S(1)} %slice.8), channel_id=1, source_target_pairs={{0,32},{32,64},{64,96},{96,0},{1,33},{33,65},{65,97},{97,1},{2,34}... | collective-permute-start | bytes 983048 | tf_op jit(solution)/shard_map/ppermute | solution.py:34
  103.0 0.0 collective-permute-done.11.refs_1_
  103.1 0.1 collective-permute-start.14
  103.2 5.4 %collective-permute-done.18.refs_1_ = bf16[4,24,2,16,128]{4,3,2,1,0:T(8,128)(2,1)S(1)} collective-permute-done((bf16[4,24,2,16,128]{4,3,2,1,0:T(8,128)(2,1)S(1)}, bf16[4,24,2,16,128]{4,3,2,1,0:T(8,128)(2,1)S(1)}, u32[]{:S(2)}, u32[]{:S(2)}) %collective-permute-start.18) | collective-permute-done | bytes 786464 | tf_op jit(solution)/shard_map/ppermute | solution.py:38
  108.6 3.7 %shard_map.98 = (f32[2,64,16,128]{3,2,1,0:T(8,128)}, bf16[2,64,128,128]{3,2,1,0:T(8,128)(2,1)}) custom-call(s32[8]{0:T(128)S(1)} %fusion.7.places_ref, bf16[24,128,256]{2,1,0:T(8,128)(2,1)S(1)} %shard_map.88.refs_4_.weight_ref, bf16[4,24,2,16,128]{4,3,2,1,0:T(8,128)(2,1)S(1)} %shard_map.97.refs_0_, ...), custom_call_target="tpu_custom_call" | custom-call | flops 503316480 | bytes 9830400 | tf_op jit(solution)/shard_map/pallas_call | solution.py:292
  112.3 0.0 collective-permute-done.13.refs_2_
  112.3 0.6 collective-permute-done.14.refs_3_
  112.9 5.4 %shard_map.99 = (f32[2,64,16,128]{3,2,1,0:T(8,128)}, bf16[2,64,128,128]{3,2,1,0:T(8,128)(2,1)}) custom-call(s32[8]{0:T(128)S(1)} %fusion.7.places_ref, bf16[40,128,256]{2,1,0:T(8,128)(2,1)S(1)} %shard_map.86.refs_3_.weight_ref, bf16[2,40,2,16,128]{4,3,2,1,0:T(8,128)(2,1)S(1)} %shard_map.96.refs_0_, ...), custom_call_target="tpu_custom_call", output_to_operand_aliasing={{0}: (7, {}), {1}: (8, {})} | custom-call | flops 838860800 | bytes 16384000 | tf_op jit(solution)/shard_map/pallas_call | solution.py:292
  (5 shorter events, 0.1 us)
Async XLA Ops:
  6.0 16.8 %collective-permute-start = (bf16[2,5,2,16,1024]{4,3,2,1,0:T(8,128)(2,1)}, bf16[2,5,2,16,1024]{4,3,2,1,0:T(8,128)(2,1)S(1)}, u32[]{:S(2)}, u32[]{:S(2)}) collective-permute-start(bf16[2,5,2,16,1024]{4,3,2,1,0:T(8,128)(2,1)} %get-tuple-element.20), channel_id=1, source_target_pairs={{0,32},{32,64},{64,96},{96,0},{1,33},{33,65},{65,97},{97,1},{2,34}... | collective-permute-start | bytes 1966088 | tf_op jit(solution)/shard_map/ppermute | solution.py:34
  6.4 17.6 %collective-permute-start.1 = (bf16[2,5,2,16,1024]{4,3,2,1,0:T(8,128)(2,1)}, bf16[2,5,2,16,1024]{4,3,2,1,0:T(8,128)(2,1)S(1)}, u32[]{:S(2)}, u32[]{:S(2)}) collective-permute-start(bf16[2,5,2,16,1024]{4,3,2,1,0:T(8,128)(2,1)} %get-tuple-element.21), channel_id=1, source_target_pairs={{0,96},{32,0},{64,32},{96,64},{1,97},{33,1},{65,33},{97,65},{2,98}... | collective-permute-start | bytes 1966088 | tf_op jit(solution)/shard_map/ppermute | solution.py:34
  8.1 6.7 %copy-start.2 = (f32[128,128]{1,0:T(8,128)S(1)}, f32[128,128]{1,0:T(8,128)}, u32[]{:S(2)}) copy-start(f32[128,128]{1,0:T(8,128)} %delays_ref.3) | copy-start | bytes 196612
  11.5 20.6 %collective-permute-start.5 = (bf16[4,3,2,16,1024]{4,3,2,1,0:T(8,128)(2,1)}, bf16[4,3,2,16,1024]{4,3,2,1,0:T(8,128)(2,1)}, u32[]{:S(2)}, u32[]{:S(2)}) collective-permute-start(bf16[4,3,2,16,1024]{4,3,2,1,0:T(8,128)(2,1)} %get-tuple-element.27), channel_id=1, source_target_pairs={{0,16},{16,0},{1,17},{17,1},{2,18},{18,2},{3,19},{19,3},{4,20},{20... | collective-permute-start | bytes 2359304 | tf_op jit(solution)/shard_map/ppermute | solution.py:38
  24.2 12.4 %collective-permute-start.2 = (bf16[1,5,2,16,1024]{4,3,2,1,0:T(8,128)(2,1)S(1)}, bf16[1,5,2,16,1024]{4,3,2,1,0:T(8,128)(2,1)S(1)}, u32[]{:S(2)}, u32[]{:S(2)}) collective-permute-start(bf16[1,5,2,16,1024]{4,3,2,1,0:T(8,128)(2,1)S(1)} %get-tuple-element.22), channel_id=1, source_target_pairs={{0,32},{32,64},{64,96},{96,0},{1,33},{33,65},{65,97},{97,1},{2,34}... | collective-permute-start | bytes 983048 | tf_op jit(solution)/shard_map/ppermute | solution.py:34
  24.6 11.9 %collective-permute-start.3 = (bf16[1,5,2,16,1024]{4,3,2,1,0:T(8,128)(2,1)S(1)}, bf16[1,5,2,16,1024]{4,3,2,1,0:T(8,128)(2,1)S(1)}, u32[]{:S(2)}, u32[]{:S(2)}) collective-permute-start(bf16[1,5,2,16,1024]{4,3,2,1,0:T(8,128)(2,1)S(1)} %get-tuple-element.23), channel_id=1, source_target_pairs={{0,96},{32,0},{64,32},{96,64},{1,97},{33,1},{65,33},{97,65},{2,98}... | collective-permute-start | bytes 983048 | tf_op jit(solution)/shard_map/ppermute | solution.py:34
  32.1 16.3 %copy-start = (bf16[1024,1024]{1,0:T(8,128)(2,1)S(1)}, bf16[1024,1024]{1,0:T(8,128)(2,1)}, u32[]{:S(2)}) copy-start(bf16[1024,1024]{1,0:T(8,128)(2,1)} %constant.116.clone.sin_ref) | copy-start | bytes 6291460
  32.1 16.3 %copy-start.1 = (bf16[1024,1024]{1,0:T(8,128)(2,1)S(1)}, bf16[1024,1024]{1,0:T(8,128)(2,1)}, u32[]{:S(2)}) copy-start(bf16[1024,1024]{1,0:T(8,128)(2,1)} %constant.115.clone.cos_ref) | copy-start | bytes 6291460
  32.1 16.3 %copy-start.3 = (f32[4,1024]{1,0:T(4,128)S(1)}, f32[4,1024]{1,0:T(4,128)}, u32[]{:S(2)}) copy-start(f32[4,1024]{1,0:T(4,128)} %taps_ref.1) | copy-start | bytes 49156
  33.6 7.3 %collective-permute-start.6 = (bf16[3,2,16,1024]{3,2,1,0:T(8,128)(2,1)S(1)}, bf16[3,2,16,1024]{3,2,1,0:T(8,128)(2,1)S(1)}, u32[]{:S(2)}, u32[]{:S(2)}) collective-permute-start(bf16[3,2,16,1024]{3,2,1,0:T(8,128)(2,1)S(1)} %get-tuple-element.29), channel_id=1, source_target_pairs={{0,32},{32,64},{64,96},{96,0},{1,33},{33,65},{65,97},{97,1},{2,34}... | collective-permute-start | bytes 589832 | tf_op jit(solution)/shard_map/ppermute | solution.py:34
  35.3 8.6 %collective-permute-start.7 = (bf16[3,2,16,1024]{3,2,1,0:T(8,128)(2,1)S(1)}, bf16[3,2,16,1024]{3,2,1,0:T(8,128)(2,1)S(1)}, u32[]{:S(2)}, u32[]{:S(2)}) collective-permute-start(bf16[3,2,16,1024]{3,2,1,0:T(8,128)(2,1)S(1)} %get-tuple-element.30), channel_id=1, source_target_pairs={{0,64},{32,96},{64,0},{96,32},{1,65},{33,97},{65,1},{97,33},{2,66}... | collective-permute-start | bytes 589832 | tf_op jit(solution)/shard_map/ppermute | solution.py:34
  36.6 9.4 %collective-permute-start.8 = (bf16[3,2,16,1024]{3,2,1,0:T(8,128)(2,1)S(1)}, bf16[3,2,16,1024]{3,2,1,0:T(8,128)(2,1)S(1)}, u32[]{:S(2)}, u32[]{:S(2)}) collective-permute-start(bf16[3,2,16,1024]{3,2,1,0:T(8,128)(2,1)S(1)} %get-tuple-element.31), channel_id=1, source_target_pairs={{0,96},{32,0},{64,32},{96,64},{1,97},{33,1},{65,33},{97,65},{2,98}... | collective-permute-start | bytes 589832 | tf_op jit(solution)/shard_map/ppermute | solution.py:34
  36.8 11.6 %collective-permute-start.4 = (bf16[1,5,2,16,1024]{4,3,2,1,0:T(8,128)(2,1)S(1)}, bf16[1,5,2,16,1024]{4,3,2,1,0:T(8,128)(2,1)S(1)}, u32[]{:S(2)}, u32[]{:S(2)}) collective-permute-start(bf16[1,5,2,16,1024]{4,3,2,1,0:T(8,128)(2,1)S(1)} %get-tuple-element.25), channel_id=1, source_target_pairs={{0,16},{16,0},{1,17},{17,1},{2,18},{18,2},{3,19},{19,3},{4,20},{20... | collective-permute-start | bytes 983048 | tf_op jit(solution)/shard_map/ppermute | solution.py:38
  46.0 2.4 %collective-permute-start.9 = (bf16[3,2,16,1024]{3,2,1,0:T(8,128)(2,1)S(1)}, bf16[3,2,16,1024]{3,2,1,0:T(8,128)(2,1)S(1)}, u32[]{:S(2)}, u32[]{:S(2)}) collective-permute-start(bf16[3,2,16,1024]{3,2,1,0:T(8,128)(2,1)S(1)} %shard_map.93.late_ref), channel_id=1, source_target_pairs={{0,1},{1,2},{2,3},{3,4},{4,5},{5,6},{6,7},{7,8},{8,9},{9,10},{10,1... | collective-permute-start | bytes 589832 | tf_op jit(solution)/shard_map/ppermute | solution.py:376
  73.2 10.5 %collective-permute-start.10 = (bf16[40,2,16,128]{3,2,1,0:T(8,128)(2,1)S(1)}, bf16[40,2,16,128]{3,2,1,0:T(8,128)(2,1)S(1)}, u32[]{:S(2)}, u32[]{:S(2)}) collective-permute-start(bf16[40,2,16,128]{3,2,1,0:T(8,128)(2,1)S(1)} %get-tuple-element.32.refs_0_), channel_id=1, source_target_pairs={{0,16},{16,0},{1,17},{17,1},{2,18},{18,2},{3,19},{19,3},{4,20},{20... | collective-permute-start | bytes 983048 | tf_op jit(solution)/shard_map/ppermute | solution.py:38
  76.2 9.7 %collective-permute-start.17 = (bf16[24,2,16,128]{3,2,1,0:T(8,128)(2,1)S(1)}, bf16[24,2,16,128]{3,2,1,0:T(8,128)(2,1)S(1)}, u32[]{:S(2)}, u32[]{:S(2)}) collective-permute-start(bf16[24,2,16,128]{3,2,1,0:T(8,128)(2,1)S(1)} %get-tuple-element.33.refs_0_), channel_id=1, source_target_pairs={{0,32},{32,64},{64,96},{96,0},{1,33},{33,65},{65,97},{97,1},{2,34}... | collective-permute-start | bytes 589832 | tf_op jit(solution)/shard_map/ppermute | solution.py:34
  76.7 9.3 %collective-permute-start.16 = (bf16[24,2,16,128]{3,2,1,0:T(8,128)(2,1)S(1)}, bf16[24,2,16,128]{3,2,1,0:T(8,128)(2,1)S(1)}, u32[]{:S(2)}, u32[]{:S(2)}) collective-permute-start(bf16[24,2,16,128]{3,2,1,0:T(8,128)(2,1)S(1)} %get-tuple-element.33.refs_0_), channel_id=1, source_target_pairs={{0,64},{32,96},{64,0},{96,32},{1,65},{33,97},{65,1},{97,33},{2,66}... | collective-permute-start | bytes 589832 | tf_op jit(solution)/shard_map/ppermute | solution.py:34
  77.9 10.7 %collective-permute-start.15 = (bf16[24,2,16,128]{3,2,1,0:T(8,128)(2,1)S(1)}, bf16[24,2,16,128]{3,2,1,0:T(8,128)(2,1)S(1)}, u32[]{:S(2)}, u32[]{:S(2)}) collective-permute-start(bf16[24,2,16,128]{3,2,1,0:T(8,128)(2,1)S(1)} %get-tuple-element.33.refs_0_), channel_id=1, source_target_pairs={{0,96},{32,0},{64,32},{96,64},{1,97},{33,1},{65,33},{97,65},{2,98}... | collective-permute-start | bytes 589832 | tf_op jit(solution)/shard_map/ppermute | solution.py:34
  83.8 16.5 %collective-permute-start.12 = (bf16[2,40,2,16,128]{4,3,2,1,0:T(8,128)(2,1)S(1)}, bf16[2,40,2,16,128]{4,3,2,1,0:T(8,128)(2,1)S(1)}, u32[]{:S(2)}, u32[]{:S(2)}) collective-permute-start(bf16[2,40,2,16,128]{4,3,2,1,0:T(8,128)(2,1)S(1)} %shard_map.96.refs_0_), channel_id=1, source_target_pairs={{0,32},{32,64},{64,96},{96,0},{1,33},{33,65},{65,97},{97,1},{2,34}... | collective-permute-start | bytes 1966088 | tf_op jit(solution)/shard_map/ppermute | solution.py:34
  84.4 18.6 %collective-permute-start.11 = (bf16[2,40,2,16,128]{4,3,2,1,0:T(8,128)(2,1)S(1)}, bf16[2,40,2,16,128]{4,3,2,1,0:T(8,128)(2,1)S(1)}, u32[]{:S(2)}, u32[]{:S(2)}) collective-permute-start(bf16[2,40,2,16,128]{4,3,2,1,0:T(8,128)(2,1)S(1)} %shard_map.96.refs_0_), channel_id=1, source_target_pairs={{0,96},{32,0},{64,32},{96,64},{1,97},{33,1},{65,33},{97,65},{2,98}... | collective-permute-start | bytes 1966088 | tf_op jit(solution)/shard_map/ppermute | solution.py:34
  88.7 19.9 %collective-permute-start.18 = (bf16[4,24,2,16,128]{4,3,2,1,0:T(8,128)(2,1)S(1)}, bf16[4,24,2,16,128]{4,3,2,1,0:T(8,128)(2,1)S(1)}, u32[]{:S(2)}, u32[]{:S(2)}) collective-permute-start(bf16[4,24,2,16,128]{4,3,2,1,0:T(8,128)(2,1)S(1)} %shard_map.97.refs_0_), channel_id=1, source_target_pairs={{0,16},{16,0},{1,17},{17,1},{2,18},{18,2},{3,19},{19,3},{4,20},{20... | collective-permute-start | bytes 2359304 | tf_op jit(solution)/shard_map/ppermute | solution.py:38
  100.3 12.0 %collective-permute-start.13 = (bf16[1,40,2,16,128]{4,3,2,1,0:T(8,128)(2,1)S(1)}, bf16[1,40,2,16,128]{4,3,2,1,0:T(8,128)(2,1)S(1)}, u32[]{:S(2)}, u32[]{:S(2)}) collective-permute-start(bf16[1,40,2,16,128]{4,3,2,1,0:T(8,128)(2,1)S(1)} %slice.8), channel_id=1, source_target_pairs={{0,32},{32,64},{64,96},{96,0},{1,33},{33,65},{65,97},{97,1},{2,34}... | collective-permute-start | bytes 983048 | tf_op jit(solution)/shard_map/ppermute | solution.py:34
  103.1 9.8 %collective-permute-start.14 = (bf16[1,40,2,16,128]{4,3,2,1,0:T(8,128)(2,1)S(1)}, bf16[1,40,2,16,128]{4,3,2,1,0:T(8,128)(2,1)S(1)}, u32[]{:S(2)}, u32[]{:S(2)}) collective-permute-start(bf16[1,40,2,16,128]{4,3,2,1,0:T(8,128)(2,1)S(1)} %slice.9), channel_id=1, source_target_pairs={{0,96},{32,0},{64,32},{96,64},{1,97},{33,1},{65,33},{97,65},{2,98}... | collective-permute-start | bytes 983048 | tf_op jit(solution)/shard_map/ppermute | solution.py:34

commit v3 on v2

--- a/solution.py
+++ b/solution.py
@@ -25,7 +25,7 @@
 EARLY = LOCAL_FRAMES - LATE
 LOCAL_CHANS = 64
 FIRST = 40
-STEP = 4
+STEP = 8
 BF16 = jnp.bfloat16
 F32 = jnp.float32
 
@@ -312,13 +312,13 @@
     )(places, weights, *arrays, *results)
 
 
-def reduce_sections(member, voltages, others):
+def reduce_sections(member, voltages):
     x_plus, x_minus, x_rest = tile_sums(member, voltages, 0, EARLY, ((4, 3), (5, 6), (0, 1, 2, 7)))
     keep, give = tile_sums(member, voltages, EARLY, LATE, ((0, 2, 4, 6), (1, 3, 5, 7)), (x_rest,))
     got = pair(give)
     from_minus, from_plus = ring(x_plus, 1), ring(x_minus, -1)
     x_next, x_prev = combine(
-        (x_rest, from_minus, from_plus), ([[(0, 2), (1, 0)]], [[(0, 3), (2, 0)]]), others
+        (x_rest, from_minus, from_plus), ([[(0, 2), (1, 0)]], [[(0, 3), (2, 0)]])
     )
     last_minus, last_plus = ring(x_next, 1), ring(x_prev, -1)
     early_own, early_give = combine(
@@ -337,10 +337,11 @@
     return early, late
 
 
-def gather_sections(first, second):
+def gather_sections(first, second, others):
     (both,) = combine((first, pair(first)), ([[(0, slice(None))], [(1, slice(None))]],))
     both_minus, both_plus = ring(both, 1), ring(both, -1)
-    own_far, pair_far = ring(both_minus[:1], 1), ring(both_plus[1:], -1)
+    own_far, pair_far = combine((both_minus, both_plus), ([[(0, 0)]], [[(1, 1)]]), others)
+    own_far, pair_far = ring(own_far, 1), ring(pair_far, -1)
     firsts = ((both, 0), (both, 1), (both_plus, 0), (both_plus, 1))
     firsts += ((own_far, 0), (pair_far, 0), (both_minus, 0), (both_minus, 1))
 
@@ -372,14 +373,14 @@
     counts = (FIRST, LOCAL_CHANS - FIRST)
     weights = [beam_weights(base + b, delays, n) for b, n in zip((0, FIRST), counts)]
 
-    early, late = reduce_sections(member, voltages, weights)
+    early, late = reduce_sections(member, voltages)
     past = lax.ppermute(late, DEV, [(i, i + 1) for i in range(FRAMES // LOCAL_FRAMES - 1)])
     spec = spectra(early, late, past, filter_taps, cos_table, sin_table)
     first, second = turn(lax.all_to_all(spec, DEV, 0, 0, tiled=True))
     rel = jnp.arange(8, dtype=jnp.int32)
     places = ((x + rel // 2) % NX) * 2 + (rel % 2 ^ y)
     places = places.astype(jnp.int32)
-    firsts, seconds = gather_sections(first, second)
+    firsts, seconds = gather_sections(first, second, weights)
     results = products(places, weights[1], FIRST, seconds)
     return tuple(products(places, weights[0], 0, firsts, results))
 

time: 118 us -> 114 us (0.966)
  Pallas kernels: 27.8 us -> 23.2 us
  local copies, waits for them, and re-layouts: 0.06 us -> 1.68 us
    ppermute x4, waiting for transfers between devices: 16.2 us -> 14.1 us  [pair(): return lax.ppermute(v, 'yh', [(0, 1), (1, 0)])]
    pallas_call x2, Pallas kernels: 8.01 us -> 6.03 us  [tile_sums(): pl.pallas_call(functools.partial(tile_sums_kernel, first, frames, groups)...]
    unnamed x8 -> x10, local copies, waits for them, and re-layouts: 0.01 us -> 1.68 us
    pallas_call x2, Pallas kernels: 9.07 us -> 7.72 us  [products(): pl.pallas_call(kernel, in_specs=[IN_SMEM] + [IN_VMEM] * (1 + len(arrays))...]
    pallas_call x6 -> x7, Pallas kernels: 2.05 us -> 0.81 us  [combine(): pl.pallas_call(functools.partial(combine_kernel, layout), in_specs=[IN_VM...]
    ppermute x14, waiting for transfers between devices: 24.1 us -> 25.4 us  [ring(): return lax.ppermute(v, 'x', [(i, (i + by) % NX) for i in range(NX)])]
  transfers between devices with their start and end apart: 19 -> 19, of which waited for: 13 -> 14; matrix products, arithmetic and copies ran while one was open for 0% -> 0% of each run, Pallas kernels for 13% -> 11%
where the time goes in v3:
time: 114 us
  waiting for transfers between devices  40.5 us (36%)
  starting transfers between devices  25 us (22%)
  Pallas kernels  23.2 us (20%)
  blocking collectives  21.8 us (19%)
  local copies, waits for them, and re-layouts  1.68 us (1%)
    ppermute x14, waiting for transfers between devices, ring(): return lax.ppermute(v, 'x', [(i, (i + by) % NX) for i in range(NX)])  25.4 us
    all_to_all x1, blocking collectives, local(): first, second = turn(lax.all_to_all(spec, DEV, 0, 0, tiled=True))  21.8 us
    ppermute x4, waiting for transfers between devices, pair(): return lax.ppermute(v, 'yh', [(0, 1), (1, 0)])  14.1 us
    ppermute x14, starting transfers between devices, ring(): return lax.ppermute(v, 'x', [(i, (i + by) % NX) for i in range(NX)])  14 us
    ppermute x4, starting transfers between devices, pair(): return lax.ppermute(v, 'yh', [(0, 1), (1, 0)])  9.72 us
    pallas_call x2, Pallas kernels, products(): pl.pallas_call(kernel, in_specs=[IN_SMEM] + [IN_VMEM] * (1 + len(arrays))...  7.72 us
    pallas_call x2, Pallas kernels, tile_sums(): pl.pallas_call(functools.partial(tile_sums_kernel, first, frames, groups)...  6.03 us
    pallas_call x2, Pallas kernels, beam_weights(): pl.pallas_call(weights_kernel, in_specs=[IN_SMEM, IN_VMEM], out_specs=IN_...  5.68 us
  transfers between devices with their start and end apart: 19, of which 14 were waited for; matrix products, arithmetic and copies ran while one was open for 0% of the time, Pallas kernels for 11%

profile of v3, /device:TPU:6, one launch (start us, length us, event | category | flops | bytes accessed | tf_op | source)
XLA Modules:
  0.0 113.8 jit_solution(9021382660244490375)
XLA Ops:
  0.6 0.7 compare_select_fusion.4
  1.4 3.5 %shard_map.87 = (bf16[2,5,2,16,1024]{4,3,2,1,0:T(8,128)(2,1)S(1)}, bf16[2,5,2,16,1024]{4,3,2,1,0:T(8,128)(2,1)S(1)}, bf16[4,5,2,16,1024]{4,3,2,1,0:T(8,128)(2,1)S(1)}) custom-call(bf16[128,256]{1,0:T(8,128)(2,1)S(1)} %fusion.member_ref, bf16[2,256,8192]{2,1,0:T(8,128)(2,1)} %volts_ref.3), custom_call_target="tpu_custom_call" | custom-call | flops 671088640 | bytes 15728640 | tf_op jit(solution)/shard_map/pallas_call | solution.py:103
  4.9 0.5 collective-permute-start
  5.4 1.6 %collective-permute-start.1 = (bf16[2,5,2,16,1024]{4,3,2,1,0:T(8,128)(2,1)S(1)}, bf16[2,5,2,16,1024]{4,3,2,1,0:T(8,128)(2,1)S(1)}, u32[]{:S(2)}, u32[]{:S(2)}) collective-permute-start(bf16[2,5,2,16,1024]{4,3,2,1,0:T(8,128)(2,1)S(1)} %get-tuple-element.23), channel_id=1, source_target_pairs={{0,96},{32,0},{64,32},{96,64},{1,97},{33,1},{65,33},{97,65},{2,98}... | collective-permute-start | bytes 1966088 | tf_op jit(solution)/shard_map/ppermute | solution.py:34
  7.0 2.5 %shard_map.90 = (bf16[4,3,2,16,1024]{4,3,2,1,0:T(8,128)(2,1)S(1)}, bf16[4,3,2,16,1024]{4,3,2,1,0:T(8,128)(2,1)S(1)}) custom-call(bf16[128,256]{1,0:T(8,128)(2,1)S(1)} %fusion.member_ref, bf16[2,256,8192]{2,1,0:T(8,128)(2,1)} %volts_ref.3, bf16[4,5,2,16,1024]{4,3,2,1,0:T(8,128)(2,1)S(1)} %get-tuple-element.21.refs_0_), custom_call_target="tpu_custom_call" | custom-call | flops 402653184 | bytes 9437184 | tf_op jit(solution)/shard_map/pallas_call | solution.py:103
  9.5 3.3 %collective-permute-start.5 = (bf16[4,3,2,16,1024]{4,3,2,1,0:T(8,128)(2,1)S(1)}, bf16[4,3,2,16,1024]{4,3,2,1,0:T(8,128)(2,1)S(1)}, u32[]{:S(2)}, u32[]{:S(2)}) collective-permute-start(bf16[4,3,2,16,1024]{4,3,2,1,0:T(8,128)(2,1)S(1)} %get-tuple-element.29), channel_id=1, source_target_pairs={{0,16},{16,0},{1,17},{17,1},{2,18},{18,2},{3,19},{19,3},{4,20},{20... | collective-permute-start | bytes 2359304 | tf_op jit(solution)/shard_map/ppermute | solution.py:38
  12.8 8.6 %collective-permute-done.refs_1_.refs_3_ = bf16[2,5,2,16,1024]{4,3,2,1,0:T(8,128)(2,1)S(1)} collective-permute-done((bf16[2,5,2,16,1024]{4,3,2,1,0:T(8,128)(2,1)S(1)}, bf16[2,5,2,16,1024]{4,3,2,1,0:T(8,128)(2,1)S(1)}, u32[]{:S(2)}, u32[]{:S(2)}) %collective-permute-start) | collective-permute-done | bytes 655392 | tf_op jit(solution)/shard_map/ppermute | solution.py:34
  21.4 1.3 %collective-permute-done.1.refs_2_.refs_4_ = bf16[2,5,2,16,1024]{4,3,2,1,0:T(8,128)(2,1)S(1)} collective-permute-done((bf16[2,5,2,16,1024]{4,3,2,1,0:T(8,128)(2,1)S(1)}, bf16[2,5,2,16,1024]{4,3,2,1,0:T(8,128)(2,1)S(1)}, u32[]{:S(2)}, u32[]{:S(2)}) %collective-permute-start.1) | collective-permute-done | bytes 655392 | tf_op jit(solution)/shard_map/ppermute | solution.py:34
  22.7 0.2 shard_map.88
  22.9 0.5 collective-permute-start.2
  23.4 1.6 %collective-permute-start.3 = (bf16[1,5,2,16,1024]{4,3,2,1,0:T(8,128)(2,1)S(1)}, bf16[1,5,2,16,1024]{4,3,2,1,0:T(8,128)(2,1)S(1)}, u32[]{:S(2)}, u32[]{:S(2)}) collective-permute-start(bf16[1,5,2,16,1024]{4,3,2,1,0:T(8,128)(2,1)S(1)} %get-tuple-element.25), channel_id=1, source_target_pairs={{0,96},{32,0},{64,32},{96,64},{1,97},{33,1},{65,33},{97,65},{2,98}... | collective-permute-start | bytes 983048 | tf_op jit(solution)/shard_map/ppermute | solution.py:34
  25.0 4.8 %collective-permute-done.5.refs_1_ = bf16[4,3,2,16,1024]{4,3,2,1,0:T(8,128)(2,1)S(1)} collective-permute-done((bf16[4,3,2,16,1024]{4,3,2,1,0:T(8,128)(2,1)S(1)}, bf16[4,3,2,16,1024]{4,3,2,1,0:T(8,128)(2,1)S(1)}, u32[]{:S(2)}, u32[]{:S(2)}) %collective-permute-start.5) | collective-permute-done | bytes 786464 | tf_op jit(solution)/shard_map/ppermute | solution.py:38
  29.8 0.0 copy-start
  29.8 0.0 copy-start.1
  29.8 0.0 copy-start.4
  29.8 0.2 shard_map.91
  30.0 1.7 %collective-permute-start.6 = (bf16[3,2,16,1024]{3,2,1,0:T(8,128)(2,1)S(1)}, bf16[3,2,16,1024]{3,2,1,0:T(8,128)(2,1)S(1)}, u32[]{:S(2)}, u32[]{:S(2)}) collective-permute-start(bf16[3,2,16,1024]{3,2,1,0:T(8,128)(2,1)S(1)} %get-tuple-element.31), channel_id=1, source_target_pairs={{0,32},{32,64},{64,96},{96,0},{1,33},{33,65},{65,97},{97,1},{2,34}... | collective-permute-start | bytes 589832 | tf_op jit(solution)/shard_map/ppermute | solution.py:34
  31.7 1.3 %collective-permute-start.7 = (bf16[3,2,16,1024]{3,2,1,0:T(8,128)(2,1)S(1)}, bf16[3,2,16,1024]{3,2,1,0:T(8,128)(2,1)S(1)}, u32[]{:S(2)}, u32[]{:S(2)}) collective-permute-start(bf16[3,2,16,1024]{3,2,1,0:T(8,128)(2,1)S(1)} %get-tuple-element.32), channel_id=1, source_target_pairs={{0,64},{32,96},{64,0},{96,32},{1,65},{33,97},{65,1},{97,33},{2,66}... | collective-permute-start | bytes 589832 | tf_op jit(solution)/shard_map/ppermute | solution.py:34
  33.0 0.0 collective-permute-start.8
  33.0 0.0 collective-permute-done.2.refs_1_
  33.0 0.0 collective-permute-done.3.refs_2_
  33.0 0.2 shard_map.89
  33.2 3.3 %collective-permute-start.4 = (bf16[1,5,2,16,1024]{4,3,2,1,0:T(8,128)(2,1)S(1)}, bf16[1,5,2,16,1024]{4,3,2,1,0:T(8,128)(2,1)S(1)}, u32[]{:S(2)}, u32[]{:S(2)}) collective-permute-start(bf16[1,5,2,16,1024]{4,3,2,1,0:T(8,128)(2,1)S(1)} %get-tuple-element.27), channel_id=1, source_target_pairs={{0,16},{16,0},{1,17},{17,1},{2,18},{18,2},{3,19},{19,3},{4,20},{20... | collective-permute-start | bytes 983048 | tf_op jit(solution)/shard_map/ppermute | solution.py:38
  36.5 1.0 collective-permute-done.6.refs_1_
  37.5 2.8 %collective-permute-done.7.refs_2_ = bf16[3,2,16,1024]{3,2,1,0:T(8,128)(2,1)S(1)} collective-permute-done((bf16[3,2,16,1024]{3,2,1,0:T(8,128)(2,1)S(1)}, bf16[3,2,16,1024]{3,2,1,0:T(8,128)(2,1)S(1)}, u32[]{:S(2)}, u32[]{:S(2)}) %collective-permute-start.7) | collective-permute-done | bytes 196640 | tf_op jit(solution)/shard_map/ppermute | solution.py:34
  40.3 2.0 %collective-permute-done.8.refs_3_ = bf16[3,2,16,1024]{3,2,1,0:T(8,128)(2,1)S(1)} collective-permute-done((bf16[3,2,16,1024]{3,2,1,0:T(8,128)(2,1)S(1)}, bf16[3,2,16,1024]{3,2,1,0:T(8,128)(2,1)S(1)}, u32[]{:S(2)}, u32[]{:S(2)}) %collective-permute-start.8) | collective-permute-done | bytes 196640 | tf_op jit(solution)/shard_map/ppermute | solution.py:34
  42.4 0.1 shard_map.92.late_ref
  42.5 1.3 %collective-permute-start.9 = (bf16[3,2,16,1024]{3,2,1,0:T(8,128)(2,1)S(1)}, bf16[3,2,16,1024]{3,2,1,0:T(8,128)(2,1)S(1)}, u32[]{:S(2)}, u32[]{:S(2)}) collective-permute-start(bf16[3,2,16,1024]{3,2,1,0:T(8,128)(2,1)S(1)} %shard_map.92.late_ref), channel_id=1, source_target_pairs={{0,1},{1,2},{2,3},{3,4},{4,5},{5,6},{6,7},{7,8},{8,9},{9,10},{10,1... | collective-permute-start | bytes 589832 | tf_op jit(solution)/shard_map/ppermute | solution.py:377
  43.8 1.0 collective-permute-done.9.past_ref
  44.8 0.0 collective-permute-done.4.got_ref
  44.8 0.0 copy-done
  44.8 0.0 copy-done.1
  44.8 0.0 copy-done.4
  44.8 2.3 %shard_map.93 = bf16[16,128,128]{2,1,0:T(8,128)(2,1)S(1)} custom-call(bf16[1,5,2,16,1024]{4,3,2,1,0:T(8,128)(2,1)S(1)} %get-tuple-element.26.own_ref, bf16[1,5,2,16,1024]{4,3,2,1,0:T(8,128)(2,1)S(1)} %collective-permute-done.4.got_ref, bf16[3,2,16,1024]{3,2,1,0:T(8,128)(2,1)S(1)} %shard_map.92.late_ref, ...), custom_call_target="tpu_custom_call" | custom-call | flops 1073741824 | bytes 6291456 | tf_op jit(solution)/shard_map/pallas_call | solution.py:196
  47.2 21.8 %all_to_all.5.in_ref = bf16[16,128,128]{2,1,0:T(8,128)(2,1)S(1)} all-to-all(bf16[16,128,128]{2,1,0:T(8,128)(2,1)S(1)} %shard_map.93), channel_id=1, replica_groups=mesh['x'=4,'yh'=2,'yl'=2,'z'=4,'core'=2] {'yl','z','core'}, dimensions={0} | all-to-all | bytes 1048576 | tf_op jit(solution)/shard_map/all_to_all | solution.py:379
  68.9 0.7 shard_map.94
  69.6 3.0 %collective-permute-start.10 = (bf16[40,2,16,128]{3,2,1,0:T(8,128)(2,1)S(1)}, bf16[40,2,16,128]{3,2,1,0:T(8,128)(2,1)S(1)}, u32[]{:S(2)}, u32[]{:S(2)}) collective-permute-start(bf16[40,2,16,128]{3,2,1,0:T(8,128)(2,1)S(1)} %get-tuple-element.34.refs_0_), channel_id=1, source_target_pairs={{0,16},{16,0},{1,17},{17,1},{2,18},{18,2},{3,19},{19,3},{4,20},{20... | collective-permute-start | bytes 983048 | tf_op jit(solution)/shard_map/ppermute | solution.py:38
  72.6 0.6 collective-permute-start.17
  73.2 1.2 %collective-permute-start.16 = (bf16[24,2,16,128]{3,2,1,0:T(8,128)(2,1)S(1)}, bf16[24,2,16,128]{3,2,1,0:T(8,128)(2,1)S(1)}, u32[]{:S(2)}, u32[]{:S(2)}) collective-permute-start(bf16[24,2,16,128]{3,2,1,0:T(8,128)(2,1)S(1)} %get-tuple-element.37.refs_0_), channel_id=1, source_target_pairs={{0,64},{32,96},{64,0},{96,32},{1,65},{33,97},{65,1},{97,33},{2,66}... | collective-permute-start | bytes 589832 | tf_op jit(solution)/shard_map/ppermute | solution.py:34
  74.4 0.8 collective-permute-start.15
  75.2 4.9 %collective-permute-done.10.refs_1_ = bf16[40,2,16,128]{3,2,1,0:T(8,128)(2,1)S(1)} collective-permute-done((bf16[40,2,16,128]{3,2,1,0:T(8,128)(2,1)S(1)}, bf16[40,2,16,128]{3,2,1,0:T(8,128)(2,1)S(1)}, u32[]{:S(2)}, u32[]{:S(2)}) %collective-permute-start.10) | collective-permute-done | bytes 327712 | tf_op jit(solution)/shard_map/ppermute | solution.py:38
  80.2 0.6 collective-permute-start.12
  80.8 1.5 %collective-permute-start.11 = (bf16[2,40,2,16,128]{4,3,2,1,0:T(8,128)(2,1)S(1)}, bf16[2,40,2,16,128]{4,3,2,1,0:T(8,128)(2,1)S(1)}, u32[]{:S(2)}, u32[]{:S(2)}) collective-permute-start(bf16[2,40,2,16,128]{4,3,2,1,0:T(8,128)(2,1)S(1)} %shard_map.95.refs_0_), channel_id=1, source_target_pairs={{0,96},{32,0},{64,32},{96,64},{1,97},{33,1},{65,33},{97,65},{2,98}... | collective-permute-start | bytes 1966088 | tf_op jit(solution)/shard_map/ppermute | solution.py:34
  82.3 0.0 collective-permute-done.17.refs_3_
  82.3 0.1 collective-permute-done.16.refs_2_
  82.4 2.7 %collective-permute-done.15.refs_1_ = bf16[24,2,16,128]{3,2,1,0:T(8,128)(2,1)S(1)} collective-permute-done((bf16[24,2,16,128]{3,2,1,0:T(8,128)(2,1)S(1)}, bf16[24,2,16,128]{3,2,1,0:T(8,128)(2,1)S(1)}, u32[]{:S(2)}, u32[]{:S(2)}) %collective-permute-start.15) | collective-permute-done | bytes 196640 | tf_op jit(solution)/shard_map/ppermute | solution.py:34
  85.1 0.1 shard_map.98.refs_0_
  85.2 0.2 collective-permute-start.18
  85.3 0.0 copy-start.2
  85.3 0.8 copy-done.2
  86.2 2.1 %shard_map.96.refs_3_.weight_ref = bf16[24,128,256]{2,1,0:T(8,128)(2,1)S(1)} custom-call(s32[1]{0:T(128)} %bitcast.1.base_ref, f32[128,128]{1,0:T(8,128)S(1)} %copy-done.2), custom_call_target="tpu_custom_call" | custom-call | flops 1000 | bytes 9830400 | tf_op jit(solution)/shard_map/pallas_call | solution.py:148
  88.3 0.0 copy-start.3
  88.3 0.8 copy-done.3
  89.2 3.6 %shard_map.86.refs_2_.weight_ref = bf16[40,128,256]{2,1,0:T(8,128)(2,1)S(1)} custom-call(s32[1]{0:T(128)} %bitcast.base_ref, f32[128,128]{1,0:T(8,128)S(1)} %copy-done.3), custom_call_target="tpu_custom_call" | custom-call | flops 1000 | bytes 16384000 | tf_op jit(solution)/shard_map/pallas_call | solution.py:148
  92.7 4.0 %collective-permute-done.12.refs_0_.refs_4_ = bf16[2,40,2,16,128]{4,3,2,1,0:T(8,128)(2,1)S(1)} collective-permute-done((bf16[2,40,2,16,128]{4,3,2,1,0:T(8,128)(2,1)S(1)}, bf16[2,40,2,16,128]{4,3,2,1,0:T(8,128)(2,1)S(1)}, u32[]{:S(2)}, u32[]{:S(2)}) %collective-permute-start.12) | collective-permute-done | bytes 655392 | tf_op jit(solution)/shard_map/ppermute | solution.py:34
  96.7 1.8 %collective-permute-done.11.refs_1_ = bf16[2,40,2,16,128]{4,3,2,1,0:T(8,128)(2,1)S(1)} collective-permute-done((bf16[2,40,2,16,128]{4,3,2,1,0:T(8,128)(2,1)S(1)}, bf16[2,40,2,16,128]{4,3,2,1,0:T(8,128)(2,1)S(1)}, u32[]{:S(2)}, u32[]{:S(2)}) %collective-permute-start.11) | collective-permute-done | bytes 655392 | tf_op jit(solution)/shard_map/ppermute | solution.py:34
  98.6 0.9 collective-permute-start.13
  99.5 1.2 %collective-permute-start.14 = (bf16[1,40,2,16,128]{4,3,2,1,0:T(8,128)(2,1)S(1)}, bf16[1,40,2,16,128]{4,3,2,1,0:T(8,128)(2,1)S(1)}, u32[]{:S(2)}, u32[]{:S(2)}) collective-permute-start(bf16[1,40,2,16,128]{4,3,2,1,0:T(8,128)(2,1)S(1)} %get-tuple-element.36), channel_id=1, source_target_pairs={{0,96},{32,0},{64,32},{96,64},{1,97},{33,1},{65,33},{97,65},{2,98}... | collective-permute-start | bytes 983048 | tf_op jit(solution)/shard_map/ppermute | solution.py:34
  100.7 4.4 %collective-permute-done.18.refs_1_ = bf16[4,24,2,16,128]{4,3,2,1,0:T(8,128)(2,1)S(1)} collective-permute-done((bf16[4,24,2,16,128]{4,3,2,1,0:T(8,128)(2,1)S(1)}, bf16[4,24,2,16,128]{4,3,2,1,0:T(8,128)(2,1)S(1)}, u32[]{:S(2)}, u32[]{:S(2)}) %collective-permute-start.18) | collective-permute-done | bytes 786464 | tf_op jit(solution)/shard_map/ppermute | solution.py:38
  105.0 3.2 %shard_map.99 = (f32[2,64,16,128]{3,2,1,0:T(8,128)}, bf16[2,64,128,128]{3,2,1,0:T(8,128)(2,1)}) custom-call(s32[8]{0:T(128)S(1)} %fusion.7.places_ref, bf16[24,128,256]{2,1,0:T(8,128)(2,1)S(1)} %shard_map.96.refs_3_.weight_ref, bf16[4,24,2,16,128]{4,3,2,1,0:T(8,128)(2,1)S(1)} %shard_map.98.refs_0_, ...), custom_call_target="tpu_custom_call" | custom-call | flops 503316480 | bytes 9830400 | tf_op jit(solution)/shard_map/pallas_call | solution.py:292
  108.3 0.0 collective-permute-done.13.refs_2_
  108.3 1.0 collective-permute-done.14.refs_3_
  109.3 4.5 %shard_map.100 = (f32[2,64,16,128]{3,2,1,0:T(8,128)}, bf16[2,64,128,128]{3,2,1,0:T(8,128)(2,1)}) custom-call(s32[8]{0:T(128)S(1)} %fusion.7.places_ref, bf16[40,128,256]{2,1,0:T(8,128)(2,1)S(1)} %shard_map.86.refs_2_.weight_ref, bf16[2,40,2,16,128]{4,3,2,1,0:T(8,128)(2,1)S(1)} %shard_map.95.refs_0_, ...), custom_call_target="tpu_custom_call", output_to_operand_aliasing={{0}: (7, {}), {1}: (8, {})} | custom-call | flops 838860800 | bytes 16384000 | tf_op jit(solution)/shard_map/pallas_call | solution.py:292
  (4 shorter events, 0.1 us)
Async XLA Ops:
  4.9 16.5 %collective-permute-start = (bf16[2,5,2,16,1024]{4,3,2,1,0:T(8,128)(2,1)S(1)}, bf16[2,5,2,16,1024]{4,3,2,1,0:T(8,128)(2,1)S(1)}, u32[]{:S(2)}, u32[]{:S(2)}) collective-permute-start(bf16[2,5,2,16,1024]{4,3,2,1,0:T(8,128)(2,1)S(1)} %get-tuple-element.22), channel_id=1, source_target_pairs={{0,32},{32,64},{64,96},{96,0},{1,33},{33,65},{65,97},{97,1},{2,34}... | collective-permute-start | bytes 1966088 | tf_op jit(solution)/shard_map/ppermute | solution.py:34
  5.4 17.4 %collective-permute-start.1 = (bf16[2,5,2,16,1024]{4,3,2,1,0:T(8,128)(2,1)S(1)}, bf16[2,5,2,16,1024]{4,3,2,1,0:T(8,128)(2,1)S(1)}, u32[]{:S(2)}, u32[]{:S(2)}) collective-permute-start(bf16[2,5,2,16,1024]{4,3,2,1,0:T(8,128)(2,1)S(1)} %get-tuple-element.23), channel_id=1, source_target_pairs={{0,96},{32,0},{64,32},{96,64},{1,97},{33,1},{65,33},{97,65},{2,98}... | collective-permute-start | bytes 1966088 | tf_op jit(solution)/shard_map/ppermute | solution.py:34
  9.5 20.3 %collective-permute-start.5 = (bf16[4,3,2,16,1024]{4,3,2,1,0:T(8,128)(2,1)S(1)}, bf16[4,3,2,16,1024]{4,3,2,1,0:T(8,128)(2,1)S(1)}, u32[]{:S(2)}, u32[]{:S(2)}) collective-permute-start(bf16[4,3,2,16,1024]{4,3,2,1,0:T(8,128)(2,1)S(1)} %get-tuple-element.29), channel_id=1, source_target_pairs={{0,16},{16,0},{1,17},{17,1},{2,18},{18,2},{3,19},{19,3},{4,20},{20... | collective-permute-start | bytes 2359304 | tf_op jit(solution)/shard_map/ppermute | solution.py:38
  22.9 10.1 %collective-permute-start.2 = (bf16[1,5,2,16,1024]{4,3,2,1,0:T(8,128)(2,1)S(1)}, bf16[1,5,2,16,1024]{4,3,2,1,0:T(8,128)(2,1)S(1)}, u32[]{:S(2)}, u32[]{:S(2)}) collective-permute-start(bf16[1,5,2,16,1024]{4,3,2,1,0:T(8,128)(2,1)S(1)} %get-tuple-element.24), channel_id=1, source_target_pairs={{0,32},{32,64},{64,96},{96,0},{1,33},{33,65},{65,97},{97,1},{2,34}... | collective-permute-start | bytes 983048 | tf_op jit(solution)/shard_map/ppermute | solution.py:34
  23.4 9.6 %collective-permute-start.3 = (bf16[1,5,2,16,1024]{4,3,2,1,0:T(8,128)(2,1)S(1)}, bf16[1,5,2,16,1024]{4,3,2,1,0:T(8,128)(2,1)S(1)}, u32[]{:S(2)}, u32[]{:S(2)}) collective-permute-start(bf16[1,5,2,16,1024]{4,3,2,1,0:T(8,128)(2,1)S(1)} %get-tuple-element.25), channel_id=1, source_target_pairs={{0,96},{32,0},{64,32},{96,64},{1,97},{33,1},{65,33},{97,65},{2,98}... | collective-permute-start | bytes 983048 | tf_op jit(solution)/shard_map/ppermute | solution.py:34
  29.8 15.0 %copy-start = (bf16[1024,1024]{1,0:T(8,128)(2,1)S(1)}, bf16[1024,1024]{1,0:T(8,128)(2,1)}, u32[]{:S(2)}) copy-start(bf16[1024,1024]{1,0:T(8,128)(2,1)} %constant.116.clone.sin_ref) | copy-start | bytes 6291460
  29.8 15.0 %copy-start.1 = (bf16[1024,1024]{1,0:T(8,128)(2,1)S(1)}, bf16[1024,1024]{1,0:T(8,128)(2,1)}, u32[]{:S(2)}) copy-start(bf16[1024,1024]{1,0:T(8,128)(2,1)} %constant.115.clone.cos_ref) | copy-start | bytes 6291460
  29.8 15.0 %copy-start.4 = (f32[4,1024]{1,0:T(4,128)S(1)}, f32[4,1024]{1,0:T(4,128)}, u32[]{:S(2)}) copy-start(f32[4,1024]{1,0:T(4,128)} %taps_ref.1) | copy-start | bytes 49156
  30.0 7.5 %collective-permute-start.6 = (bf16[3,2,16,1024]{3,2,1,0:T(8,128)(2,1)S(1)}, bf16[3,2,16,1024]{3,2,1,0:T(8,128)(2,1)S(1)}, u32[]{:S(2)}, u32[]{:S(2)}) collective-permute-start(bf16[3,2,16,1024]{3,2,1,0:T(8,128)(2,1)S(1)} %get-tuple-element.31), channel_id=1, source_target_pairs={{0,32},{32,64},{64,96},{96,0},{1,33},{33,65},{65,97},{97,1},{2,34}... | collective-permute-start | bytes 589832 | tf_op jit(solution)/shard_map/ppermute | solution.py:34
  31.7 8.6 %collective-permute-start.7 = (bf16[3,2,16,1024]{3,2,1,0:T(8,128)(2,1)S(1)}, bf16[3,2,16,1024]{3,2,1,0:T(8,128)(2,1)S(1)}, u32[]{:S(2)}, u32[]{:S(2)}) collective-permute-start(bf16[3,2,16,1024]{3,2,1,0:T(8,128)(2,1)S(1)} %get-tuple-element.32), channel_id=1, source_target_pairs={{0,64},{32,96},{64,0},{96,32},{1,65},{33,97},{65,1},{97,33},{2,66}... | collective-permute-start | bytes 589832 | tf_op jit(solution)/shard_map/ppermute | solution.py:34
  33.0 9.4 %collective-permute-start.8 = (bf16[3,2,16,1024]{3,2,1,0:T(8,128)(2,1)S(1)}, bf16[3,2,16,1024]{3,2,1,0:T(8,128)(2,1)S(1)}, u32[]{:S(2)}, u32[]{:S(2)}) collective-permute-start(bf16[3,2,16,1024]{3,2,1,0:T(8,128)(2,1)S(1)} %get-tuple-element.33), channel_id=1, source_target_pairs={{0,96},{32,0},{64,32},{96,64},{1,97},{33,1},{65,33},{97,65},{2,98}... | collective-permute-start | bytes 589832 | tf_op jit(solution)/shard_map/ppermute | solution.py:34
  33.2 11.6 %collective-permute-start.4 = (bf16[1,5,2,16,1024]{4,3,2,1,0:T(8,128)(2,1)S(1)}, bf16[1,5,2,16,1024]{4,3,2,1,0:T(8,128)(2,1)S(1)}, u32[]{:S(2)}, u32[]{:S(2)}) collective-permute-start(bf16[1,5,2,16,1024]{4,3,2,1,0:T(8,128)(2,1)S(1)} %get-tuple-element.27), channel_id=1, source_target_pairs={{0,16},{16,0},{1,17},{17,1},{2,18},{18,2},{3,19},{19,3},{4,20},{20... | collective-permute-start | bytes 983048 | tf_op jit(solution)/shard_map/ppermute | solution.py:38
  42.5 2.4 %collective-permute-start.9 = (bf16[3,2,16,1024]{3,2,1,0:T(8,128)(2,1)S(1)}, bf16[3,2,16,1024]{3,2,1,0:T(8,128)(2,1)S(1)}, u32[]{:S(2)}, u32[]{:S(2)}) collective-permute-start(bf16[3,2,16,1024]{3,2,1,0:T(8,128)(2,1)S(1)} %shard_map.92.late_ref), channel_id=1, source_target_pairs={{0,1},{1,2},{2,3},{3,4},{4,5},{5,6},{6,7},{7,8},{8,9},{9,10},{10,1... | collective-permute-start | bytes 589832 | tf_op jit(solution)/shard_map/ppermute | solution.py:377
  69.6 10.5 %collective-permute-start.10 = (bf16[40,2,16,128]{3,2,1,0:T(8,128)(2,1)S(1)}, bf16[40,2,16,128]{3,2,1,0:T(8,128)(2,1)S(1)}, u32[]{:S(2)}, u32[]{:S(2)}) collective-permute-start(bf16[40,2,16,128]{3,2,1,0:T(8,128)(2,1)S(1)} %get-tuple-element.34.refs_0_), channel_id=1, source_target_pairs={{0,16},{16,0},{1,17},{17,1},{2,18},{18,2},{3,19},{19,3},{4,20},{20... | collective-permute-start | bytes 983048 | tf_op jit(solution)/shard_map/ppermute | solution.py:38
  72.6 9.7 %collective-permute-start.17 = (bf16[24,2,16,128]{3,2,1,0:T(8,128)(2,1)S(1)}, bf16[24,2,16,128]{3,2,1,0:T(8,128)(2,1)S(1)}, u32[]{:S(2)}, u32[]{:S(2)}) collective-permute-start(bf16[24,2,16,128]{3,2,1,0:T(8,128)(2,1)S(1)} %get-tuple-element.37.refs_0_), channel_id=1, source_target_pairs={{0,32},{32,64},{64,96},{96,0},{1,33},{33,65},{65,97},{97,1},{2,34}... | collective-permute-start | bytes 589832 | tf_op jit(solution)/shard_map/ppermute | solution.py:34
  73.2 9.3 %collective-permute-start.16 = (bf16[24,2,16,128]{3,2,1,0:T(8,128)(2,1)S(1)}, bf16[24,2,16,128]{3,2,1,0:T(8,128)(2,1)S(1)}, u32[]{:S(2)}, u32[]{:S(2)}) collective-permute-start(bf16[24,2,16,128]{3,2,1,0:T(8,128)(2,1)S(1)} %get-tuple-element.37.refs_0_), channel_id=1, source_target_pairs={{0,64},{32,96},{64,0},{96,32},{1,65},{33,97},{65,1},{97,33},{2,66}... | collective-permute-start | bytes 589832 | tf_op jit(solution)/shard_map/ppermute | solution.py:34
  74.4 10.7 %collective-permute-start.15 = (bf16[24,2,16,128]{3,2,1,0:T(8,128)(2,1)S(1)}, bf16[24,2,16,128]{3,2,1,0:T(8,128)(2,1)S(1)}, u32[]{:S(2)}, u32[]{:S(2)}) collective-permute-start(bf16[24,2,16,128]{3,2,1,0:T(8,128)(2,1)S(1)} %get-tuple-element.37.refs_0_), channel_id=1, source_target_pairs={{0,96},{32,0},{64,32},{96,64},{1,97},{33,1},{65,33},{97,65},{2,98}... | collective-permute-start | bytes 589832 | tf_op jit(solution)/shard_map/ppermute | solution.py:34
  80.2 16.5 %collective-permute-start.12 = (bf16[2,40,2,16,128]{4,3,2,1,0:T(8,128)(2,1)S(1)}, bf16[2,40,2,16,128]{4,3,2,1,0:T(8,128)(2,1)S(1)}, u32[]{:S(2)}, u32[]{:S(2)}) collective-permute-start(bf16[2,40,2,16,128]{4,3,2,1,0:T(8,128)(2,1)S(1)} %shard_map.95.refs_0_), channel_id=1, source_target_pairs={{0,32},{32,64},{64,96},{96,0},{1,33},{33,65},{65,97},{97,1},{2,34}... | collective-permute-start | bytes 1966088 | tf_op jit(solution)/shard_map/ppermute | solution.py:34
  80.8 17.7 %collective-permute-start.11 = (bf16[2,40,2,16,128]{4,3,2,1,0:T(8,128)(2,1)S(1)}, bf16[2,40,2,16,128]{4,3,2,1,0:T(8,128)(2,1)S(1)}, u32[]{:S(2)}, u32[]{:S(2)}) collective-permute-start(bf16[2,40,2,16,128]{4,3,2,1,0:T(8,128)(2,1)S(1)} %shard_map.95.refs_0_), channel_id=1, source_target_pairs={{0,96},{32,0},{64,32},{96,64},{1,97},{33,1},{65,33},{97,65},{2,98}... | collective-permute-start | bytes 1966088 | tf_op jit(solution)/shard_map/ppermute | solution.py:34
  85.2 19.9 %collective-permute-start.18 = (bf16[4,24,2,16,128]{4,3,2,1,0:T(8,128)(2,1)S(1)}, bf16[4,24,2,16,128]{4,3,2,1,0:T(8,128)(2,1)S(1)}, u32[]{:S(2)}, u32[]{:S(2)}) collective-permute-start(bf16[4,24,2,16,128]{4,3,2,1,0:T(8,128)(2,1)S(1)} %shard_map.98.refs_0_), channel_id=1, source_target_pairs={{0,16},{16,0},{1,17},{17,1},{2,18},{18,2},{3,19},{19,3},{4,20},{20... | collective-permute-start | bytes 2359304 | tf_op jit(solution)/shard_map/ppermute | solution.py:38
  85.3 0.8 copy-start.2
  88.3 0.8 copy-start.3
  98.6 9.7 %collective-permute-start.13 = (bf16[1,40,2,16,128]{4,3,2,1,0:T(8,128)(2,1)S(1)}, bf16[1,40,2,16,128]{4,3,2,1,0:T(8,128)(2,1)S(1)}, u32[]{:S(2)}, u32[]{:S(2)}) collective-permute-start(bf16[1,40,2,16,128]{4,3,2,1,0:T(8,128)(2,1)S(1)} %get-tuple-element.35), channel_id=1, source_target_pairs={{0,32},{32,64},{64,96},{96,0},{1,33},{33,65},{65,97},{97,1},{2,34}... | collective-permute-start | bytes 983048 | tf_op jit(solution)/shard_map/ppermute | solution.py:34
  99.5 9.8 %collective-permute-start.14 = (bf16[1,40,2,16,128]{4,3,2,1,0:T(8,128)(2,1)S(1)}, bf16[1,40,2,16,128]{4,3,2,1,0:T(8,128)(2,1)S(1)}, u32[]{:S(2)}, u32[]{:S(2)}) collective-permute-start(bf16[1,40,2,16,128]{4,3,2,1,0:T(8,128)(2,1)S(1)} %get-tuple-element.36), channel_id=1, source_target_pairs={{0,96},{32,0},{64,32},{96,64},{1,97},{33,1},{65,33},{97,65},{2,98}... | collective-permute-start | bytes 983048 | tf_op jit(solution)/shard_map/ppermute | solution.py:34

commit v4 on v3

--- a/solution.py
+++ b/solution.py
@@ -25,7 +25,6 @@
 EARLY = LOCAL_FRAMES - LATE
 LOCAL_CHANS = 64
 FIRST = 40
-STEP = 8
 BF16 = jnp.bfloat16
 F32 = jnp.float32
 
@@ -165,39 +164,36 @@
             return early_refs[0][0, t, z].astype(F32) + early_refs[1][0, t, z].astype(F32)
         return late_ref[t - EARLY, z].astype(F32)
 
-    @pl.when(pl.program_id(0) == 0)
-    def _():
-        for z in range(2):
-            for t in range(LOCAL_FRAMES):
-                total = taps_ref[0:1, :] * frame(t, z)
-                for m in range(1, TAPS):
-                    total = total + taps_ref[m : m + 1, :] * frame(t - m, z)
-                filt_ref[z * TILES + t * PER : z * TILES + (t + 1) * PER, :] = total.astype(BF16)
-
-    by_cos = jnp.dot(filt_ref[...], cos_ref[...], preferred_element_type=F32)
-    by_sin = jnp.dot(filt_ref[...], sin_ref[...], preferred_element_type=F32)
-    real = by_cos[0:128] + by_sin[128:256]
-    quad = by_cos[128:256] - by_sin[0:128]
-    for n in range(real.shape[1] // 128):
-        lanes = slice(n * 128, (n + 1) * 128)
-        own, other = real[:, lanes], quad[:, lanes]
-        out_ref[2 * n] = jnp.concatenate([own[:, 0:64], other[:, 0:64]], axis=1).astype(BF16)
-        out_ref[2 * n + 1] = jnp.concatenate([own[:, 64:128], other[:, 64:128]], axis=1).astype(BF16)
+    for z in range(2):
+        for t in range(LOCAL_FRAMES):
+            total = taps_ref[0:1, :] * frame(t, z)
+            for m in range(1, TAPS):
+                total = total + taps_ref[m : m + 1, :] * frame(t - m, z)
+            filt_ref[z * TILES + t * PER : z * TILES + (t + 1) * PER, :] = total.astype(BF16)
+
+    block = 256
+    for begin in range(0, CHANNELS, block):
+        columns = slice(begin, begin + block)
+        by_cos = jnp.dot(filt_ref[...], cos_ref[:, columns], preferred_element_type=F32)
+        by_sin = jnp.dot(filt_ref[...], sin_ref[:, columns], preferred_element_type=F32)
+        real = by_cos[0:128] + by_sin[128:256]
+        quad = by_cos[128:256] - by_sin[0:128]
+        for n in range(block // 128):
+            lanes = slice(n * 128, (n + 1) * 128)
+            own, other = real[:, lanes], quad[:, lanes]
+            place = begin // LOCAL_CHANS + 2 * n
+            out_ref[place] = jnp.concatenate([own[:, 0:64], other[:, 0:64]], axis=1).astype(BF16)
+            out_ref[place + 1] = jnp.concatenate([own[:, 64:128], other[:, 64:128]], axis=1).astype(BF16)
 
 
 def spectra(early, late, past, taps, cos_table, sin_table):
-    block = 512
-    whole = lambda a: pl.BlockSpec(a.shape, lambda i: (0,) * a.ndim)
-    columns = pl.BlockSpec((CHANNELS, block), lambda i: (0, i))
-
-    def kernel(own_ref, got_ref, late_ref, past_ref, taps_ref, cos_ref, sin_ref, *refs):
-        spectra_kernel((own_ref, got_ref), late_ref, past_ref, taps_ref, cos_ref, sin_ref, *refs[-2:])
+    def kernel(own_ref, got_ref, late_ref, past_ref, taps_ref, cos_ref, sin_ref, out_ref, filt_ref):
+        spectra_kernel((own_ref, got_ref), late_ref, past_ref, taps_ref, cos_ref, sin_ref, out_ref, filt_ref)
 
     return pl.pallas_call(
         kernel,
-        grid=(CHANNELS // block,),
-        in_specs=[whole(a) for a in (*early, late, past, taps)] + [columns] * 2,
-        out_specs=pl.BlockSpec((block // LOCAL_CHANS, TILES, 128), lambda i: (i, 0, 0)),
+        in_specs=[IN_VMEM] * 7,
+        out_specs=IN_VMEM,
         out_shape=jax.ShapeDtypeStruct((CHANNELS // LOCAL_CHANS, TILES, 128), BF16),
         scratch_shapes=[pltpu.VMEM((256, CHANNELS), BF16)],
         compiler_params=params(12),
@@ -235,10 +231,11 @@
     vis_scale = 1.0 / (FRAMES * FEEDS / TILES)
     beam_scale = 1.0 / math.sqrt(FEEDS)
     dims = (((1,), (1,)), ((), ()))
-    steps = weight_ref.shape[0] // STEP
+    each = both_ref.shape[0]
+    steps = weight_ref.shape[0] // each
 
     def copies(step):
-        here, there = pl.ds(step * STEP, STEP), pl.ds(begin + step * STEP, STEP)
+        here, there = pl.ds(step * each, each), pl.ds(begin + step * each, each)
         return [
             pltpu.make_async_copy(source.at[z, here], target.at[z, there], sem.at[z, step])
             for source, target, sem in ((vis_out, vis_ref, vis_sem), (beam_out, beam_ref, beam_sem))
@@ -247,8 +244,8 @@
 
     @pl.loop(0, steps)
     def _(step):
-        for c in range(STEP):
-            here = step * STEP + c
+        for c in range(each):
+            here = step * each + c
             for place, (array, index) in enumerate(blocks):
                 row = pl.multiple_of(places_ref[place] * PER, PER)
                 real, quad = block_refs[array][index, here, 0], block_refs[array][index, here, 1]
@@ -256,8 +253,8 @@
                 both_ref[c, pl.ds(row, PER), 128:256] = quad
                 both_ref[c, pl.ds(TILES + row, PER), 0:128] = quad
                 both_ref[c, pl.ds(TILES + row, PER), 128:256] = -real
-        for c in range(STEP):
-            here = step * STEP + c
+        for c in range(each):
+            here = step * each + c
             beams = jnp.dot(weight_ref[here], both_ref[c], preferred_element_type=F32) * beam_scale
             beam_out[0, here] = beams[:, 0:128].astype(BF16)
             beam_out[1, here] = beams[:, 128:256].astype(BF16)
@@ -285,6 +282,7 @@
             arrays.append(array)
         layout.append((next(n for n, a in enumerate(arrays) if a is array), index))
     count, beams = weights.shape[:2]
+    each = next(n for n in (10, 8) if count % n == 0)
 
     def kernel(places_ref, weight_ref, *refs):
         products_kernel(begin, layout, places_ref, weight_ref, refs[: len(arrays)], *refs[len(arrays) + len(results) :])
@@ -298,11 +296,11 @@
             jax.ShapeDtypeStruct((2, LOCAL_CHANS, beams, FRAMES), BF16),
         ],
         scratch_shapes=[
-            pltpu.VMEM((STEP, 2 * TILES, 256), BF16),
+            pltpu.VMEM((each, 2 * TILES, 256), BF16),
             pltpu.VMEM((2, count, PER, TILES), F32),
             pltpu.VMEM((2, count, beams, FRAMES), BF16),
-            pltpu.SemaphoreType.DMA((2, count // STEP)),
-            pltpu.SemaphoreType.DMA((2, count // STEP)),
+            pltpu.SemaphoreType.DMA((2, count // each)),
+            pltpu.SemaphoreType.DMA((2, count // each)),
         ],
         input_output_aliases={2 + len(arrays) + n: n for n in range(len(results))},
         compiler_params=params(8),

time: 114 us -> 113 us (level)
  no operation moved by 1% of the time
where the time goes in v4:
time: 113 us
  waiting for transfers between devices  40.5 us (36%)
  starting transfers between devices  25 us (22%)
  Pallas kernels  22.2 us (20%)
  blocking collectives  21.8 us (19%)
  local copies, waits for them, and re-layouts  1.68 us (1%)
    ppermute x14, waiting for transfers between devices, ring(): return lax.ppermute(v, 'x', [(i, (i + by) % NX) for i in range(NX)])  25.4 us
    all_to_all x1, blocking collectives, local(): first, second = turn(lax.all_to_all(spec, DEV, 0, 0, tiled=True))  21.8 us
    ppermute x4, waiting for transfers between devices, pair(): return lax.ppermute(v, 'yh', [(0, 1), (1, 0)])  14.1 us
    ppermute x14, starting transfers between devices, ring(): return lax.ppermute(v, 'x', [(i, (i + by) % NX) for i in range(NX)])  14 us
    ppermute x4, starting transfers between devices, pair(): return lax.ppermute(v, 'yh', [(0, 1), (1, 0)])  9.72 us
    pallas_call x2, Pallas kernels, products(): pl.pallas_call(kernel, in_specs=[IN_SMEM] + [IN_VMEM] * (1 + len(arrays))...  7.59 us
    pallas_call x2, Pallas kernels, tile_sums(): pl.pallas_call(functools.partial(tile_sums_kernel, first, frames, groups)...  6.03 us
    pallas_call x2, Pallas kernels, beam_weights(): pl.pallas_call(weights_kernel, in_specs=[IN_SMEM, IN_VMEM], out_specs=IN_...  5.68 us
  transfers between devices with their start and end apart: 19, of which 14 were waited for; matrix products, arithmetic and copies ran while one was open for 0% of the time, Pallas kernels for 11%

profile of v4, /device:TPU:6, one launch (start us, length us, event | category | flops | bytes accessed | tf_op | source)
XLA Modules:
  0.0 112.7 jit_solution(14617373475277098206)
XLA Ops:
  0.6 0.7 compare_select_fusion.4
  1.4 3.5 %shard_map.87 = (bf16[2,5,2,16,1024]{4,3,2,1,0:T(8,128)(2,1)S(1)}, bf16[2,5,2,16,1024]{4,3,2,1,0:T(8,128)(2,1)S(1)}, bf16[4,5,2,16,1024]{4,3,2,1,0:T(8,128)(2,1)S(1)}) custom-call(bf16[128,256]{1,0:T(8,128)(2,1)S(1)} %fusion.member_ref, bf16[2,256,8192]{2,1,0:T(8,128)(2,1)} %volts_ref.3), custom_call_target="tpu_custom_call" | custom-call | flops 671088640 | bytes 15728640 | tf_op jit(solution)/shard_map/pallas_call | solution.py:102
  4.9 0.5 collective-permute-start
  5.4 1.6 %collective-permute-start.1 = (bf16[2,5,2,16,1024]{4,3,2,1,0:T(8,128)(2,1)S(1)}, bf16[2,5,2,16,1024]{4,3,2,1,0:T(8,128)(2,1)S(1)}, u32[]{:S(2)}, u32[]{:S(2)}) collective-permute-start(bf16[2,5,2,16,1024]{4,3,2,1,0:T(8,128)(2,1)S(1)} %get-tuple-element.23), channel_id=1, source_target_pairs={{0,96},{32,0},{64,32},{96,64},{1,97},{33,1},{65,33},{97,65},{2,98}... | collective-permute-start | bytes 1966088 | tf_op jit(solution)/shard_map/ppermute | solution.py:33
  7.0 2.5 %shard_map.90 = (bf16[4,3,2,16,1024]{4,3,2,1,0:T(8,128)(2,1)S(1)}, bf16[4,3,2,16,1024]{4,3,2,1,0:T(8,128)(2,1)S(1)}) custom-call(bf16[128,256]{1,0:T(8,128)(2,1)S(1)} %fusion.member_ref, bf16[2,256,8192]{2,1,0:T(8,128)(2,1)} %volts_ref.3, bf16[4,5,2,16,1024]{4,3,2,1,0:T(8,128)(2,1)S(1)} %get-tuple-element.21.refs_0_), custom_call_target="tpu_custom_call" | custom-call | flops 402653184 | bytes 9437184 | tf_op jit(solution)/shard_map/pallas_call | solution.py:102
  9.5 3.3 %collective-permute-start.5 = (bf16[4,3,2,16,1024]{4,3,2,1,0:T(8,128)(2,1)S(1)}, bf16[4,3,2,16,1024]{4,3,2,1,0:T(8,128)(2,1)S(1)}, u32[]{:S(2)}, u32[]{:S(2)}) collective-permute-start(bf16[4,3,2,16,1024]{4,3,2,1,0:T(8,128)(2,1)S(1)} %get-tuple-element.29), channel_id=1, source_target_pairs={{0,16},{16,0},{1,17},{17,1},{2,18},{18,2},{3,19},{19,3},{4,20},{20... | collective-permute-start | bytes 2359304 | tf_op jit(solution)/shard_map/ppermute | solution.py:37
  12.8 8.6 %collective-permute-done.refs_1_.refs_3_ = bf16[2,5,2,16,1024]{4,3,2,1,0:T(8,128)(2,1)S(1)} collective-permute-done((bf16[2,5,2,16,1024]{4,3,2,1,0:T(8,128)(2,1)S(1)}, bf16[2,5,2,16,1024]{4,3,2,1,0:T(8,128)(2,1)S(1)}, u32[]{:S(2)}, u32[]{:S(2)}) %collective-permute-start) | collective-permute-done | bytes 655392 | tf_op jit(solution)/shard_map/ppermute | solution.py:33
  21.4 1.3 %collective-permute-done.1.refs_2_.refs_4_ = bf16[2,5,2,16,1024]{4,3,2,1,0:T(8,128)(2,1)S(1)} collective-permute-done((bf16[2,5,2,16,1024]{4,3,2,1,0:T(8,128)(2,1)S(1)}, bf16[2,5,2,16,1024]{4,3,2,1,0:T(8,128)(2,1)S(1)}, u32[]{:S(2)}, u32[]{:S(2)}) %collective-permute-start.1) | collective-permute-done | bytes 655392 | tf_op jit(solution)/shard_map/ppermute | solution.py:33
  22.7 0.2 shard_map.88
  22.9 0.5 collective-permute-start.2
  23.4 1.6 %collective-permute-start.3 = (bf16[1,5,2,16,1024]{4,3,2,1,0:T(8,128)(2,1)S(1)}, bf16[1,5,2,16,1024]{4,3,2,1,0:T(8,128)(2,1)S(1)}, u32[]{:S(2)}, u32[]{:S(2)}) collective-permute-start(bf16[1,5,2,16,1024]{4,3,2,1,0:T(8,128)(2,1)S(1)} %get-tuple-element.25), channel_id=1, source_target_pairs={{0,96},{32,0},{64,32},{96,64},{1,97},{33,1},{65,33},{97,65},{2,98}... | collective-permute-start | bytes 983048 | tf_op jit(solution)/shard_map/ppermute | solution.py:33
  25.0 4.8 %collective-permute-done.5.refs_1_ = bf16[4,3,2,16,1024]{4,3,2,1,0:T(8,128)(2,1)S(1)} collective-permute-done((bf16[4,3,2,16,1024]{4,3,2,1,0:T(8,128)(2,1)S(1)}, bf16[4,3,2,16,1024]{4,3,2,1,0:T(8,128)(2,1)S(1)}, u32[]{:S(2)}, u32[]{:S(2)}) %collective-permute-start.5) | collective-permute-done | bytes 786464 | tf_op jit(solution)/shard_map/ppermute | solution.py:37
  29.8 0.0 copy-start
  29.8 0.0 copy-start.1
  29.8 0.0 copy-start.4
  29.8 0.2 shard_map.91
  30.0 1.7 %collective-permute-start.6 = (bf16[3,2,16,1024]{3,2,1,0:T(8,128)(2,1)S(1)}, bf16[3,2,16,1024]{3,2,1,0:T(8,128)(2,1)S(1)}, u32[]{:S(2)}, u32[]{:S(2)}) collective-permute-start(bf16[3,2,16,1024]{3,2,1,0:T(8,128)(2,1)S(1)} %get-tuple-element.31), channel_id=1, source_target_pairs={{0,32},{32,64},{64,96},{96,0},{1,33},{33,65},{65,97},{97,1},{2,34}... | collective-permute-start | bytes 589832 | tf_op jit(solution)/shard_map/ppermute | solution.py:33
  31.7 1.3 %collective-permute-start.7 = (bf16[3,2,16,1024]{3,2,1,0:T(8,128)(2,1)S(1)}, bf16[3,2,16,1024]{3,2,1,0:T(8,128)(2,1)S(1)}, u32[]{:S(2)}, u32[]{:S(2)}) collective-permute-start(bf16[3,2,16,1024]{3,2,1,0:T(8,128)(2,1)S(1)} %get-tuple-element.32), channel_id=1, source_target_pairs={{0,64},{32,96},{64,0},{96,32},{1,65},{33,97},{65,1},{97,33},{2,66}... | collective-permute-start | bytes 589832 | tf_op jit(solution)/shard_map/ppermute | solution.py:33
  33.0 0.0 collective-permute-start.8
  33.0 0.0 collective-permute-done.2.refs_1_
  33.0 0.0 collective-permute-done.3.refs_2_
  33.0 0.2 shard_map.89
  33.2 3.3 %collective-permute-start.4 = (bf16[1,5,2,16,1024]{4,3,2,1,0:T(8,128)(2,1)S(1)}, bf16[1,5,2,16,1024]{4,3,2,1,0:T(8,128)(2,1)S(1)}, u32[]{:S(2)}, u32[]{:S(2)}) collective-permute-start(bf16[1,5,2,16,1024]{4,3,2,1,0:T(8,128)(2,1)S(1)} %get-tuple-element.27), channel_id=1, source_target_pairs={{0,16},{16,0},{1,17},{17,1},{2,18},{18,2},{3,19},{19,3},{4,20},{20... | collective-permute-start | bytes 983048 | tf_op jit(solution)/shard_map/ppermute | solution.py:37
  36.5 1.0 collective-permute-done.6.refs_1_
  37.5 2.8 %collective-permute-done.7.refs_2_ = bf16[3,2,16,1024]{3,2,1,0:T(8,128)(2,1)S(1)} collective-permute-done((bf16[3,2,16,1024]{3,2,1,0:T(8,128)(2,1)S(1)}, bf16[3,2,16,1024]{3,2,1,0:T(8,128)(2,1)S(1)}, u32[]{:S(2)}, u32[]{:S(2)}) %collective-permute-start.7) | collective-permute-done | bytes 196640 | tf_op jit(solution)/shard_map/ppermute | solution.py:33
  40.3 2.0 %collective-permute-done.8.refs_3_ = bf16[3,2,16,1024]{3,2,1,0:T(8,128)(2,1)S(1)} collective-permute-done((bf16[3,2,16,1024]{3,2,1,0:T(8,128)(2,1)S(1)}, bf16[3,2,16,1024]{3,2,1,0:T(8,128)(2,1)S(1)}, u32[]{:S(2)}, u32[]{:S(2)}) %collective-permute-start.8) | collective-permute-done | bytes 196640 | tf_op jit(solution)/shard_map/ppermute | solution.py:33
  42.4 0.1 shard_map.92.late_ref
  42.5 1.3 %collective-permute-start.9 = (bf16[3,2,16,1024]{3,2,1,0:T(8,128)(2,1)S(1)}, bf16[3,2,16,1024]{3,2,1,0:T(8,128)(2,1)S(1)}, u32[]{:S(2)}, u32[]{:S(2)}) collective-permute-start(bf16[3,2,16,1024]{3,2,1,0:T(8,128)(2,1)S(1)} %shard_map.92.late_ref), channel_id=1, source_target_pairs={{0,1},{1,2},{2,3},{3,4},{4,5},{5,6},{6,7},{7,8},{8,9},{9,10},{10,1... | collective-permute-start | bytes 589832 | tf_op jit(solution)/shard_map/ppermute | solution.py:375
  43.8 1.0 collective-permute-done.9.past_ref
  44.8 0.0 collective-permute-done.4.got_ref
  44.8 0.0 copy-done
  44.8 0.0 copy-done.1
  44.8 0.0 copy-done.4
  44.8 1.4 %shard_map.93 = bf16[16,128,128]{2,1,0:T(8,128)(2,1)S(1)} custom-call(bf16[1,5,2,16,1024]{4,3,2,1,0:T(8,128)(2,1)S(1)} %get-tuple-element.26.own_ref, bf16[1,5,2,16,1024]{4,3,2,1,0:T(8,128)(2,1)S(1)} %collective-permute-done.4.got_ref, bf16[3,2,16,1024]{3,2,1,0:T(8,128)(2,1)S(1)} %shard_map.92.late_ref, ...), custom_call_target="tpu_custom_call" | custom-call | flops 1073741824 | bytes 6291456 | tf_op jit(solution)/shard_map/pallas_call | solution.py:193
  46.3 21.8 %all_to_all.5.in_ref = bf16[16,128,128]{2,1,0:T(8,128)(2,1)S(1)} all-to-all(bf16[16,128,128]{2,1,0:T(8,128)(2,1)S(1)} %shard_map.93), channel_id=1, replica_groups=mesh['x'=4,'yh'=2,'yl'=2,'z'=4,'core'=2] {'yl','z','core'}, dimensions={0} | all-to-all | bytes 1048576 | tf_op jit(solution)/shard_map/all_to_all | solution.py:377
  68.0 0.7 shard_map.94
  68.7 3.0 %collective-permute-start.10 = (bf16[40,2,16,128]{3,2,1,0:T(8,128)(2,1)S(1)}, bf16[40,2,16,128]{3,2,1,0:T(8,128)(2,1)S(1)}, u32[]{:S(2)}, u32[]{:S(2)}) collective-permute-start(bf16[40,2,16,128]{3,2,1,0:T(8,128)(2,1)S(1)} %get-tuple-element.34.refs_0_), channel_id=1, source_target_pairs={{0,16},{16,0},{1,17},{17,1},{2,18},{18,2},{3,19},{19,3},{4,20},{20... | collective-permute-start | bytes 983048 | tf_op jit(solution)/shard_map/ppermute | solution.py:37
  71.7 0.6 collective-permute-start.17
  72.3 1.2 %collective-permute-start.16 = (bf16[24,2,16,128]{3,2,1,0:T(8,128)(2,1)S(1)}, bf16[24,2,16,128]{3,2,1,0:T(8,128)(2,1)S(1)}, u32[]{:S(2)}, u32[]{:S(2)}) collective-permute-start(bf16[24,2,16,128]{3,2,1,0:T(8,128)(2,1)S(1)} %get-tuple-element.37.refs_0_), channel_id=1, source_target_pairs={{0,64},{32,96},{64,0},{96,32},{1,65},{33,97},{65,1},{97,33},{2,66}... | collective-permute-start | bytes 589832 | tf_op jit(solution)/shard_map/ppermute | solution.py:33
  73.5 0.8 collective-permute-start.15
  74.3 4.9 %collective-permute-done.10.refs_1_ = bf16[40,2,16,128]{3,2,1,0:T(8,128)(2,1)S(1)} collective-permute-done((bf16[40,2,16,128]{3,2,1,0:T(8,128)(2,1)S(1)}, bf16[40,2,16,128]{3,2,1,0:T(8,128)(2,1)S(1)}, u32[]{:S(2)}, u32[]{:S(2)}) %collective-permute-start.10) | collective-permute-done | bytes 327712 | tf_op jit(solution)/shard_map/ppermute | solution.py:37
  79.3 0.6 collective-permute-start.12
  79.9 1.5 %collective-permute-start.11 = (bf16[2,40,2,16,128]{4,3,2,1,0:T(8,128)(2,1)S(1)}, bf16[2,40,2,16,128]{4,3,2,1,0:T(8,128)(2,1)S(1)}, u32[]{:S(2)}, u32[]{:S(2)}) collective-permute-start(bf16[2,40,2,16,128]{4,3,2,1,0:T(8,128)(2,1)S(1)} %shard_map.95.refs_0_), channel_id=1, source_target_pairs={{0,96},{32,0},{64,32},{96,64},{1,97},{33,1},{65,33},{97,65},{2,98}... | collective-permute-start | bytes 1966088 | tf_op jit(solution)/shard_map/ppermute | solution.py:33
  81.4 0.0 collective-permute-done.17.refs_3_
  81.4 0.1 collective-permute-done.16.refs_2_
  81.5 2.7 %collective-permute-done.15.refs_1_ = bf16[24,2,16,128]{3,2,1,0:T(8,128)(2,1)S(1)} collective-permute-done((bf16[24,2,16,128]{3,2,1,0:T(8,128)(2,1)S(1)}, bf16[24,2,16,128]{3,2,1,0:T(8,128)(2,1)S(1)}, u32[]{:S(2)}, u32[]{:S(2)}) %collective-permute-start.15) | collective-permute-done | bytes 196640 | tf_op jit(solution)/shard_map/ppermute | solution.py:33
  84.2 0.1 shard_map.98.refs_0_
  84.3 0.2 collective-permute-start.18
  84.5 0.0 copy-start.2
  84.5 0.8 copy-done.2
  85.3 2.1 %shard_map.96.refs_3_.weight_ref = bf16[24,128,256]{2,1,0:T(8,128)(2,1)S(1)} custom-call(s32[1]{0:T(128)} %bitcast.1.base_ref, f32[128,128]{1,0:T(8,128)S(1)} %copy-done.2), custom_call_target="tpu_custom_call" | custom-call | flops 1000 | bytes 9830400 | tf_op jit(solution)/shard_map/pallas_call | solution.py:147
  87.4 0.0 copy-start.3
  87.4 0.8 copy-done.3
  88.3 3.6 %shard_map.86.refs_2_.weight_ref = bf16[40,128,256]{2,1,0:T(8,128)(2,1)S(1)} custom-call(s32[1]{0:T(128)} %bitcast.base_ref, f32[128,128]{1,0:T(8,128)S(1)} %copy-done.3), custom_call_target="tpu_custom_call" | custom-call | flops 1000 | bytes 16384000 | tf_op jit(solution)/shard_map/pallas_call | solution.py:147
  91.8 4.0 %collective-permute-done.12.refs_0_.refs_4_ = bf16[2,40,2,16,128]{4,3,2,1,0:T(8,128)(2,1)S(1)} collective-permute-done((bf16[2,40,2,16,128]{4,3,2,1,0:T(8,128)(2,1)S(1)}, bf16[2,40,2,16,128]{4,3,2,1,0:T(8,128)(2,1)S(1)}, u32[]{:S(2)}, u32[]{:S(2)}) %collective-permute-start.12) | collective-permute-done | bytes 655392 | tf_op jit(solution)/shard_map/ppermute | solution.py:33
  95.8 1.8 %collective-permute-done.11.refs_1_ = bf16[2,40,2,16,128]{4,3,2,1,0:T(8,128)(2,1)S(1)} collective-permute-done((bf16[2,40,2,16,128]{4,3,2,1,0:T(8,128)(2,1)S(1)}, bf16[2,40,2,16,128]{4,3,2,1,0:T(8,128)(2,1)S(1)}, u32[]{:S(2)}, u32[]{:S(2)}) %collective-permute-start.11) | collective-permute-done | bytes 655392 | tf_op jit(solution)/shard_map/ppermute | solution.py:33
  97.7 0.9 collective-permute-start.13
  98.6 1.2 %collective-permute-start.14 = (bf16[1,40,2,16,128]{4,3,2,1,0:T(8,128)(2,1)S(1)}, bf16[1,40,2,16,128]{4,3,2,1,0:T(8,128)(2,1)S(1)}, u32[]{:S(2)}, u32[]{:S(2)}) collective-permute-start(bf16[1,40,2,16,128]{4,3,2,1,0:T(8,128)(2,1)S(1)} %get-tuple-element.36), channel_id=1, source_target_pairs={{0,96},{32,0},{64,32},{96,64},{1,97},{33,1},{65,33},{97,65},{2,98}... | collective-permute-start | bytes 983048 | tf_op jit(solution)/shard_map/ppermute | solution.py:33
  99.8 4.4 %collective-permute-done.18.refs_1_ = bf16[4,24,2,16,128]{4,3,2,1,0:T(8,128)(2,1)S(1)} collective-permute-done((bf16[4,24,2,16,128]{4,3,2,1,0:T(8,128)(2,1)S(1)}, bf16[4,24,2,16,128]{4,3,2,1,0:T(8,128)(2,1)S(1)}, u32[]{:S(2)}, u32[]{:S(2)}) %collective-permute-start.18) | collective-permute-done | bytes 786464 | tf_op jit(solution)/shard_map/ppermute | solution.py:37
  104.1 3.2 %shard_map.99 = (f32[2,64,16,128]{3,2,1,0:T(8,128)}, bf16[2,64,128,128]{3,2,1,0:T(8,128)(2,1)}) custom-call(s32[8]{0:T(128)S(1)} %fusion.7.places_ref, bf16[24,128,256]{2,1,0:T(8,128)(2,1)S(1)} %shard_map.96.refs_3_.weight_ref, bf16[4,24,2,16,128]{4,3,2,1,0:T(8,128)(2,1)S(1)} %shard_map.98.refs_0_, ...), custom_call_target="tpu_custom_call" | custom-call | flops 503316480 | bytes 9830400 | tf_op jit(solution)/shard_map/pallas_call | solution.py:290
  107.4 0.0 collective-permute-done.13.refs_2_
  107.4 1.0 collective-permute-done.14.refs_3_
  108.4 4.4 %shard_map.100 = (f32[2,64,16,128]{3,2,1,0:T(8,128)}, bf16[2,64,128,128]{3,2,1,0:T(8,128)(2,1)}) custom-call(s32[8]{0:T(128)S(1)} %fusion.7.places_ref, bf16[40,128,256]{2,1,0:T(8,128)(2,1)S(1)} %shard_map.86.refs_2_.weight_ref, bf16[2,40,2,16,128]{4,3,2,1,0:T(8,128)(2,1)S(1)} %shard_map.95.refs_0_, ...), custom_call_target="tpu_custom_call", output_to_operand_aliasing={{0}: (7, {}), {1}: (8, {})} | custom-call | flops 838860800 | bytes 16384000 | tf_op jit(solution)/shard_map/pallas_call | solution.py:290
  (4 shorter events, 0.1 us)
Async XLA Ops:
  4.9 16.5 %collective-permute-start = (bf16[2,5,2,16,1024]{4,3,2,1,0:T(8,128)(2,1)S(1)}, bf16[2,5,2,16,1024]{4,3,2,1,0:T(8,128)(2,1)S(1)}, u32[]{:S(2)}, u32[]{:S(2)}) collective-permute-start(bf16[2,5,2,16,1024]{4,3,2,1,0:T(8,128)(2,1)S(1)} %get-tuple-element.22), channel_id=1, source_target_pairs={{0,32},{32,64},{64,96},{96,0},{1,33},{33,65},{65,97},{97,1},{2,34}... | collective-permute-start | bytes 1966088 | tf_op jit(solution)/shard_map/ppermute | solution.py:33
  5.4 17.4 %collective-permute-start.1 = (bf16[2,5,2,16,1024]{4,3,2,1,0:T(8,128)(2,1)S(1)}, bf16[2,5,2,16,1024]{4,3,2,1,0:T(8,128)(2,1)S(1)}, u32[]{:S(2)}, u32[]{:S(2)}) collective-permute-start(bf16[2,5,2,16,1024]{4,3,2,1,0:T(8,128)(2,1)S(1)} %get-tuple-element.23), channel_id=1, source_target_pairs={{0,96},{32,0},{64,32},{96,64},{1,97},{33,1},{65,33},{97,65},{2,98}... | collective-permute-start | bytes 1966088 | tf_op jit(solution)/shard_map/ppermute | solution.py:33
  9.5 20.3 %collective-permute-start.5 = (bf16[4,3,2,16,1024]{4,3,2,1,0:T(8,128)(2,1)S(1)}, bf16[4,3,2,16,1024]{4,3,2,1,0:T(8,128)(2,1)S(1)}, u32[]{:S(2)}, u32[]{:S(2)}) collective-permute-start(bf16[4,3,2,16,1024]{4,3,2,1,0:T(8,128)(2,1)S(1)} %get-tuple-element.29), channel_id=1, source_target_pairs={{0,16},{16,0},{1,17},{17,1},{2,18},{18,2},{3,19},{19,3},{4,20},{20... | collective-permute-start | bytes 2359304 | tf_op jit(solution)/shard_map/ppermute | solution.py:37
  22.9 10.1 %collective-permute-start.2 = (bf16[1,5,2,16,1024]{4,3,2,1,0:T(8,128)(2,1)S(1)}, bf16[1,5,2,16,1024]{4,3,2,1,0:T(8,128)(2,1)S(1)}, u32[]{:S(2)}, u32[]{:S(2)}) collective-permute-start(bf16[1,5,2,16,1024]{4,3,2,1,0:T(8,128)(2,1)S(1)} %get-tuple-element.24), channel_id=1, source_target_pairs={{0,32},{32,64},{64,96},{96,0},{1,33},{33,65},{65,97},{97,1},{2,34}... | collective-permute-start | bytes 983048 | tf_op jit(solution)/shard_map/ppermute | solution.py:33
  23.4 9.6 %collective-permute-start.3 = (bf16[1,5,2,16,1024]{4,3,2,1,0:T(8,128)(2,1)S(1)}, bf16[1,5,2,16,1024]{4,3,2,1,0:T(8,128)(2,1)S(1)}, u32[]{:S(2)}, u32[]{:S(2)}) collective-permute-start(bf16[1,5,2,16,1024]{4,3,2,1,0:T(8,128)(2,1)S(1)} %get-tuple-element.25), channel_id=1, source_target_pairs={{0,96},{32,0},{64,32},{96,64},{1,97},{33,1},{65,33},{97,65},{2,98}... | collective-permute-start | bytes 983048 | tf_op jit(solution)/shard_map/ppermute | solution.py:33
  29.8 15.0 %copy-start = (bf16[1024,1024]{1,0:T(8,128)(2,1)S(1)}, bf16[1024,1024]{1,0:T(8,128)(2,1)}, u32[]{:S(2)}) copy-start(bf16[1024,1024]{1,0:T(8,128)(2,1)} %constant.116.clone.sin_ref) | copy-start | bytes 6291460
  29.8 15.0 %copy-start.1 = (bf16[1024,1024]{1,0:T(8,128)(2,1)S(1)}, bf16[1024,1024]{1,0:T(8,128)(2,1)}, u32[]{:S(2)}) copy-start(bf16[1024,1024]{1,0:T(8,128)(2,1)} %constant.115.clone.cos_ref) | copy-start | bytes 6291460
  29.8 15.0 %copy-start.4 = (f32[4,1024]{1,0:T(4,128)S(1)}, f32[4,1024]{1,0:T(4,128)}, u32[]{:S(2)}) copy-start(f32[4,1024]{1,0:T(4,128)} %taps_ref.1) | copy-start | bytes 49156
  30.0 7.5 %collective-permute-start.6 = (bf16[3,2,16,1024]{3,2,1,0:T(8,128)(2,1)S(1)}, bf16[3,2,16,1024]{3,2,1,0:T(8,128)(2,1)S(1)}, u32[]{:S(2)}, u32[]{:S(2)}) collective-permute-start(bf16[3,2,16,1024]{3,2,1,0:T(8,128)(2,1)S(1)} %get-tuple-element.31), channel_id=1, source_target_pairs={{0,32},{32,64},{64,96},{96,0},{1,33},{33,65},{65,97},{97,1},{2,34}... | collective-permute-start | bytes 589832 | tf_op jit(solution)/shard_map/ppermute | solution.py:33
  31.7 8.6 %collective-permute-start.7 = (bf16[3,2,16,1024]{3,2,1,0:T(8,128)(2,1)S(1)}, bf16[3,2,16,1024]{3,2,1,0:T(8,128)(2,1)S(1)}, u32[]{:S(2)}, u32[]{:S(2)}) collective-permute-start(bf16[3,2,16,1024]{3,2,1,0:T(8,128)(2,1)S(1)} %get-tuple-element.32), channel_id=1, source_target_pairs={{0,64},{32,96},{64,0},{96,32},{1,65},{33,97},{65,1},{97,33},{2,66}... | collective-permute-start | bytes 589832 | tf_op jit(solution)/shard_map/ppermute | solution.py:33
  33.0 9.4 %collective-permute-start.8 = (bf16[3,2,16,1024]{3,2,1,0:T(8,128)(2,1)S(1)}, bf16[3,2,16,1024]{3,2,1,0:T(8,128)(2,1)S(1)}, u32[]{:S(2)}, u32[]{:S(2)}) collective-permute-start(bf16[3,2,16,1024]{3,2,1,0:T(8,128)(2,1)S(1)} %get-tuple-element.33), channel_id=1, source_target_pairs={{0,96},{32,0},{64,32},{96,64},{1,97},{33,1},{65,33},{97,65},{2,98}... | collective-permute-start | bytes 589832 | tf_op jit(solution)/shard_map/ppermute | solution.py:33
  33.2 11.6 %collective-permute-start.4 = (bf16[1,5,2,16,1024]{4,3,2,1,0:T(8,128)(2,1)S(1)}, bf16[1,5,2,16,1024]{4,3,2,1,0:T(8,128)(2,1)S(1)}, u32[]{:S(2)}, u32[]{:S(2)}) collective-permute-start(bf16[1,5,2,16,1024]{4,3,2,1,0:T(8,128)(2,1)S(1)} %get-tuple-element.27), channel_id=1, source_target_pairs={{0,16},{16,0},{1,17},{17,1},{2,18},{18,2},{3,19},{19,3},{4,20},{20... | collective-permute-start | bytes 983048 | tf_op jit(solution)/shard_map/ppermute | solution.py:37
  42.5 2.4 %collective-permute-start.9 = (bf16[3,2,16,1024]{3,2,1,0:T(8,128)(2,1)S(1)}, bf16[3,2,16,1024]{3,2,1,0:T(8,128)(2,1)S(1)}, u32[]{:S(2)}, u32[]{:S(2)}) collective-permute-start(bf16[3,2,16,1024]{3,2,1,0:T(8,128)(2,1)S(1)} %shard_map.92.late_ref), channel_id=1, source_target_pairs={{0,1},{1,2},{2,3},{3,4},{4,5},{5,6},{6,7},{7,8},{8,9},{9,10},{10,1... | collective-permute-start | bytes 589832 | tf_op jit(solution)/shard_map/ppermute | solution.py:375
  68.7 10.5 %collective-permute-start.10 = (bf16[40,2,16,128]{3,2,1,0:T(8,128)(2,1)S(1)}, bf16[40,2,16,128]{3,2,1,0:T(8,128)(2,1)S(1)}, u32[]{:S(2)}, u32[]{:S(2)}) collective-permute-start(bf16[40,2,16,128]{3,2,1,0:T(8,128)(2,1)S(1)} %get-tuple-element.34.refs_0_), channel_id=1, source_target_pairs={{0,16},{16,0},{1,17},{17,1},{2,18},{18,2},{3,19},{19,3},{4,20},{20... | collective-permute-start | bytes 983048 | tf_op jit(solution)/shard_map/ppermute | solution.py:37
  71.7 9.7 %collective-permute-start.17 = (bf16[24,2,16,128]{3,2,1,0:T(8,128)(2,1)S(1)}, bf16[24,2,16,128]{3,2,1,0:T(8,128)(2,1)S(1)}, u32[]{:S(2)}, u32[]{:S(2)}) collective-permute-start(bf16[24,2,16,128]{3,2,1,0:T(8,128)(2,1)S(1)} %get-tuple-element.37.refs_0_), channel_id=1, source_target_pairs={{0,32},{32,64},{64,96},{96,0},{1,33},{33,65},{65,97},{97,1},{2,34}... | collective-permute-start | bytes 589832 | tf_op jit(solution)/shard_map/ppermute | solution.py:33
  72.3 9.3 %collective-permute-start.16 = (bf16[24,2,16,128]{3,2,1,0:T(8,128)(2,1)S(1)}, bf16[24,2,16,128]{3,2,1,0:T(8,128)(2,1)S(1)}, u32[]{:S(2)}, u32[]{:S(2)}) collective-permute-start(bf16[24,2,16,128]{3,2,1,0:T(8,128)(2,1)S(1)} %get-tuple-element.37.refs_0_), channel_id=1, source_target_pairs={{0,64},{32,96},{64,0},{96,32},{1,65},{33,97},{65,1},{97,33},{2,66}... | collective-permute-start | bytes 589832 | tf_op jit(solution)/shard_map/ppermute | solution.py:33
  73.5 10.7 %collective-permute-start.15 = (bf16[24,2,16,128]{3,2,1,0:T(8,128)(2,1)S(1)}, bf16[24,2,16,128]{3,2,1,0:T(8,128)(2,1)S(1)}, u32[]{:S(2)}, u32[]{:S(2)}) collective-permute-start(bf16[24,2,16,128]{3,2,1,0:T(8,128)(2,1)S(1)} %get-tuple-element.37.refs_0_), channel_id=1, source_target_pairs={{0,96},{32,0},{64,32},{96,64},{1,97},{33,1},{65,33},{97,65},{2,98}... | collective-permute-start | bytes 589832 | tf_op jit(solution)/shard_map/ppermute | solution.py:33
  79.3 16.5 %collective-permute-start.12 = (bf16[2,40,2,16,128]{4,3,2,1,0:T(8,128)(2,1)S(1)}, bf16[2,40,2,16,128]{4,3,2,1,0:T(8,128)(2,1)S(1)}, u32[]{:S(2)}, u32[]{:S(2)}) collective-permute-start(bf16[2,40,2,16,128]{4,3,2,1,0:T(8,128)(2,1)S(1)} %shard_map.95.refs_0_), channel_id=1, source_target_pairs={{0,32},{32,64},{64,96},{96,0},{1,33},{33,65},{65,97},{97,1},{2,34}... | collective-permute-start | bytes 1966088 | tf_op jit(solution)/shard_map/ppermute | solution.py:33
  79.9 17.7 %collective-permute-start.11 = (bf16[2,40,2,16,128]{4,3,2,1,0:T(8,128)(2,1)S(1)}, bf16[2,40,2,16,128]{4,3,2,1,0:T(8,128)(2,1)S(1)}, u32[]{:S(2)}, u32[]{:S(2)}) collective-permute-start(bf16[2,40,2,16,128]{4,3,2,1,0:T(8,128)(2,1)S(1)} %shard_map.95.refs_0_), channel_id=1, source_target_pairs={{0,96},{32,0},{64,32},{96,64},{1,97},{33,1},{65,33},{97,65},{2,98}... | collective-permute-start | bytes 1966088 | tf_op jit(solution)/shard_map/ppermute | solution.py:33
  84.3 19.9 %collective-permute-start.18 = (bf16[4,24,2,16,128]{4,3,2,1,0:T(8,128)(2,1)S(1)}, bf16[4,24,2,16,128]{4,3,2,1,0:T(8,128)(2,1)S(1)}, u32[]{:S(2)}, u32[]{:S(2)}) collective-permute-start(bf16[4,24,2,16,128]{4,3,2,1,0:T(8,128)(2,1)S(1)} %shard_map.98.refs_0_), channel_id=1, source_target_pairs={{0,16},{16,0},{1,17},{17,1},{2,18},{18,2},{3,19},{19,3},{4,20},{20... | collective-permute-start | bytes 2359304 | tf_op jit(solution)/shard_map/ppermute | solution.py:37
  84.5 0.8 copy-start.2
  87.4 0.8 copy-start.3
  97.7 9.7 %collective-permute-start.13 = (bf16[1,40,2,16,128]{4,3,2,1,0:T(8,128)(2,1)S(1)}, bf16[1,40,2,16,128]{4,3,2,1,0:T(8,128)(2,1)S(1)}, u32[]{:S(2)}, u32[]{:S(2)}) collective-permute-start(bf16[1,40,2,16,128]{4,3,2,1,0:T(8,128)(2,1)S(1)} %get-tuple-element.35), channel_id=1, source_target_pairs={{0,32},{32,64},{64,96},{96,0},{1,33},{33,65},{65,97},{97,1},{2,34}... | collective-permute-start | bytes 983048 | tf_op jit(solution)/shard_map/ppermute | solution.py:33
  98.6 9.8 %collective-permute-start.14 = (bf16[1,40,2,16,128]{4,3,2,1,0:T(8,128)(2,1)S(1)}, bf16[1,40,2,16,128]{4,3,2,1,0:T(8,128)(2,1)S(1)}, u32[]{:S(2)}, u32[]{:S(2)}) collective-permute-start(bf16[1,40,2,16,128]{4,3,2,1,0:T(8,128)(2,1)S(1)} %get-tuple-element.36), channel_id=1, source_target_pairs={{0,96},{32,0},{64,32},{96,64},{1,97},{33,1},{65,33},{97,65},{2,98}... | collective-permute-start | bytes 983048 | tf_op jit(solution)/shard_map/ppermute | solution.py:33

commit v5 on v4

--- a/solution.py
+++ b/solution.py
@@ -24,7 +24,7 @@
 LATE = 3
 EARLY = LOCAL_FRAMES - LATE
 LOCAL_CHANS = 64
-FIRST = 40
+FIRST = 44
 BF16 = jnp.bfloat16
 F32 = jnp.float32
 
@@ -242,13 +242,18 @@
             for z in range(2)
         ]
 
-    @pl.loop(0, steps)
-    def _(step):
+    def load(pieces, part, here):
+        array, index = pieces[part % len(pieces)]
+        if len(pieces) > 1:
+            here = here - part * (steps // 2) * each
+        return [block_refs[array][(*index, here, z)] for z in range(2)]
+
+    def work(part, step):
         for c in range(each):
             here = step * each + c
-            for place, (array, index) in enumerate(blocks):
+            for place, pieces in enumerate(blocks):
                 row = pl.multiple_of(places_ref[place] * PER, PER)
-                real, quad = block_refs[array][index, here, 0], block_refs[array][index, here, 1]
+                real, quad = load(pieces, part, here)
                 both_ref[c, pl.ds(row, PER), 0:128] = real
                 both_ref[c, pl.ds(row, PER), 128:256] = quad
                 both_ref[c, pl.ds(TILES + row, PER), 0:128] = quad
@@ -258,8 +263,7 @@
             beams = jnp.dot(weight_ref[here], both_ref[c], preferred_element_type=F32) * beam_scale
             beam_out[0, here] = beams[:, 0:128].astype(BF16)
             beam_out[1, here] = beams[:, 128:256].astype(BF16)
-            array, index = blocks[0]
-            real, quad = block_refs[array][index, here, 0], block_refs[array][index, here, 1]
+            real, quad = load(blocks[0], part, here)
             mine = jnp.concatenate(
                 [jnp.concatenate([real, quad], axis=1), jnp.concatenate([quad, -real], axis=1)], axis=0
             )
@@ -269,6 +273,9 @@
         for copy in copies(step):
             copy.start()
 
+    pl.loop(0, steps // 2)(functools.partial(work, 0))
+    pl.loop(steps // 2, steps)(functools.partial(work, 1))
+
     @pl.loop(0, steps)
     def _(step):
         for copy in copies(step):
@@ -277,12 +284,14 @@
 
 def products(places, weights, begin, blocks, results=()):
     arrays, layout = [], []
-    for array, index in blocks:
-        if not any(array is a for a in arrays):
-            arrays.append(array)
-        layout.append((next(n for n, a in enumerate(arrays) if a is array), index))
+    for pieces in blocks:
+        layout.append([])
+        for array, index in pieces:
+            if not any(array is a for a in arrays):
+                arrays.append(array)
+            layout[-1].append((next(n for n, a in enumerate(arrays) if a is array), index))
     count, beams = weights.shape[:2]
-    each = next(n for n in (10, 8) if count % n == 0)
+    each = next(n for n in (11, 10) if count % n == 0)
 
     def kernel(places_ref, weight_ref, *refs):
         products_kernel(begin, layout, places_ref, weight_ref, refs[: len(arrays)], *refs[len(arrays) + len(results) :])
@@ -336,18 +345,23 @@
 
 
 def gather_sections(first, second, others):
-    (both,) = combine((first, pair(first)), ([[(0, slice(None))], [(1, slice(None))]],))
-    both_minus, both_plus = ring(both, 1), ring(both, -1)
-    own_far, pair_far = combine((both_minus, both_plus), ([[(0, 0)]], [[(1, 1)]]), others)
-    own_far, pair_far = ring(own_far, 1), ring(pair_far, -1)
-    firsts = ((both, 0), (both, 1), (both_plus, 0), (both_plus, 1))
-    firsts += ((own_far, 0), (pair_far, 0), (both_minus, 0), (both_minus, 1))
+    half = first.shape[0] // 2
+    low, high = slice(0, half), slice(half, None)
+    own = [ring(first, by) for by in (1, -1)]
+    first_pair = pair(first)
+    pairs = [ring(first_pair, by) for by in (1, -1)]
+    far = []
+    for minus, plus, needed in (own + [()], pairs + [others]):
+        parts = combine((minus, plus), ([[(0, n)] for n in range(half)], [[(1, half + n)] for n in range(half)]), needed)
+        far.append((ring(parts[0], 1), ring(parts[1], -1)))
+    firsts = [(first,), (first_pair,), (own[1],), (pairs[1],), far[0], far[1], (own[0],), (pairs[0],)]
+    firsts = [[(v, ()) for v in pieces] for pieces in firsts]
 
     (mine,) = combine(
         (second, ring(second, -1), ring(second, 2), ring(second, 1)), ([[(n, slice(None))] for n in range(NX)],)
     )
     theirs = pair(mine)
-    seconds = tuple((v, n) for n in range(NX) for v in (mine, theirs))
+    seconds = [[(v, (n,))] for n in range(NX) for v in (mine, theirs)]
     return firsts, seconds
 
 

time: 113 us -> 116 us (1.027)
  starting transfers between devices: 25 us -> 29.8 us
  local copies, waits for them, and re-layouts: 1.68 us -> 0.02 us
    ppermute x4, waiting for transfers between devices: 14.1 us -> 4.85 us  [pair(): return lax.ppermute(v, 'yh', [(0, 1), (1, 0)])]
    ppermute x14 -> x18, waiting for transfers between devices: 25.4 us -> 34.1 us  [ring(): return lax.ppermute(v, 'x', [(i, (i + by) % NX) for i in range(NX)])]
    ppermute x14 -> x18, starting transfers between devices: 14 us -> 18.3 us  [ring(): return lax.ppermute(v, 'x', [(i, (i + by) % NX) for i in range(NX)])]
    unnamed x10 -> x8, local copies, waits for them, and re-layouts: 1.68 us -> 0.02 us
  transfers between devices with their start and end apart: 19 -> 23, of which waited for: 14 -> 16; matrix products, arithmetic and copies ran while one was open for 0% -> 0% of each run, Pallas kernels for 11% -> 10%
where the time goes in v5:
time: 116 us; the launch traced here: 115 us
  waiting for transfers between devices  40 us (34%)
  starting transfers between devices  29.8 us (26%)
  Pallas kernels  21.9 us (19%)
  blocking collectives  21.9 us (19%)
    ppermute x18, waiting for transfers between devices, ring(): return lax.ppermute(v, 'x', [(i, (i + by) % NX) for i in range(NX)])  34.1 us
    all_to_all x1, blocking collectives, local(): first, second = turn(lax.all_to_all(spec, DEV, 0, 0, tiled=True))  21.9 us
    ppermute x18, starting transfers between devices, ring(): return lax.ppermute(v, 'x', [(i, (i + by) % NX) for i in range(NX)])  18.3 us
    ppermute x4, starting transfers between devices, pair(): return lax.ppermute(v, 'yh', [(0, 1), (1, 0)])  10.2 us
    pallas_call x2, Pallas kernels, products(): pl.pallas_call(kernel, in_specs=[IN_SMEM] + [IN_VMEM] * (1 + len(arrays))...  7.28 us
    pallas_call x2, Pallas kernels, tile_sums(): pl.pallas_call(functools.partial(tile_sums_kernel, first, frames, groups)...  6.03 us
    pallas_call x2, Pallas kernels, beam_weights(): pl.pallas_call(weights_kernel, in_specs=[IN_SMEM, IN_VMEM], out_specs=IN_...  5.69 us
    ppermute x4, waiting for transfers between devices, pair(): return lax.ppermute(v, 'yh', [(0, 1), (1, 0)])  4.85 us
  transfers between devices with their start and end apart: 23, of which 16 were waited for; matrix products, arithmetic and copies ran while one was open for 0% of the time, Pallas kernels for 10%

profile of v5, /device:TPU:6, one launch (start us, length us, event | category | flops | bytes accessed | tf_op | source)
XLA Modules:
  0.0 115.4 jit_solution(7156412669618608555)
XLA Ops:
  0.6 0.7 compare_select_fusion.4
  1.4 3.5 %shard_map.87 = (bf16[2,5,2,16,1024]{4,3,2,1,0:T(8,128)(2,1)S(1)}, bf16[2,5,2,16,1024]{4,3,2,1,0:T(8,128)(2,1)S(1)}, bf16[4,5,2,16,1024]{4,3,2,1,0:T(8,128)(2,1)S(1)}) custom-call(bf16[128,256]{1,0:T(8,128)(2,1)S(1)} %fusion.member_ref, bf16[2,256,8192]{2,1,0:T(8,128)(2,1)} %volts_ref.3), custom_call_target="tpu_custom_call" | custom-call | flops 671088640 | bytes 15728640 | tf_op jit(solution)/shard_map/pallas_call | solution.py:102
  4.9 0.5 collective-permute-start
  5.4 1.6 %collective-permute-start.1 = (bf16[2,5,2,16,1024]{4,3,2,1,0:T(8,128)(2,1)S(1)}, bf16[2,5,2,16,1024]{4,3,2,1,0:T(8,128)(2,1)S(1)}, u32[]{:S(2)}, u32[]{:S(2)}) collective-permute-start(bf16[2,5,2,16,1024]{4,3,2,1,0:T(8,128)(2,1)S(1)} %get-tuple-element.25), channel_id=1, source_target_pairs={{0,96},{32,0},{64,32},{96,64},{1,97},{33,1},{65,33},{97,65},{2,98}... | collective-permute-start | bytes 1966088 | tf_op jit(solution)/shard_map/ppermute | solution.py:33
  7.0 2.5 %shard_map.90 = (bf16[4,3,2,16,1024]{4,3,2,1,0:T(8,128)(2,1)S(1)}, bf16[4,3,2,16,1024]{4,3,2,1,0:T(8,128)(2,1)S(1)}) custom-call(bf16[128,256]{1,0:T(8,128)(2,1)S(1)} %fusion.member_ref, bf16[2,256,8192]{2,1,0:T(8,128)(2,1)} %volts_ref.3, bf16[4,5,2,16,1024]{4,3,2,1,0:T(8,128)(2,1)S(1)} %get-tuple-element.23.refs_0_), custom_call_target="tpu_custom_call" | custom-call | flops 402653184 | bytes 9437184 | tf_op jit(solution)/shard_map/pallas_call | solution.py:102
  9.5 3.3 %collective-permute-start.5 = (bf16[4,3,2,16,1024]{4,3,2,1,0:T(8,128)(2,1)S(1)}, bf16[4,3,2,16,1024]{4,3,2,1,0:T(8,128)(2,1)S(1)}, u32[]{:S(2)}, u32[]{:S(2)}) collective-permute-start(bf16[4,3,2,16,1024]{4,3,2,1,0:T(8,128)(2,1)S(1)} %get-tuple-element.31), channel_id=1, source_target_pairs={{0,16},{16,0},{1,17},{17,1},{2,18},{18,2},{3,19},{19,3},{4,20},{20... | collective-permute-start | bytes 2359304 | tf_op jit(solution)/shard_map/ppermute | solution.py:37
  12.8 8.6 %collective-permute-done.refs_1_.refs_3_ = bf16[2,5,2,16,1024]{4,3,2,1,0:T(8,128)(2,1)S(1)} collective-permute-done((bf16[2,5,2,16,1024]{4,3,2,1,0:T(8,128)(2,1)S(1)}, bf16[2,5,2,16,1024]{4,3,2,1,0:T(8,128)(2,1)S(1)}, u32[]{:S(2)}, u32[]{:S(2)}) %collective-permute-start) | collective-permute-done | bytes 655392 | tf_op jit(solution)/shard_map/ppermute | solution.py:33
  21.4 1.3 %collective-permute-done.1.refs_2_.refs_4_ = bf16[2,5,2,16,1024]{4,3,2,1,0:T(8,128)(2,1)S(1)} collective-permute-done((bf16[2,5,2,16,1024]{4,3,2,1,0:T(8,128)(2,1)S(1)}, bf16[2,5,2,16,1024]{4,3,2,1,0:T(8,128)(2,1)S(1)}, u32[]{:S(2)}, u32[]{:S(2)}) %collective-permute-start.1) | collective-permute-done | bytes 655392 | tf_op jit(solution)/shard_map/ppermute | solution.py:33
  22.7 0.2 shard_map.88
  22.9 0.5 collective-permute-start.2
  23.4 1.6 %collective-permute-start.3 = (bf16[1,5,2,16,1024]{4,3,2,1,0:T(8,128)(2,1)S(1)}, bf16[1,5,2,16,1024]{4,3,2,1,0:T(8,128)(2,1)S(1)}, u32[]{:S(2)}, u32[]{:S(2)}) collective-permute-start(bf16[1,5,2,16,1024]{4,3,2,1,0:T(8,128)(2,1)S(1)} %get-tuple-element.27), channel_id=1, source_target_pairs={{0,96},{32,0},{64,32},{96,64},{1,97},{33,1},{65,33},{97,65},{2,98}... | collective-permute-start | bytes 983048 | tf_op jit(solution)/shard_map/ppermute | solution.py:33
  25.0 4.8 %collective-permute-done.5.refs_1_ = bf16[4,3,2,16,1024]{4,3,2,1,0:T(8,128)(2,1)S(1)} collective-permute-done((bf16[4,3,2,16,1024]{4,3,2,1,0:T(8,128)(2,1)S(1)}, bf16[4,3,2,16,1024]{4,3,2,1,0:T(8,128)(2,1)S(1)}, u32[]{:S(2)}, u32[]{:S(2)}) %collective-permute-start.5) | collective-permute-done | bytes 786464 | tf_op jit(solution)/shard_map/ppermute | solution.py:37
  29.8 0.2 shard_map.91
  30.0 1.7 %collective-permute-start.6 = (bf16[3,2,16,1024]{3,2,1,0:T(8,128)(2,1)S(1)}, bf16[3,2,16,1024]{3,2,1,0:T(8,128)(2,1)S(1)}, u32[]{:S(2)}, u32[]{:S(2)}) collective-permute-start(bf16[3,2,16,1024]{3,2,1,0:T(8,128)(2,1)S(1)} %get-tuple-element.33), channel_id=1, source_target_pairs={{0,32},{32,64},{64,96},{96,0},{1,33},{33,65},{65,97},{97,1},{2,34}... | collective-permute-start | bytes 589832 | tf_op jit(solution)/shard_map/ppermute | solution.py:33
  31.7 1.3 %collective-permute-start.7 = (bf16[3,2,16,1024]{3,2,1,0:T(8,128)(2,1)S(1)}, bf16[3,2,16,1024]{3,2,1,0:T(8,128)(2,1)S(1)}, u32[]{:S(2)}, u32[]{:S(2)}) collective-permute-start(bf16[3,2,16,1024]{3,2,1,0:T(8,128)(2,1)S(1)} %get-tuple-element.34), channel_id=1, source_target_pairs={{0,64},{32,96},{64,0},{96,32},{1,65},{33,97},{65,1},{97,33},{2,66}... | collective-permute-start | bytes 589832 | tf_op jit(solution)/shard_map/ppermute | solution.py:33
  33.0 0.0 collective-permute-start.8
  33.0 0.0 collective-permute-done.2.refs_1_
  33.0 0.0 collective-permute-done.3.refs_2_
  33.0 0.2 shard_map.89
  33.2 3.3 %collective-permute-start.4 = (bf16[1,5,2,16,1024]{4,3,2,1,0:T(8,128)(2,1)S(1)}, bf16[1,5,2,16,1024]{4,3,2,1,0:T(8,128)(2,1)S(1)}, u32[]{:S(2)}, u32[]{:S(2)}) collective-permute-start(bf16[1,5,2,16,1024]{4,3,2,1,0:T(8,128)(2,1)S(1)} %get-tuple-element.29), channel_id=1, source_target_pairs={{0,16},{16,0},{1,17},{17,1},{2,18},{18,2},{3,19},{19,3},{4,20},{20... | collective-permute-start | bytes 983048 | tf_op jit(solution)/shard_map/ppermute | solution.py:37
  36.5 1.0 collective-permute-done.6.refs_1_
  37.5 2.8 %collective-permute-done.7.refs_2_ = bf16[3,2,16,1024]{3,2,1,0:T(8,128)(2,1)S(1)} collective-permute-done((bf16[3,2,16,1024]{3,2,1,0:T(8,128)(2,1)S(1)}, bf16[3,2,16,1024]{3,2,1,0:T(8,128)(2,1)S(1)}, u32[]{:S(2)}, u32[]{:S(2)}) %collective-permute-start.7) | collective-permute-done | bytes 196640 | tf_op jit(solution)/shard_map/ppermute | solution.py:33
  40.3 2.0 %collective-permute-done.8.refs_3_ = bf16[3,2,16,1024]{3,2,1,0:T(8,128)(2,1)S(1)} collective-permute-done((bf16[3,2,16,1024]{3,2,1,0:T(8,128)(2,1)S(1)}, bf16[3,2,16,1024]{3,2,1,0:T(8,128)(2,1)S(1)}, u32[]{:S(2)}, u32[]{:S(2)}) %collective-permute-start.8) | collective-permute-done | bytes 196640 | tf_op jit(solution)/shard_map/ppermute | solution.py:33
  42.4 0.1 shard_map.92.late_ref
  42.5 1.3 %collective-permute-start.9 = (bf16[3,2,16,1024]{3,2,1,0:T(8,128)(2,1)S(1)}, bf16[3,2,16,1024]{3,2,1,0:T(8,128)(2,1)S(1)}, u32[]{:S(2)}, u32[]{:S(2)}) collective-permute-start(bf16[3,2,16,1024]{3,2,1,0:T(8,128)(2,1)S(1)} %shard_map.92.late_ref), channel_id=1, source_target_pairs={{0,1},{1,2},{2,3},{3,4},{4,5},{5,6},{6,7},{7,8},{8,9},{9,10},{10,1... | collective-permute-start | bytes 589832 | tf_op jit(solution)/shard_map/ppermute | solution.py:389
  43.8 1.0 collective-permute-done.9.past_ref
  44.8 0.0 collective-permute-done.4.got_ref
  44.8 0.0 copy-done
  44.8 0.0 copy-done.1
  44.8 0.0 copy-done.3
  44.8 1.4 %shard_map.93 = bf16[16,128,128]{2,1,0:T(8,128)(2,1)S(1)} custom-call(bf16[1,5,2,16,1024]{4,3,2,1,0:T(8,128)(2,1)S(1)} %get-tuple-element.28.own_ref, bf16[1,5,2,16,1024]{4,3,2,1,0:T(8,128)(2,1)S(1)} %collective-permute-done.4.got_ref, bf16[3,2,16,1024]{3,2,1,0:T(8,128)(2,1)S(1)} %shard_map.92.late_ref, ...), custom_call_target="tpu_custom_call" | custom-call | flops 1073741824 | bytes 6291456 | tf_op jit(solution)/shard_map/pallas_call | solution.py:193
  46.3 0.0 copy-start.2
  46.3 21.9 %all_to_all.5.in_ref = bf16[16,128,128]{2,1,0:T(8,128)(2,1)S(1)} all-to-all(bf16[16,128,128]{2,1,0:T(8,128)(2,1)S(1)} %shard_map.93), channel_id=1, replica_groups=mesh['x'=4,'yh'=2,'yl'=2,'z'=4,'core'=2] {'yl','z','core'}, dimensions={0} | all-to-all | bytes 1048576 | tf_op jit(solution)/shard_map/all_to_all | solution.py:391
  68.2 0.7 shard_map.94
  68.9 3.0 %collective-permute-start.10 = (bf16[44,2,16,128]{3,2,1,0:T(8,128)(2,1)S(1)}, bf16[44,2,16,128]{3,2,1,0:T(8,128)(2,1)S(1)}, u32[]{:S(2)}, u32[]{:S(2)}) collective-permute-start(bf16[44,2,16,128]{3,2,1,0:T(8,128)(2,1)S(1)} %get-tuple-element.36.refs_0_), channel_id=1, source_target_pairs={{0,16},{16,0},{1,17},{17,1},{2,18},{18,2},{3,19},{19,3},{4,20},{20... | collective-permute-start | bytes 1081352 | tf_op jit(solution)/shard_map/ppermute | solution.py:37
  71.8 0.6 collective-permute-start.21
  72.4 1.2 %collective-permute-start.20 = (bf16[20,2,16,128]{3,2,1,0:T(8,128)(2,1)S(1)}, bf16[20,2,16,128]{3,2,1,0:T(8,128)(2,1)S(1)}, u32[]{:S(2)}, u32[]{:S(2)}) collective-permute-start(bf16[20,2,16,128]{3,2,1,0:T(8,128)(2,1)S(1)} %get-tuple-element.41.refs_0_), channel_id=1, source_target_pairs={{0,64},{32,96},{64,0},{96,32},{1,65},{33,97},{65,1},{97,33},{2,66}... | collective-permute-start | bytes 491528 | tf_op jit(solution)/shard_map/ppermute | solution.py:33
  73.6 0.8 collective-permute-start.19
  74.5 4.3 %collective-permute-done.21.refs_3_ = bf16[20,2,16,128]{3,2,1,0:T(8,128)(2,1)S(1)} collective-permute-done((bf16[20,2,16,128]{3,2,1,0:T(8,128)(2,1)S(1)}, bf16[20,2,16,128]{3,2,1,0:T(8,128)(2,1)S(1)}, u32[]{:S(2)}, u32[]{:S(2)}) %collective-permute-start.21) | collective-permute-done | bytes 163872 | tf_op jit(solution)/shard_map/ppermute | solution.py:33
  78.8 1.9 %collective-permute-done.20.refs_2_ = bf16[20,2,16,128]{3,2,1,0:T(8,128)(2,1)S(1)} collective-permute-done((bf16[20,2,16,128]{3,2,1,0:T(8,128)(2,1)S(1)}, bf16[20,2,16,128]{3,2,1,0:T(8,128)(2,1)S(1)}, u32[]{:S(2)}, u32[]{:S(2)}) %collective-permute-start.20) | collective-permute-done | bytes 163872 | tf_op jit(solution)/shard_map/ppermute | solution.py:33
  80.6 1.7 %collective-permute-done.19.refs_1_ = bf16[20,2,16,128]{3,2,1,0:T(8,128)(2,1)S(1)} collective-permute-done((bf16[20,2,16,128]{3,2,1,0:T(8,128)(2,1)S(1)}, bf16[20,2,16,128]{3,2,1,0:T(8,128)(2,1)S(1)}, u32[]{:S(2)}, u32[]{:S(2)}) %collective-permute-start.19) | collective-permute-done | bytes 163872 | tf_op jit(solution)/shard_map/ppermute | solution.py:33
  82.3 0.7 collective-permute-start.22
  83.1 0.9 collective-permute-start.13
  83.9 1.2 %collective-permute-start.11 = (bf16[44,2,16,128]{3,2,1,0:T(8,128)(2,1)S(1)}, bf16[44,2,16,128]{3,2,1,0:T(8,128)(2,1)S(1)}, u32[]{:S(2)}, u32[]{:S(2)}) collective-permute-start(bf16[44,2,16,128]{3,2,1,0:T(8,128)(2,1)S(1)} %get-tuple-element.36.refs_0_), channel_id=1, source_target_pairs={{0,96},{32,0},{64,32},{96,64},{1,97},{33,1},{65,33},{97,65},{2,98}... | collective-permute-start | bytes 1081352 | tf_op jit(solution)/shard_map/ppermute | solution.py:33
  85.1 0.0 collective-permute-done.10.refs_1_
  85.1 2.1 %collective-permute-start.16 = (bf16[44,2,16,128]{3,2,1,0:T(8,128)(2,1)S(1)}, bf16[44,2,16,128]{3,2,1,0:T(8,128)(2,1)S(1)}, u32[]{:S(2)}, u32[]{:S(2)}) collective-permute-start(bf16[44,2,16,128]{3,2,1,0:T(8,128)(2,1)S(1)} %collective-permute-done.10.refs_1_), channel_id=1, source_target_pairs={{0,32},{32,64},{64,96},{96,0},{1,33},{33,65},{65,97},{97,1},{2,34}... | collective-permute-start | bytes 1081352 | tf_op jit(solution)/shard_map/ppermute | solution.py:33
  87.2 0.0 collective-permute-start.12
  87.2 1.8 %shard_map.96.refs_3_.weight_ref = bf16[20,128,256]{2,1,0:T(8,128)(2,1)S(1)} custom-call(s32[1]{0:T(128)} %bitcast.1.base_ref, f32[128,128]{1,0:T(8,128)S(1)} %copy-done.2), custom_call_target="tpu_custom_call" | custom-call | flops 1000 | bytes 8192000 | tf_op jit(solution)/shard_map/pallas_call | solution.py:147
  89.0 3.9 %shard_map.86.refs_2_.weight_ref = bf16[44,128,256]{2,1,0:T(8,128)(2,1)S(1)} custom-call(s32[1]{0:T(128)} %bitcast.base_ref, f32[128,128]{1,0:T(8,128)S(1)} %copy-done.2), custom_call_target="tpu_custom_call" | custom-call | flops 1000 | bytes 18022400 | tf_op jit(solution)/shard_map/pallas_call | solution.py:147
  92.9 1.5 %collective-permute-done.13.refs_0_.refs_8_ = bf16[44,2,16,128]{3,2,1,0:T(8,128)(2,1)S(1)} collective-permute-done((bf16[44,2,16,128]{3,2,1,0:T(8,128)(2,1)S(1)}, bf16[44,2,16,128]{3,2,1,0:T(8,128)(2,1)S(1)}, u32[]{:S(2)}, u32[]{:S(2)}) %collective-permute-start.13) | collective-permute-done | bytes 360480 | tf_op jit(solution)/shard_map/ppermute | solution.py:33
  94.4 2.1 %collective-permute-done.11.refs_1_.refs_2_ = bf16[44,2,16,128]{3,2,1,0:T(8,128)(2,1)S(1)} collective-permute-done((bf16[44,2,16,128]{3,2,1,0:T(8,128)(2,1)S(1)}, bf16[44,2,16,128]{3,2,1,0:T(8,128)(2,1)S(1)}, u32[]{:S(2)}, u32[]{:S(2)}) %collective-permute-start.11) | collective-permute-done | bytes 360480 | tf_op jit(solution)/shard_map/ppermute | solution.py:33
  96.5 0.3 collective-permute-start.14
  96.8 2.0 %collective-permute-start.15 = (bf16[22,2,16,128]{3,2,1,0:T(8,128)(2,1)S(1)}, bf16[22,2,16,128]{3,2,1,0:T(8,128)(2,1)S(1)}, u32[]{:S(2)}, u32[]{:S(2)}) collective-permute-start(bf16[22,2,16,128]{3,2,1,0:T(8,128)(2,1)S(1)} %get-tuple-element.38), channel_id=1, source_target_pairs={{0,96},{32,0},{64,32},{96,64},{1,97},{33,1},{65,33},{97,65},{2,98}... | collective-permute-start | bytes 540680 | tf_op jit(solution)/shard_map/ppermute | solution.py:33
  98.8 3.3 %collective-permute-done.16.refs_0_.refs_9_ = bf16[44,2,16,128]{3,2,1,0:T(8,128)(2,1)S(1)} collective-permute-done((bf16[44,2,16,128]{3,2,1,0:T(8,128)(2,1)S(1)}, bf16[44,2,16,128]{3,2,1,0:T(8,128)(2,1)S(1)}, u32[]{:S(2)}, u32[]{:S(2)}) %collective-permute-start.16) | collective-permute-done | bytes 360480 | tf_op jit(solution)/shard_map/ppermute | solution.py:33
  102.2 1.3 %collective-permute-done.12.refs_1_.refs_3_ = bf16[44,2,16,128]{3,2,1,0:T(8,128)(2,1)S(1)} collective-permute-done((bf16[44,2,16,128]{3,2,1,0:T(8,128)(2,1)S(1)}, bf16[44,2,16,128]{3,2,1,0:T(8,128)(2,1)S(1)}, u32[]{:S(2)}, u32[]{:S(2)}) %collective-permute-start.12) | collective-permute-done | bytes 360480 | tf_op jit(solution)/shard_map/ppermute | solution.py:33
  103.5 0.4 collective-permute-start.17
  103.9 1.7 %collective-permute-start.18 = (bf16[22,2,16,128]{3,2,1,0:T(8,128)(2,1)S(1)}, bf16[22,2,16,128]{3,2,1,0:T(8,128)(2,1)S(1)}, u32[]{:S(2)}, u32[]{:S(2)}) collective-permute-start(bf16[22,2,16,128]{3,2,1,0:T(8,128)(2,1)S(1)} %get-tuple-element.40), channel_id=1, source_target_pairs={{0,96},{32,0},{64,32},{96,64},{1,97},{33,1},{65,33},{97,65},{2,98}... | collective-permute-start | bytes 540680 | tf_op jit(solution)/shard_map/ppermute | solution.py:33
  105.6 0.0 collective-permute-done.22.refs_1_
  105.6 2.7 %shard_map.99 = (f32[2,64,16,128]{3,2,1,0:T(8,128)}, bf16[2,64,128,128]{3,2,1,0:T(8,128)(2,1)}) custom-call(s32[8]{0:T(128)S(1)} %fusion.7.places_ref, bf16[20,128,256]{2,1,0:T(8,128)(2,1)S(1)} %shard_map.96.refs_3_.weight_ref, bf16[4,20,2,16,128]{4,3,2,1,0:T(8,128)(2,1)S(1)} %shard_map.98.refs_0_, ...), custom_call_target="tpu_custom_call" | custom-call | flops 419430400 | bytes 8192000 | tf_op jit(solution)/shard_map/pallas_call | solution.py:299
  108.3 0.0 collective-permute-done.14.refs_4_
  108.3 0.0 collective-permute-done.15.refs_5_
  108.3 0.7 collective-permute-done.17.refs_6_
  109.0 1.6 %collective-permute-done.18.refs_7_ = bf16[22,2,16,128]{3,2,1,0:T(8,128)(2,1)S(1)} collective-permute-done((bf16[22,2,16,128]{3,2,1,0:T(8,128)(2,1)S(1)}, bf16[22,2,16,128]{3,2,1,0:T(8,128)(2,1)S(1)}, u32[]{:S(2)}, u32[]{:S(2)}) %collective-permute-start.18) | collective-permute-done | bytes 180256 | tf_op jit(solution)/shard_map/ppermute | solution.py:33
  110.6 4.6 %shard_map.100 = (f32[2,64,16,128]{3,2,1,0:T(8,128)}, bf16[2,64,128,128]{3,2,1,0:T(8,128)(2,1)}) custom-call(s32[8]{0:T(128)S(1)} %fusion.7.places_ref, bf16[44,128,256]{2,1,0:T(8,128)(2,1)S(1)} %shard_map.86.refs_2_.weight_ref, bf16[44,2,16,128]{3,2,1,0:T(8,128)(2,1)S(1)} %get-tuple-element.36.refs_0_, ...), custom_call_target="tpu_custom_call", output_to_operand_aliasing={{0}: (12, {}), {1}: (13, {})} | custom-call | flops 922746880 | bytes 18022400 | tf_op jit(solution)/shard_map/pallas_call | solution.py:299
  (9 shorter events, 0.1 us)
Async XLA Ops:
  4.9 16.5 %collective-permute-start = (bf16[2,5,2,16,1024]{4,3,2,1,0:T(8,128)(2,1)S(1)}, bf16[2,5,2,16,1024]{4,3,2,1,0:T(8,128)(2,1)S(1)}, u32[]{:S(2)}, u32[]{:S(2)}) collective-permute-start(bf16[2,5,2,16,1024]{4,3,2,1,0:T(8,128)(2,1)S(1)} %get-tuple-element.24), channel_id=1, source_target_pairs={{0,32},{32,64},{64,96},{96,0},{1,33},{33,65},{65,97},{97,1},{2,34}... | collective-permute-start | bytes 1966088 | tf_op jit(solution)/shard_map/ppermute | solution.py:33
  5.4 17.4 %collective-permute-start.1 = (bf16[2,5,2,16,1024]{4,3,2,1,0:T(8,128)(2,1)S(1)}, bf16[2,5,2,16,1024]{4,3,2,1,0:T(8,128)(2,1)S(1)}, u32[]{:S(2)}, u32[]{:S(2)}) collective-permute-start(bf16[2,5,2,16,1024]{4,3,2,1,0:T(8,128)(2,1)S(1)} %get-tuple-element.25), channel_id=1, source_target_pairs={{0,96},{32,0},{64,32},{96,64},{1,97},{33,1},{65,33},{97,65},{2,98}... | collective-permute-start | bytes 1966088 | tf_op jit(solution)/shard_map/ppermute | solution.py:33
  9.5 20.3 %collective-permute-start.5 = (bf16[4,3,2,16,1024]{4,3,2,1,0:T(8,128)(2,1)S(1)}, bf16[4,3,2,16,1024]{4,3,2,1,0:T(8,128)(2,1)S(1)}, u32[]{:S(2)}, u32[]{:S(2)}) collective-permute-start(bf16[4,3,2,16,1024]{4,3,2,1,0:T(8,128)(2,1)S(1)} %get-tuple-element.31), channel_id=1, source_target_pairs={{0,16},{16,0},{1,17},{17,1},{2,18},{18,2},{3,19},{19,3},{4,20},{20... | collective-permute-start | bytes 2359304 | tf_op jit(solution)/shard_map/ppermute | solution.py:37
  22.9 10.1 %collective-permute-start.2 = (bf16[1,5,2,16,1024]{4,3,2,1,0:T(8,128)(2,1)S(1)}, bf16[1,5,2,16,1024]{4,3,2,1,0:T(8,128)(2,1)S(1)}, u32[]{:S(2)}, u32[]{:S(2)}) collective-permute-start(bf16[1,5,2,16,1024]{4,3,2,1,0:T(8,128)(2,1)S(1)} %get-tuple-element.26), channel_id=1, source_target_pairs={{0,32},{32,64},{64,96},{96,0},{1,33},{33,65},{65,97},{97,1},{2,34}... | collective-permute-start | bytes 983048 | tf_op jit(solution)/shard_map/ppermute | solution.py:33
  23.4 9.6 %collective-permute-start.3 = (bf16[1,5,2,16,1024]{4,3,2,1,0:T(8,128)(2,1)S(1)}, bf16[1,5,2,16,1024]{4,3,2,1,0:T(8,128)(2,1)S(1)}, u32[]{:S(2)}, u32[]{:S(2)}) collective-permute-start(bf16[1,5,2,16,1024]{4,3,2,1,0:T(8,128)(2,1)S(1)} %get-tuple-element.27), channel_id=1, source_target_pairs={{0,96},{32,0},{64,32},{96,64},{1,97},{33,1},{65,33},{97,65},{2,98}... | collective-permute-start | bytes 983048 | tf_op jit(solution)/shard_map/ppermute | solution.py:33
  29.8 15.0 %copy-start = (bf16[1024,1024]{1,0:T(8,128)(2,1)S(1)}, bf16[1024,1024]{1,0:T(8,128)(2,1)}, u32[]{:S(2)}) copy-start(bf16[1024,1024]{1,0:T(8,128)(2,1)} %constant.116.clone.sin_ref) | copy-start | bytes 6291460
  29.8 15.0 %copy-start.1 = (bf16[1024,1024]{1,0:T(8,128)(2,1)S(1)}, bf16[1024,1024]{1,0:T(8,128)(2,1)}, u32[]{:S(2)}) copy-start(bf16[1024,1024]{1,0:T(8,128)(2,1)} %constant.115.clone.cos_ref) | copy-start | bytes 6291460
  29.8 15.0 %copy-start.3 = (f32[4,1024]{1,0:T(4,128)S(1)}, f32[4,1024]{1,0:T(4,128)}, u32[]{:S(2)}) copy-start(f32[4,1024]{1,0:T(4,128)} %taps_ref.1) | copy-start | bytes 49156
  30.0 7.5 %collective-permute-start.6 = (bf16[3,2,16,1024]{3,2,1,0:T(8,128)(2,1)S(1)}, bf16[3,2,16,1024]{3,2,1,0:T(8,128)(2,1)S(1)}, u32[]{:S(2)}, u32[]{:S(2)}) collective-permute-start(bf16[3,2,16,1024]{3,2,1,0:T(8,128)(2,1)S(1)} %get-tuple-element.33), channel_id=1, source_target_pairs={{0,32},{32,64},{64,96},{96,0},{1,33},{33,65},{65,97},{97,1},{2,34}... | collective-permute-start | bytes 589832 | tf_op jit(solution)/shard_map/ppermute | solution.py:33
  31.7 8.6 %collective-permute-start.7 = (bf16[3,2,16,1024]{3,2,1,0:T(8,128)(2,1)S(1)}, bf16[3,2,16,1024]{3,2,1,0:T(8,128)(2,1)S(1)}, u32[]{:S(2)}, u32[]{:S(2)}) collective-permute-start(bf16[3,2,16,1024]{3,2,1,0:T(8,128)(2,1)S(1)} %get-tuple-element.34), channel_id=1, source_target_pairs={{0,64},{32,96},{64,0},{96,32},{1,65},{33,97},{65,1},{97,33},{2,66}... | collective-permute-start | bytes 589832 | tf_op jit(solution)/shard_map/ppermute | solution.py:33
  33.0 9.4 %collective-permute-start.8 = (bf16[3,2,16,1024]{3,2,1,0:T(8,128)(2,1)S(1)}, bf16[3,2,16,1024]{3,2,1,0:T(8,128)(2,1)S(1)}, u32[]{:S(2)}, u32[]{:S(2)}) collective-permute-start(bf16[3,2,16,1024]{3,2,1,0:T(8,128)(2,1)S(1)} %get-tuple-element.35), channel_id=1, source_target_pairs={{0,96},{32,0},{64,32},{96,64},{1,97},{33,1},{65,33},{97,65},{2,98}... | collective-permute-start | bytes 589832 | tf_op jit(solution)/shard_map/ppermute | solution.py:33
  33.2 11.6 %collective-permute-start.4 = (bf16[1,5,2,16,1024]{4,3,2,1,0:T(8,128)(2,1)S(1)}, bf16[1,5,2,16,1024]{4,3,2,1,0:T(8,128)(2,1)S(1)}, u32[]{:S(2)}, u32[]{:S(2)}) collective-permute-start(bf16[1,5,2,16,1024]{4,3,2,1,0:T(8,128)(2,1)S(1)} %get-tuple-element.29), channel_id=1, source_target_pairs={{0,16},{16,0},{1,17},{17,1},{2,18},{18,2},{3,19},{19,3},{4,20},{20... | collective-permute-start | bytes 983048 | tf_op jit(solution)/shard_map/ppermute | solution.py:37
  42.5 2.4 %collective-permute-start.9 = (bf16[3,2,16,1024]{3,2,1,0:T(8,128)(2,1)S(1)}, bf16[3,2,16,1024]{3,2,1,0:T(8,128)(2,1)S(1)}, u32[]{:S(2)}, u32[]{:S(2)}) collective-permute-start(bf16[3,2,16,1024]{3,2,1,0:T(8,128)(2,1)S(1)} %shard_map.92.late_ref), channel_id=1, source_target_pairs={{0,1},{1,2},{2,3},{3,4},{4,5},{5,6},{6,7},{7,8},{8,9},{9,10},{10,1... | collective-permute-start | bytes 589832 | tf_op jit(solution)/shard_map/ppermute | solution.py:389
  46.3 40.9 %copy-start.2 = (f32[128,128]{1,0:T(8,128)S(1)}, f32[128,128]{1,0:T(8,128)}, u32[]{:S(2)}) copy-start(f32[128,128]{1,0:T(8,128)} %delays_ref.3) | copy-start | bytes 196612
  68.9 16.3 %collective-permute-start.10 = (bf16[44,2,16,128]{3,2,1,0:T(8,128)(2,1)S(1)}, bf16[44,2,16,128]{3,2,1,0:T(8,128)(2,1)S(1)}, u32[]{:S(2)}, u32[]{:S(2)}) collective-permute-start(bf16[44,2,16,128]{3,2,1,0:T(8,128)(2,1)S(1)} %get-tuple-element.36.refs_0_), channel_id=1, source_target_pairs={{0,16},{16,0},{1,17},{17,1},{2,18},{18,2},{3,19},{19,3},{4,20},{20... | collective-permute-start | bytes 1081352 | tf_op jit(solution)/shard_map/ppermute | solution.py:37
  71.8 6.9 %collective-permute-start.21 = (bf16[20,2,16,128]{3,2,1,0:T(8,128)(2,1)S(1)}, bf16[20,2,16,128]{3,2,1,0:T(8,128)(2,1)S(1)}, u32[]{:S(2)}, u32[]{:S(2)}) collective-permute-start(bf16[20,2,16,128]{3,2,1,0:T(8,128)(2,1)S(1)} %get-tuple-element.41.refs_0_), channel_id=1, source_target_pairs={{0,32},{32,64},{64,96},{96,0},{1,33},{33,65},{65,97},{97,1},{2,34}... | collective-permute-start | bytes 491528 | tf_op jit(solution)/shard_map/ppermute | solution.py:33
  72.4 8.2 %collective-permute-start.20 = (bf16[20,2,16,128]{3,2,1,0:T(8,128)(2,1)S(1)}, bf16[20,2,16,128]{3,2,1,0:T(8,128)(2,1)S(1)}, u32[]{:S(2)}, u32[]{:S(2)}) collective-permute-start(bf16[20,2,16,128]{3,2,1,0:T(8,128)(2,1)S(1)} %get-tuple-element.41.refs_0_), channel_id=1, source_target_pairs={{0,64},{32,96},{64,0},{96,32},{1,65},{33,97},{65,1},{97,33},{2,66}... | collective-permute-start | bytes 491528 | tf_op jit(solution)/shard_map/ppermute | solution.py:33
  73.6 8.7 %collective-permute-start.19 = (bf16[20,2,16,128]{3,2,1,0:T(8,128)(2,1)S(1)}, bf16[20,2,16,128]{3,2,1,0:T(8,128)(2,1)S(1)}, u32[]{:S(2)}, u32[]{:S(2)}) collective-permute-start(bf16[20,2,16,128]{3,2,1,0:T(8,128)(2,1)S(1)} %get-tuple-element.41.refs_0_), channel_id=1, source_target_pairs={{0,96},{32,0},{64,32},{96,64},{1,97},{33,1},{65,33},{97,65},{2,98}... | collective-permute-start | bytes 491528 | tf_op jit(solution)/shard_map/ppermute | solution.py:33
  82.3 23.2 %collective-permute-start.22 = (bf16[4,20,2,16,128]{4,3,2,1,0:T(8,128)(2,1)S(1)}, bf16[4,20,2,16,128]{4,3,2,1,0:T(8,128)(2,1)S(1)}, u32[]{:S(2)}, u32[]{:S(2)}) collective-permute-start(bf16[4,20,2,16,128]{4,3,2,1,0:T(8,128)(2,1)S(1)} %shard_map.98.refs_0_), channel_id=1, source_target_pairs={{0,16},{16,0},{1,17},{17,1},{2,18},{18,2},{3,19},{19,3},{4,20},{20... | collective-permute-start | bytes 1966088 | tf_op jit(solution)/shard_map/ppermute | solution.py:37
  83.1 11.4 %collective-permute-start.13 = (bf16[44,2,16,128]{3,2,1,0:T(8,128)(2,1)S(1)}, bf16[44,2,16,128]{3,2,1,0:T(8,128)(2,1)S(1)}, u32[]{:S(2)}, u32[]{:S(2)}) collective-permute-start(bf16[44,2,16,128]{3,2,1,0:T(8,128)(2,1)S(1)} %get-tuple-element.36.refs_0_), channel_id=1, source_target_pairs={{0,32},{32,64},{64,96},{96,0},{1,33},{33,65},{65,97},{97,1},{2,34}... | collective-permute-start | bytes 1081352 | tf_op jit(solution)/shard_map/ppermute | solution.py:33
  83.9 12.6 %collective-permute-start.11 = (bf16[44,2,16,128]{3,2,1,0:T(8,128)(2,1)S(1)}, bf16[44,2,16,128]{3,2,1,0:T(8,128)(2,1)S(1)}, u32[]{:S(2)}, u32[]{:S(2)}) collective-permute-start(bf16[44,2,16,128]{3,2,1,0:T(8,128)(2,1)S(1)} %get-tuple-element.36.refs_0_), channel_id=1, source_target_pairs={{0,96},{32,0},{64,32},{96,64},{1,97},{33,1},{65,33},{97,65},{2,98}... | collective-permute-start | bytes 1081352 | tf_op jit(solution)/shard_map/ppermute | solution.py:33
  85.1 17.0 %collective-permute-start.16 = (bf16[44,2,16,128]{3,2,1,0:T(8,128)(2,1)S(1)}, bf16[44,2,16,128]{3,2,1,0:T(8,128)(2,1)S(1)}, u32[]{:S(2)}, u32[]{:S(2)}) collective-permute-start(bf16[44,2,16,128]{3,2,1,0:T(8,128)(2,1)S(1)} %collective-permute-done.10.refs_1_), channel_id=1, source_target_pairs={{0,32},{32,64},{64,96},{96,0},{1,33},{33,65},{65,97},{97,1},{2,34}... | collective-permute-start | bytes 1081352 | tf_op jit(solution)/shard_map/ppermute | solution.py:33
  87.2 16.2 %collective-permute-start.12 = (bf16[44,2,16,128]{3,2,1,0:T(8,128)(2,1)S(1)}, bf16[44,2,16,128]{3,2,1,0:T(8,128)(2,1)S(1)}, u32[]{:S(2)}, u32[]{:S(2)}) collective-permute-start(bf16[44,2,16,128]{3,2,1,0:T(8,128)(2,1)S(1)} %collective-permute-done.10.refs_1_), channel_id=1, source_target_pairs={{0,96},{32,0},{64,32},{96,64},{1,97},{33,1},{65,33},{97,65},{2,98}... | collective-permute-start | bytes 1081352 | tf_op jit(solution)/shard_map/ppermute | solution.py:33
  96.5 11.7 %collective-permute-start.14 = (bf16[22,2,16,128]{3,2,1,0:T(8,128)(2,1)S(1)}, bf16[22,2,16,128]{3,2,1,0:T(8,128)(2,1)S(1)}, u32[]{:S(2)}, u32[]{:S(2)}) collective-permute-start(bf16[22,2,16,128]{3,2,1,0:T(8,128)(2,1)S(1)} %get-tuple-element.37), channel_id=1, source_target_pairs={{0,32},{32,64},{64,96},{96,0},{1,33},{33,65},{65,97},{97,1},{2,34}... | collective-permute-start | bytes 540680 | tf_op jit(solution)/shard_map/ppermute | solution.py:33
  96.8 11.5 %collective-permute-start.15 = (bf16[22,2,16,128]{3,2,1,0:T(8,128)(2,1)S(1)}, bf16[22,2,16,128]{3,2,1,0:T(8,128)(2,1)S(1)}, u32[]{:S(2)}, u32[]{:S(2)}) collective-permute-start(bf16[22,2,16,128]{3,2,1,0:T(8,128)(2,1)S(1)} %get-tuple-element.38), channel_id=1, source_target_pairs={{0,96},{32,0},{64,32},{96,64},{1,97},{33,1},{65,33},{97,65},{2,98}... | collective-permute-start | bytes 540680 | tf_op jit(solution)/shard_map/ppermute | solution.py:33
  103.5 5.6 %collective-permute-start.17 = (bf16[22,2,16,128]{3,2,1,0:T(8,128)(2,1)S(1)}, bf16[22,2,16,128]{3,2,1,0:T(8,128)(2,1)S(1)}, u32[]{:S(2)}, u32[]{:S(2)}) collective-permute-start(bf16[22,2,16,128]{3,2,1,0:T(8,128)(2,1)S(1)} %get-tuple-element.39), channel_id=1, source_target_pairs={{0,32},{32,64},{64,96},{96,0},{1,33},{33,65},{65,97},{97,1},{2,34}... | collective-permute-start | bytes 540680 | tf_op jit(solution)/shard_map/ppermute | solution.py:33
  103.9 6.7 %collective-permute-start.18 = (bf16[22,2,16,128]{3,2,1,0:T(8,128)(2,1)S(1)}, bf16[22,2,16,128]{3,2,1,0:T(8,128)(2,1)S(1)}, u32[]{:S(2)}, u32[]{:S(2)}) collective-permute-start(bf16[22,2,16,128]{3,2,1,0:T(8,128)(2,1)S(1)} %get-tuple-element.40), channel_id=1, source_target_pairs={{0,96},{32,0},{64,32},{96,64},{1,97},{33,1},{65,33},{97,65},{2,98}... | collective-permute-start | bytes 540680 | tf_op jit(solution)/shard_map/ppermute | solution.py:33
